TPU v7x, 32 devices: a whole 2x2x4 slice. The times are simulated.
32 devices in a mesh: wide: 4 (over x, core), narrow: 8 (over z, y).
Axes of the slice: x: 2, y: 2, z: 4, core: 2. Of those that a mesh axis runs over, the one named last changes fastest.
Arguments:
- right_side: float32 [512, 128, 128], P(('wide', 'narrow')), may hold values from -120 to 120
- resistance: float32 [512, 128], P(('wide', 'narrow')), may hold values from 0.3 to 3
- omega: float32 [32], replicated, may hold values from 0.5 to 2
- pcoef: float32 [32768], P(('wide', 'narrow')), may hold values from 0.1 to 1
- branch_nodes: int32 [512, 2, 128], P(('wide', 'narrow')), may hold values from 0 to 2047, as said below
- self_blocks: bfloat16 [512, 128, 128], P(('wide', 'narrow')), may hold values from -1 to 3
- couple_list: int32 [3, 7168], P(None, ('wide', 'narrow')), may hold values from 0 to 15, as said below
- couple_blocks: bfloat16 [7168, 128, 128], P(('wide', 'narrow')), may hold values from -0.109375 to 0.109375
- jacobi_ids: int32 [512], P(('wide', 'narrow')), may hold values from 0 to 7
- preconditioners: bfloat16 [8, 128, 128], replicated, may hold values from -1 to 2
Outputs:
- solution: float32 [512, 128, 128], P(('wide', 'narrow'))
- residual_norms: float32 [2, 32], replicated
Inputs may be any that keep to these rules, and one draw needn't show every extreme that they name: `couple_list`: row 0 names a row block of the entry's device, row 1 a block of the owner, row 2 the owner's narrow index in the same wide group. Over the entries of one device, at most 4 distinct blocks of one owner are named; exactly 4 of the device itself, and at least one of every owner. No pair of row block and source block appears twice. `branch_nodes`: A value v of 1024 or more names node v - 1024 of the next device along narrow in the same wide group; such values never stand on the last device along narrow.
All inputs are finite; a program needn't handle non-finite values.
Results may differ from a plain program's by a relative error of at most 0.0034.
Values may be sent and summed in bfloat16 or wider, within the bound.
No kernel may reach another device: no remote copies, remote signals or barrier semaphores. Data moves between devices by JAX's collectives and lax.ppermute only.
A program may use at most 128 MiB of HBM per device.

v0:
```python
import jax
import jax.numpy as jnp
from jax import lax
from jax.sharding import PartitionSpec as P

F = 32
CASES = 2
ITERS = 3


def shifted(block, axis, distance):
    devices = range(lax.axis_size(axis))
    route = [(i - distance, i) for i in devices if i - distance in devices]
    return lax.ppermute(block, axis, route)


def system_dot(first, second):
    return jnp.sum((first * second).reshape(-1, CASES, 2, F), axis=(0, 2))


def expand(values):
    return jnp.broadcast_to(values[:, None, :], (CASES, 2, F)).reshape(2 * CASES * F)


def turned(values):
    parts = values.reshape(values.shape[:-1] + (CASES, 2, F))
    return jnp.stack([-parts[..., 1, :], parts[..., 0, :]], axis=-2).reshape(values.shape)


def node_drop(field, branch_nodes, pcoef):
    nodes_dev = pcoef.shape[0]
    rows = field.reshape(-1, field.shape[2])
    first = branch_nodes[:, 0, :].reshape(-1)
    second = branch_nodes[:, 1, :].reshape(-1)
    charge = jax.ops.segment_sum(rows, first, 2 * nodes_dev) - jax.ops.segment_sum(
        rows, second, 2 * nodes_dev
    )
    arrived = shifted(charge[nodes_dev:], "narrow", 1)
    potential = pcoef[:, None] * (charge[:nodes_dev] + arrived)
    beyond = shifted(potential, "narrow", -1)
    extended = jnp.concatenate([potential, beyond], axis=0)
    drop = jnp.take(extended, first, axis=0) - jnp.take(extended, second, axis=0)
    return drop.reshape(field.shape)


def least_squares(hess, beta):
    zero = jnp.zeros_like(beta)
    rotated = [beta] + [zero for later in range(ITERS)]
    cosines = []
    sines = []
    upper = [[None for later in range(ITERS)] for other in range(ITERS)]
    for column in range(ITERS):
        entries = [hess[index][column] for index in range(column + 1)] + [hess[column + 1][column]]
        for index in range(column):
            top = entries[index]
            low = entries[index + 1]
            entries[index] = cosines[index] * top + sines[index] * low
            entries[index + 1] = -sines[index] * top + cosines[index] * low
        top = entries[column]
        low = entries[column + 1]
        radius = jnp.sqrt(top * top + low * low)
        cosine = top / radius
        sine = low / radius
        cosines.append(cosine)
        sines.append(sine)
        entries[column] = radius
        rotated[column + 1] = -sine * rotated[column]
        rotated[column] = cosine * rotated[column]
        for index in range(column + 1):
            upper[index][column] = entries[index]
    weights = [None for later in range(ITERS)]
    for index in reversed(range(ITERS)):
        accum = rotated[index]
        for other in range(index + 1, ITERS):
            accum = accum - upper[index][other] * weights[other]
        weights[index] = accum / upper[index][index]
    return (weights, jnp.abs(rotated[ITERS]))


def on_device(
    right_side,
    resistance,
    omega,
    pcoef,
    branch_nodes,
    self_blocks,
    couple_list,
    couple_blocks,
    jacobi_ids,
    preconditioners,
):
    block_count = right_side.shape[0]
    row_block = couple_list[0]
    owner_index = couple_list[2]
    flat_index = owner_index * block_count + couple_list[1]
    frequency = jnp.tile(omega, 2 * CASES)
    chosen = jnp.take(preconditioners, jacobi_ids, axis=0)
    beta = jnp.sqrt(lax.psum(system_dot(right_side, right_side), ("wide", "narrow")))
    basis = [right_side / expand(beta)]
    directions = []
    hess = [[None for later in range(ITERS)] for other in range(ITERS + 1)]
    for column in range(ITERS):
        direction = jnp.einsum(
            "nab,nbc->nac",
            chosen,
            basis[column].astype(jnp.bfloat16),
            preferred_element_type=jnp.float32,
        )
        directions.append(direction)
        operate_rounded = direction.astype(jnp.bfloat16)
        flux = jnp.einsum(
            "nab,nbc->nac", self_blocks, operate_rounded, preferred_element_type=jnp.float32
        )
        whole = lax.all_gather(operate_rounded, "narrow", axis=0, tiled=True)
        coupled = jnp.einsum(
            "eab,ebc->eac",
            couple_blocks,
            jnp.take(whole, flat_index, axis=0),
            preferred_element_type=jnp.float32,
        )
        flux = flux + jax.ops.segment_sum(coupled, row_block, block_count)
        drop = node_drop(direction, branch_nodes, pcoef)
        image = resistance[:, :, None] * direction + turned(frequency * flux - drop / frequency)
        local_dots = jnp.stack([system_dot(basis[index], image) for index in range(column + 1)])
        projected, squared = lax.psum((local_dots, system_dot(image, image)), ("wide", "narrow"))
        for index in range(column + 1):
            image = image - expand(projected[index]) * basis[index]
        remainder_sq = squared - jnp.sum(projected * projected, axis=0)
        for index in range(column + 1):
            hess[index][column] = projected[index]
        length = jnp.sqrt(remainder_sq)
        hess[column + 1][column] = length
        if column + 1 < ITERS:
            basis.append(image / expand(length))
    weights, residual_norms = least_squares(hess, beta)
    solution = expand(weights[0]) * directions[0]
    for column in range(1, ITERS):
        solution = solution + expand(weights[column]) * directions[column]
    return (solution, residual_norms)


def solution(mesh):
    placed = (
        P(("wide", "narrow"), None, None),
        P(("wide", "narrow"), None),
        P(),
        P(("wide", "narrow")),
        P(("wide", "narrow"), None, None),
        P(("wide", "narrow"), None, None),
        P(None, ("wide", "narrow")),
        P(("wide", "narrow"), None, None),
        P(("wide", "narrow")),
        P(),
    )
    return jax.shard_map(
        on_device,
        mesh=mesh,
        in_specs=placed,
        out_specs=(P(("wide", "narrow"), None, None), P()),
        check_vma=False,
    )
```

profile of v0, /device:TPU:0, one launch (start us, length us, event | category | flops | bytes accessed | tf_op | source)
XLA Modules:
  0.0 721.6 jit_solution(16329323222123137055)
XLA Ops:
  8.6 1.5 multiply_reduce_fusion.9
  10.2 42.0 %psum.49 = f32[2,32]{1,0:T(2,128)S(1)} all-reduce(f32[2,32]{1,0:T(2,128)S(1)} %reduce_sum.144), channel_id=1, replica_groups=mesh['wide'=4,'narrow'=8] {'wide','narrow'}, use_global_device_ids=true, to_apply=%region_2.3 | all-reduce | flops 64 | bytes 512 | tf_op jit(solution)/shard_map/psum | solution.py:98
  52.3 1.6 gather_fusion
  54.0 2.6 fusion.41
  56.7 12.4 %scatter_custom_fusion.1 = f32[2048,128]{1,0:T(8,128)} fusion(s32[2048]{0:T(1024)S(1)} %bitcast.131, f32[2048,128]{1,0:T(8,128)S(1)} %bitcast.120, f32[]{:T(128)} %constant.16.clone.1), kind=kCustom, calls=%fused_computation.85 | custom fusion | flops 262144 | bytes 1048580 | tf_op jit(solution)/shard_map/scatter-add | solution.py:35
  69.1 12.4 %scatter_custom_fusion.2 = f32[2048,128]{1,0:T(8,128)} fusion(s32[2048]{0:T(1024)S(1)} %bitcast.136, f32[2048,128]{1,0:T(8,128)S(1)} %bitcast.121, f32[]{:T(128)} %constant.16.clone.1), kind=kCustom, calls=%fused_computation.83 | custom fusion | flops 262144 | bytes 1048580 | tf_op jit(solution)/shard_map/scatter-add | solution.py:35
  81.6 1.6 sub.54
  84.0 5.0 collective-permute-start
  89.0 2.5 convolution_bitcast_fusion.5
  91.6 1.6 copy.44
  93.3 15.2 %collective-permute-done = f32[1024,128]{1,0:T(8,128)} collective-permute-done((f32[1024,128]{1,0:T(8,128)}, f32[1024,128]{1,0:T(8,128)}, u32[]{:S(2)}, u32[]{:S(2)}) %collective-permute-start) | collective-permute-done | bytes 524320 | tf_op jit(solution)/shard_map/ppermute | solution.py:14
  109.7 1.5 collective-permute-start.1
  111.2 14.8 %collective-permute-done.1 = f32[1024,128]{1,0:T(8,128)S(1)} collective-permute-done((f32[1024,128]{1,0:T(8,128)S(1)}, f32[1024,128]{1,0:T(8,128)S(1)}, u32[]{:S(2)}, u32[]{:S(2)}) %collective-permute-start.1) | collective-permute-done | bytes 524320 | tf_op jit(solution)/shard_map/ppermute | solution.py:14
  126.1 7.6 %gather_fusion.2 = f32[2048,128]{1,0:T(8,128)} fusion(f32[2048,128]{1,0:T(8,128)S(1)} %pad_maximum_fusion, s32[2048]{0:T(1024)S(1)} %fusion.30), kind=kCustom, calls=%fused_computation.1.clone | custom fusion | bytes 2105344 | tf_op jit(solution)/shard_map/jit(_take)/gather | solution.py:42
  133.6 7.6 %gather_fusion.3 = f32[2048,128]{1,0:T(8,128)} fusion(f32[2048,128]{1,0:T(8,128)S(1)} %pad_maximum_fusion, s32[2048]{0:T(1024)S(1)} %fusion.31), kind=kCustom, calls=%fused_computation.4.clone | custom fusion | bytes 2105344 | tf_op jit(solution)/shard_map/jit(_take)/gather | solution.py:42
  141.3 3.9 select_subtract_fusion.2
  145.2 10.5 %gather_fusion.1 = bf16[224,128,128]{2,1,0:T(8,128)(2,1)} fusion(bf16[128,128,128]{2,1,0:T(8,128)(2,1)} %all-gather.4.cloned.1.call-done, s32[1024]{0:T(1024)S(1)} %pad_clamp_fusion), kind=kCustom, calls=%fused_computation.clone | custom fusion | bytes 14680960 | tf_op jit(solution)/shard_map/jit(_take)/gather | solution.py:118
  155.7 12.0 %convolution_bitcast_fusion.2 = f32[224,128,128]{1,2,0:T(8,128)} fusion(bf16[224,128,128]{2,1,0:T(8,128)(2,1)} %param.21, bf16[224,128,128]{2,1,0:T(8,128)(2,1)} %gather_fusion.1, pred[224]{0:T(512)(128)(4,1)S(1)} %compare_and_fusion.2), kind=kOutput, calls=%fused_computation.21 | convolution fusion | flops 943194112 | bytes 29360352 | tf_op jit(solution)/shard_map/eab,ebc->eac/dot_general | solution.py:115
  167.8 15.1 %copy.45 = f32[224,128,128]{2,1,0:T(8,128)} copy(f32[224,128,128]{1,2,0:T(8,128)} %convolution_bitcast_fusion.2) | data formatting | bytes 29360128 | tf_op jit(solution)/shard_map/eab,ebc->eac/dot_general | solution.py:115
  182.9 29.4 %scatter_fusion = f32[16,128,128]{2,1,0:T(8,128)S(1)} fusion(f32[16,128,128]{2,1,0:T(8,128)S(1)} %copy.44, s32[224]{0:T(256)S(1)} %bitcast.141, f32[224,128,128]{2,1,0:T(8,128)} %copy.45), kind=kCustom, calls=%fused_computation.10 | custom fusion | flops 3670016 | bytes 44041088 | tf_op jit(solution)/shard_map/scatter-add | solution.py:121
  212.3 2.4 divide_subtract_fusion.2
  214.7 1.6 copy.46
  217.8 1.9 multiply_reduce_fusion.8
  219.9 52.7 %all-reduce.2 = (f32[2,32]{1,0:T(2,128)S(1)}, f32[1,2,32]{2,1,0:T(2,128)S(1)}) all-reduce(f32[2,32]{1,0:T(2,128)S(1)} %reduce_sum.153, f32[1,2,32]{2,1,0:T(2,128)S(1)} %bitcast.147), channel_id=1, replica_groups=mesh['wide'=4,'narrow'=8] {'wide','narrow'}, use_global_device_ids=true, to_apply=%region_11.14 | all-reduce | flops 128 | bytes 1024 | tf_op jit(solution)/shard_map/psum | solution.py:125
  275.3 12.9 %scatter_custom_fusion.5 = f32[2048,128]{1,0:T(8,128)} fusion(s32[2048]{0:T(1024)S(1)} %bitcast.139, f32[2048,128]{1,0:T(8,128)S(1)} %bitcast.116, f32[]{:T(128)} %constant.16.clone.1), kind=kCustom, calls=%fused_computation.79 | custom fusion | flops 262144 | bytes 1048580 | tf_op jit(solution)/shard_map/scatter-add | solution.py:35
  288.1 12.5 %scatter_custom_fusion.4 = f32[2048,128]{1,0:T(8,128)} fusion(s32[2048]{0:T(1024)S(1)} %bitcast.134, f32[2048,128]{1,0:T(8,128)S(1)} %bitcast.117, f32[]{:T(128)} %constant.16.clone.1), kind=kCustom, calls=%fused_computation.81 | custom fusion | flops 262144 | bytes 1048580 | tf_op jit(solution)/shard_map/scatter-add | solution.py:35
  300.6 1.6 sub.59
  302.3 4.2 collective-permute-start.2
  306.5 23.5 %collective-permute-done.2 = f32[1024,128]{1,0:T(8,128)S(1)} collective-permute-done((f32[1024,128]{1,0:T(8,128)S(1)}, f32[1024,128]{1,0:T(8,128)S(1)}, u32[]{:S(2)}, u32[]{:S(2)}) %collective-permute-start.2) | collective-permute-done | bytes 524320 | tf_op jit(solution)/shard_map/ppermute | solution.py:14
  333.2 11.3 %collective-permute-done.3 = f32[1024,128]{1,0:T(8,128)} collective-permute-done((f32[1024,128]{1,0:T(8,128)}, f32[1024,128]{1,0:T(8,128)}, u32[]{:S(2)}, u32[]{:S(2)}) %collective-permute-start.3) | collective-permute-done | bytes 524320 | tf_op jit(solution)/shard_map/ppermute | solution.py:14
  345.8 7.6 %gather_fusion.5 = f32[2048,128]{1,0:T(8,128)} fusion(f32[2048,128]{1,0:T(8,128)S(1)} %pad_maximum_fusion.2, s32[2048]{0:T(1024)S(1)} %fusion.30), kind=kCustom, calls=%fused_computation.5.clone | custom fusion | bytes 2105344 | tf_op jit(solution)/shard_map/jit(_take)/gather | solution.py:42
  353.4 7.6 %gather_fusion.6 = f32[2048,128]{1,0:T(8,128)} fusion(f32[2048,128]{1,0:T(8,128)S(1)} %pad_maximum_fusion.2, s32[2048]{0:T(1024)S(1)} %fusion.31), kind=kCustom, calls=%fused_computation.6.clone | custom fusion | bytes 2105344 | tf_op jit(solution)/shard_map/jit(_take)/gather | solution.py:42
  361.0 3.9 select_subtract_fusion.1
  364.9 10.5 %gather_fusion.4 = bf16[224,128,128]{2,1,0:T(8,128)(2,1)} fusion(bf16[128,128,128]{2,1,0:T(8,128)(2,1)} %all-gather.6.cloned.1.call-done, s32[1024]{0:T(1024)S(1)} %pad_clamp_fusion), kind=kCustom, calls=%fused_computation.2.clone | custom fusion | bytes 14680960 | tf_op jit(solution)/shard_map/jit(_take)/gather | solution.py:118
  375.4 12.0 %convolution_bitcast_fusion.1 = f32[224,128,128]{1,2,0:T(8,128)} fusion(bf16[224,128,128]{2,1,0:T(8,128)(2,1)} %param.21, bf16[224,128,128]{2,1,0:T(8,128)(2,1)} %gather_fusion.4, pred[224]{0:T(512)(128)(4,1)S(1)} %compare_and_fusion.2), kind=kOutput, calls=%fused_computation.20 | convolution fusion | flops 943194112 | bytes 29360352 | tf_op jit(solution)/shard_map/eab,ebc->eac/dot_general | solution.py:115
  387.5 15.1 %copy.51 = f32[224,128,128]{2,1,0:T(8,128)} copy(f32[224,128,128]{1,2,0:T(8,128)} %convolution_bitcast_fusion.1) | data formatting | bytes 29360128 | tf_op jit(solution)/shard_map/eab,ebc->eac/dot_general | solution.py:115
  402.6 29.4 %scatter_fusion.1 = f32[16,128,128]{2,1,0:T(8,128)S(1)} fusion(f32[16,128,128]{2,1,0:T(8,128)S(1)} %copy.50, s32[224]{0:T(256)S(1)} %bitcast.142, f32[224,128,128]{2,1,0:T(8,128)} %copy.51), kind=kCustom, calls=%fused_computation.13 | custom fusion | flops 3670016 | bytes 44041088 | tf_op jit(solution)/shard_map/scatter-add | solution.py:121
  432.0 2.4 divide_subtract_fusion.1
  434.4 2.7 copy.52
  437.1 1.3 slice_negate_fusion.1
  439.6 2.6 copy.53
  442.2 3.3 multiply_reduce_fusion.6
  445.8 45.3 %all-reduce.1 = (f32[2,32]{1,0:T(2,128)S(1)}, f32[2,2,32]{2,1,0:T(2,128)S(1)}) all-reduce(f32[2,32]{1,0:T(2,128)S(1)} %reduce_sum.202, f32[2,2,32]{2,1,0:T(2,128)S(1)} %pad_maximum_fusion.7), channel_id=1, replica_groups=mesh['wide'=4,'narrow'=8] {'wide','narrow'}, use_global_device_ids=true, to_apply=%region_22.25 | all-reduce | flops 192 | bytes 1536 | tf_op jit(solution)/shard_map/psum | solution.py:125
  491.4 1.5 subtract_divide_fusion
  495.1 12.5 %scatter_custom_fusion.8 = f32[2048,128]{1,0:T(8,128)} fusion(s32[2048]{0:T(1024)S(1)} %bitcast.140, f32[2048,128]{1,0:T(8,128)S(1)} %bitcast.118, f32[]{:T(128)} %constant.16.clone.1), kind=kCustom, calls=%fused_computation.75 | custom fusion | flops 262144 | bytes 1048580 | tf_op jit(solution)/shard_map/scatter-add | solution.py:35
  507.6 12.4 %scatter_custom_fusion.7 = f32[2048,128]{1,0:T(8,128)} fusion(s32[2048]{0:T(1024)S(1)} %bitcast.135, f32[2048,128]{1,0:T(8,128)S(1)} %bitcast.119, f32[]{:T(128)} %constant.16.clone.1), kind=kCustom, calls=%fused_computation.77 | custom fusion | flops 262144 | bytes 1048580 | tf_op jit(solution)/shard_map/scatter-add | solution.py:35
  520.1 1.6 sub.65
  521.8 4.2 collective-permute-start.4
  526.0 19.5 %collective-permute-done.4 = f32[1024,128]{1,0:T(8,128)S(1)} collective-permute-done((f32[1024,128]{1,0:T(8,128)S(1)}, f32[1024,128]{1,0:T(8,128)S(1)}, u32[]{:S(2)}, u32[]{:S(2)}) %collective-permute-start.4) | collective-permute-done | bytes 524320 | tf_op jit(solution)/shard_map/ppermute | solution.py:14
  548.6 16.4 %collective-permute-done.5 = f32[1024,128]{1,0:T(8,128)} collective-permute-done((f32[1024,128]{1,0:T(8,128)}, f32[1024,128]{1,0:T(8,128)}, u32[]{:S(2)}, u32[]{:S(2)}) %collective-permute-start.5) | collective-permute-done | bytes 524320 | tf_op jit(solution)/shard_map/ppermute | solution.py:14
  566.3 7.6 %gather_fusion.8 = f32[2048,128]{1,0:T(8,128)} fusion(f32[2048,128]{1,0:T(8,128)S(1)} %pad_maximum_fusion.4, s32[2048]{0:T(1024)S(1)} %fusion.30), kind=kCustom, calls=%fused_computation.7.clone | custom fusion | bytes 2105344 | tf_op jit(solution)/shard_map/jit(_take)/gather | solution.py:42
  573.9 7.5 %gather_fusion.9 = f32[2048,128]{1,0:T(8,128)} fusion(f32[2048,128]{1,0:T(8,128)S(1)} %pad_maximum_fusion.4, s32[2048]{0:T(1024)S(1)} %fusion.31), kind=kCustom, calls=%fused_computation.8.clone | custom fusion | bytes 2105344 | tf_op jit(solution)/shard_map/jit(_take)/gather | solution.py:42
  581.5 3.9 select_subtract_fusion
  585.4 10.5 %gather_fusion.7 = bf16[224,128,128]{2,1,0:T(8,128)(2,1)} fusion(bf16[128,128,128]{2,1,0:T(8,128)(2,1)} %all-gather.8.cloned.1.call-done, s32[1024]{0:T(1024)S(1)} %pad_clamp_fusion), kind=kCustom, calls=%fused_computation.3.clone | custom fusion | bytes 14680960 | tf_op jit(solution)/shard_map/jit(_take)/gather | solution.py:118
  595.9 12.0 %convolution_bitcast_fusion = f32[224,128,128]{1,2,0:T(8,128)} fusion(bf16[224,128,128]{2,1,0:T(8,128)(2,1)} %param.21, bf16[224,128,128]{2,1,0:T(8,128)(2,1)} %gather_fusion.7, pred[224]{0:T(512)(128)(4,1)S(1)} %compare_and_fusion.2), kind=kOutput, calls=%fused_computation.19 | convolution fusion | flops 943194112 | bytes 29360352 | tf_op jit(solution)/shard_map/eab,ebc->eac/dot_general | solution.py:115
  608.0 15.1 %copy.57 = f32[224,128,128]{2,1,0:T(8,128)} copy(f32[224,128,128]{1,2,0:T(8,128)} %convolution_bitcast_fusion) | data formatting | bytes 29360128 | tf_op jit(solution)/shard_map/eab,ebc->eac/dot_general | solution.py:115
  623.1 29.4 %scatter_fusion.2 = f32[16,128,128]{2,1,0:T(8,128)S(1)} fusion(f32[16,128,128]{2,1,0:T(8,128)S(1)} %copy.56, s32[224]{0:T(256)S(1)} %bitcast.143, f32[224,128,128]{2,1,0:T(8,128)} %copy.57), kind=kCustom, calls=%fused_computation.16 | custom fusion | flops 3670016 | bytes 44041088 | tf_op jit(solution)/shard_map/scatter-add | solution.py:121
  652.5 2.4 divide_subtract_fusion
  654.9 2.7 copy.58
  657.6 1.3 slice_negate_fusion
  660.1 2.5 copy.59
  662.7 2.8 multiply_reduce_fusion
  665.9 45.3 %all-reduce = (f32[3,2,32]{2,1,0:T(2,128)S(1)}, f32[2,32]{1,0:T(2,128)S(1)}) all-reduce(f32[3,2,32]{2,1,0:T(2,128)S(1)} %pad_maximum_fusion.6, f32[2,32]{1,0:T(2,128)S(1)} %reduce_sum.215), channel_id=1, replica_groups=mesh['wide'=4,'narrow'=8] {'wide','narrow'}, use_global_device_ids=true, to_apply=%region_33.36 | all-reduce | flops 256 | bytes 2048 | tf_op jit(solution)/shard_map/psum | solution.py:125
  712.1 2.7 multiply_add_fusion
  (133 shorter events, 23.5 us)
Async XLA Ops:
  7.2 81.9 %copy-start = (bf16[16,128,128]{2,1,0:T(8,128)(2,1)S(1)}, bf16[16,128,128]{2,1,0:T(8,128)(2,1)}, u32[]{:S(2)}) copy-start(bf16[16,128,128]{2,1,0:T(8,128)(2,1)} %param.19) | copy-start | bytes 1572868
  7.2 49.5 %copy-start.17 = (s32[16,2,128]{2,1,0:T(2,128)S(1)}, s32[16,2,128]{2,1,0:T(2,128)}, u32[]{:S(2)}) copy-start(s32[16,2,128]{2,1,0:T(2,128)} %param.18) | copy-start | bytes 49156
  7.2 81.8 %copy-start.18 = (s32[3,224]{1,0:T(4,128)S(1)}, s32[3,224]{1,0:T(4,128)}, u32[]{:S(2)}) copy-start(s32[3,224]{1,0:T(4,128)} %param.20) | copy-start | bytes 8068
  7.2 138.0 %all-gather.4.cloned.1.call-start = ((), (), s32[]{:S(2)}) async-start(), calls=%async_computation | async-start | bytes 4718592 | tf_op jit(solution)/shard_map/all_gather | solution.py:114
  54.0 219.1 %copy-start.12 = (bf16[16,128,128]{2,1,0:T(8,128)(2,1)}, bf16[16,128,128]{2,1,0:T(8,128)(2,1)S(1)}, u32[]{:S(2)}) copy-start(bf16[16,128,128]{2,1,0:T(8,128)(2,1)S(1)} %gather_fusion) | copy-start | bytes 1572868
  54.0 39.2 %copy-start.19 = (f32[32]{0:T(128)S(1)}, f32[32]{0:T(128)}, u32[]{:S(2)}) copy-start(f32[32]{0:T(128)} %param.16) | copy-start | bytes 388
  54.0 54.4 %copy-start.16 = (f32[1024]{0:T(1024)S(1)}, f32[1024]{0:T(1024)}, u32[]{:S(2)}) copy-start(f32[1024]{0:T(1024)} %param.17) | copy-start | bytes 12292
  56.6 35.0 %copy-start.14 = (f32[16,128,128]{2,1,0:T(8,128)}, f32[16,128,128]{2,1,0:T(8,128)S(1)}, u32[]{:S(2)}) copy-start(f32[16,128,128]{2,1,0:T(8,128)S(1)} %get-tuple-element.42) | copy-start | bytes 3145732
  56.6 308.3 %all-gather.6.cloned.1.call-start = ((), (), s32[]{:S(2)}) async-start(), calls=%async_computation.1 | async-start | bytes 4718592 | tf_op jit(solution)/shard_map/all_gather | solution.py:114
  84.0 24.4 %collective-permute-start = (f32[1024,128]{1,0:T(8,128)}, f32[1024,128]{1,0:T(8,128)}, u32[]{:S(2)}, u32[]{:S(2)}) collective-permute-start(f32[1024,128]{1,0:T(8,128)} %slice.115), channel_id=1, source_target_pairs={{0,1},{1,2},{2,3},{3,4},{4,5},{5,6},{6,7},{8,9},{9,10},{10,11},{11... | collective-permute-start | bytes 1572872 | tf_op jit(solution)/shard_map/ppermute | solution.py:14
  109.7 16.3 %collective-permute-start.1 = (f32[1024,128]{1,0:T(8,128)S(1)}, f32[1024,128]{1,0:T(8,128)S(1)}, u32[]{:S(2)}, u32[]{:S(2)}) collective-permute-start(f32[1024,128]{1,0:T(8,128)S(1)} %fusion.11), channel_id=1, source_target_pairs={{1,0},{2,1},{3,2},{4,3},{5,4},{6,5},{7,6},{9,8},{10,9},{11,10},{12... | collective-permute-start | bytes 1572872 | tf_op jit(solution)/shard_map/ppermute | solution.py:14
  212.3 5.5 copy-start.1
  212.3 5.5 copy-start.15
  273.1 1.0 copy-start.4
  275.2 57.2 %copy-start.6 = (f32[16,128,128]{2,1,0:T(8,128)}, f32[16,128,128]{2,1,0:T(8,128)S(1)}, u32[]{:S(2)}) copy-start(f32[16,128,128]{2,1,0:T(8,128)S(1)} %get-tuple-element.44) | copy-start | bytes 3145732
  275.2 57.2 %copy-start.11 = (bf16[16,128,128]{2,1,0:T(8,128)(2,1)S(1)}, bf16[16,128,128]{2,1,0:T(8,128)(2,1)}, u32[]{:S(2)}) copy-start(bf16[16,128,128]{2,1,0:T(8,128)(2,1)} %get-tuple-element.43) | copy-start | bytes 1572868
  275.2 310.2 %all-gather.8.cloned.1.call-start = ((), (), s32[]{:S(2)}) async-start(), calls=%async_computation.2 | async-start | bytes 4718592 | tf_op jit(solution)/shard_map/all_gather | solution.py:114
  302.3 27.8 %collective-permute-start.2 = (f32[1024,128]{1,0:T(8,128)S(1)}, f32[1024,128]{1,0:T(8,128)S(1)}, u32[]{:S(2)}, u32[]{:S(2)}) collective-permute-start(f32[1024,128]{1,0:T(8,128)S(1)} %slice.119), channel_id=1, source_target_pairs={{0,1},{1,2},{2,3},{3,4},{4,5},{5,6},{6,7},{8,9},{9,10},{10,11},{11... | collective-permute-start | bytes 1572872 | tf_op jit(solution)/shard_map/ppermute | solution.py:14
  331.1 13.5 %collective-permute-start.3 = (f32[1024,128]{1,0:T(8,128)}, f32[1024,128]{1,0:T(8,128)}, u32[]{:S(2)}, u32[]{:S(2)}) collective-permute-start(f32[1024,128]{1,0:T(8,128)} %fusion.10), channel_id=1, source_target_pairs={{1,0},{2,1},{3,2},{4,3},{5,4},{6,5},{7,6},{9,8},{10,9},{11,10},{12... | collective-permute-start | bytes 1572872 | tf_op jit(solution)/shard_map/ppermute | solution.py:14
  432.0 10.2 %copy-start.2 = (f32[16,128,128]{2,1,0:T(8,128)S(1)}, f32[16,128,128]{2,1,0:T(8,128)}, u32[]{:S(2)}) copy-start(f32[16,128,128]{2,1,0:T(8,128)} %param.14) | copy-start | bytes 3145732
  434.4 57.0 %copy-start.5 = (f32[16,128,128]{2,1,0:T(8,128)S(1)}, f32[16,128,128]{2,1,0:T(8,128)}, u32[]{:S(2)}) copy-start(f32[16,128,128]{2,1,0:T(8,128)} %copy-done.4) | copy-start | bytes 3145732
  438.5 55.5 %copy-start.13 = (bf16[16,128,128]{2,1,0:T(8,128)(2,1)S(1)}, bf16[16,128,128]{2,1,0:T(8,128)(2,1)}, u32[]{:S(2)}) copy-start(bf16[16,128,128]{2,1,0:T(8,128)(2,1)} %copy-done.12) | copy-start | bytes 1572868
  492.9 1.0 copy-start.9
  495.1 52.6 %copy-start.8 = (f32[16,128,128]{2,1,0:T(8,128)}, f32[16,128,128]{2,1,0:T(8,128)S(1)}, u32[]{:S(2)}) copy-start(f32[16,128,128]{2,1,0:T(8,128)S(1)} %get-tuple-element.46) | copy-start | bytes 3145732
  495.1 52.6 %copy-start.10 = (bf16[16,128,128]{2,1,0:T(8,128)(2,1)S(1)}, bf16[16,128,128]{2,1,0:T(8,128)(2,1)}, u32[]{:S(2)}) copy-start(bf16[16,128,128]{2,1,0:T(8,128)(2,1)} %get-tuple-element.45) | copy-start | bytes 1572868
  521.8 23.7 %collective-permute-start.4 = (f32[1024,128]{1,0:T(8,128)S(1)}, f32[1024,128]{1,0:T(8,128)S(1)}, u32[]{:S(2)}, u32[]{:S(2)}) collective-permute-start(f32[1024,128]{1,0:T(8,128)S(1)} %slice.125), channel_id=1, source_target_pairs={{0,1},{1,2},{2,3},{3,4},{4,5},{5,6},{6,7},{8,9},{9,10},{10,11},{11... | collective-permute-start | bytes 1572872 | tf_op jit(solution)/shard_map/ppermute | solution.py:14
  546.4 18.6 %collective-permute-start.5 = (f32[1024,128]{1,0:T(8,128)}, f32[1024,128]{1,0:T(8,128)}, u32[]{:S(2)}, u32[]{:S(2)}) collective-permute-start(f32[1024,128]{1,0:T(8,128)} %fusion.9), channel_id=1, source_target_pairs={{1,0},{2,1},{3,2},{4,3},{5,4},{6,5},{7,6},{9,8},{10,9},{11,10},{12... | collective-permute-start | bytes 1572872 | tf_op jit(solution)/shard_map/ppermute | solution.py:14
  652.5 10.2 %copy-start.3 = (f32[16,128,128]{2,1,0:T(8,128)S(1)}, f32[16,128,128]{2,1,0:T(8,128)}, u32[]{:S(2)}) copy-start(f32[16,128,128]{2,1,0:T(8,128)} %param.14) | copy-start | bytes 3145732
  654.9 57.2 %copy-start.7 = (f32[16,128,128]{2,1,0:T(8,128)S(1)}, f32[16,128,128]{2,1,0:T(8,128)}, u32[]{:S(2)}) copy-start(f32[16,128,128]{2,1,0:T(8,128)} %copy-done.6) | copy-start | bytes 3145732
Sparse Core Ops, SparseCore 0:
  56.7 86.9 all-gather.3
  275.3 86.9 all-gather.5
  495.3 87.1 all-gather.7
where the time goes:
time: 731 us; the launch traced here: 722 us
  other arithmetic  215 us (29%)
  blocking collectives  185 us (25%)
  local copies, waits for them, and re-layouts  144 us (20%)
  waiting for transfers between devices  101 us (14%)
  matrix products  44.6 us (6%)
  starting transfers between devices  17.5 us (2%)
  between operations  14.4 us (2%)
    psum x3, blocking collectives, on_device(): lax.psum((local_dots, system_dot(image, image)), ('wide', 'narrow'))  143 us
    ppermute x6, waiting for transfers between devices, shifted(): return lax.ppermute(block, axis, route)  101 us
    scatter-add x3, other arithmetic, on_device(): flux = flux + jax.ops.segment_sum(coupled, row_block, block_count)  88.2 us
    dot_general x3, local copies, waits for them, and re-layouts, on_device(): jnp.einsum('eab,ebc->eac', couple_blocks, jnp.take(whole, flat_index, axi...  45.3 us
    psum x1, blocking collectives, on_device(): lax.psum(system_dot(right_side, right_side), ('wide', 'narrow'))  42 us
    scatter-add x3, other arithmetic, node_drop(): jax.ops.segment_sum(rows, second, 2 * nodes_dev)  37.8 us
    scatter-add x3, other arithmetic, node_drop(): jax.ops.segment_sum(rows, first, 2 * nodes_dev)  37.4 us
    dot_general x3, matrix products, on_device(): jnp.einsum('eab,ebc->eac', couple_blocks, jnp.take(whole, flat_index, axi...  36.1 us
  transfers between devices with their start and end apart: 9, of which 6 were waited for; matrix products, arithmetic and copies ran while one was open for 21% of the time, Pallas kernels for 0%

commit v1 on v0

v1 whole, which is shorter than its diff:
```python
import functools
import jax
import jax.numpy as jnp
from jax import lax
from jax.experimental import pallas as pl
from jax.experimental.pallas import tpu as pltpu
from jax.sharding import PartitionSpec as P

F = 32
CASES = 2
ITERS = 3
CAP = 4
AXES = ("wide", "narrow")
STEP = 2.0**-8
LIMIT = 60 * 1024 * 1024
f32 = jnp.float32
bf16 = jnp.bfloat16
i32 = jnp.int32


def whole(shape, dtype):
    return jax.ShapeDtypeStruct(shape, dtype)


VM = pl.BlockSpec(memory_space=pltpu.VMEM)
SM = pl.BlockSpec(memory_space=pltpu.SMEM)


def lane_is_real(shape):
    lane = lax.broadcasted_iota(i32, shape, len(shape) - 1)
    return lax.rem(lane, 2 * F) < F


def both_parts(row):
    other = jnp.where(lane_is_real(row.shape), pltpu.roll(row, 128 - F, 1), pltpu.roll(row, F, 1))
    return row + other


def turned(values):
    return jnp.where(
        lane_is_real(values.shape),
        -pltpu.roll(values, 128 - F, 1),
        pltpu.roll(values, F, 1),
    )


def setup_kernel(peers, blocks, lists_ref, right_ref, pcoef_ref, pay_ref, slot_ref):
    keys = peers * blocks
    entries = lists_ref.shape[1]
    column = lists_ref[1:2, :]
    owner = lists_ref[2:3, :]
    key = owner * blocks + column
    one = (lax.broadcasted_iota(i32, (keys, entries), 0) == key).astype(f32)
    present = jnp.max(one, axis=1, keepdims=True)
    row = lax.broadcasted_iota(i32, (keys, keys), 0)
    col = lax.broadcasted_iota(i32, (keys, keys), 1)
    before = jnp.where((row // blocks == col // blocks) & (col <= row), 1.0, 0.0).astype(bf16)
    rank = jnp.dot(
        before,
        jnp.broadcast_to(present, (keys, 128)).astype(bf16),
        preferred_element_type=f32,
    )
    place = jnp.sum(one * (rank[:, :1] - 1.0), axis=0, keepdims=True)
    slot_ref[...] = owner * CAP + place.astype(i32)
    lane = lax.broadcasted_iota(i32, (keys, 128), 1)
    name = lax.broadcasted_iota(i32, (keys, 128), 0)
    chosen = (
        (name // blocks == lane // CAP)
        & (rank == (lane % CAP + 1).astype(f32))
        & (present > 0.0)
    )
    needs = jnp.sum(jnp.where(chosen, (name % blocks).astype(f32), 0.0), axis=0, keepdims=True)
    right = right_ref[...]
    squares = jnp.sum(jnp.sum(right * right, axis=0), axis=0, keepdims=True)
    rows = jnp.concatenate([squares, needs, jnp.zeros((6, 128), f32), pcoef_ref[...]], axis=0)
    pay_ref[...] = jnp.broadcast_to(rows[None], pay_ref.shape)


def emit(w_of, jacobi_ref, needs_ref, table_ref, ends_ref, z_ref, zb_ref, send_ref, near_ref, far_ref):
    blocks = z_ref.shape[0]
    size = z_ref.shape[1]
    nodes = near_ref.shape[0]
    for n in range(blocks):
        z = jnp.dot(table_ref[jacobi_ref[n]], w_of(n).astype(bf16), preferred_element_type=f32)
        z_ref[n] = z
        zb_ref[n] = z.astype(bf16)
    peers = send_ref.shape[0]
    for j in range(peers):
        for s in range(CAP):
            send_ref[j, s] = zb_ref[needs_ref[j, s]]
    field = zb_ref[...].reshape(blocks * size, zb_ref.shape[2])
    chunk = 256
    for part, out in ((0, near_ref), (1, far_ref)):

        def body(step, carry, part=part, out=out):
            start = pl.multiple_of(step * chunk, chunk)
            node = lax.broadcasted_iota(i32, (chunk, blocks * size), 0) + (start + part * nodes)
            first = (node == ends_ref[0:1, :]).astype(f32)
            second = (node == ends_ref[1:2, :]).astype(f32)
            gather = (first - second).astype(bf16)
            out[pl.ds(start, chunk), :] = jnp.dot(
                gather, field, preferred_element_type=f32
            ).astype(bf16)
            return carry

        lax.fori_loop(0, nodes // chunk, body, 0)


def start_kernel(
    pay_ref, right_ref, jacobi_ref, needs_ref, table_ref, ends_ref,
    w_ref, z_ref, zb_ref, send_ref, near_ref, far_ref, beta_ref,
):
    total = jnp.sum(pay_ref[:, 0, :], axis=0, keepdims=True)
    beta = jnp.sqrt(both_parts(total))
    beta_ref[...] = jnp.broadcast_to(beta, beta_ref.shape)
    w_ref[...] = right_ref[...] / beta[None]
    emit(
        lambda n: w_ref[n], jacobi_ref, needs_ref, table_ref, ends_ref,
        z_ref, zb_ref, send_ref, near_ref, far_ref,
    )


def local_kernel(
    z_ref, zb_ref, self_ref, res_ref, freq_ref, near_ref, far_ref, arrived_ref, beyond_ref,
    scale_ref, cols_ref, part_ref, pot_ref,
):
    blocks, size, width = z_ref.shape
    nodes = near_ref.shape[0]
    pot_ref[:nodes] = (
        scale_ref[:nodes] * (near_ref[...].astype(f32) + arrived_ref[...].astype(f32))
    ).astype(bf16)
    pot_ref[nodes:] = (
        scale_ref[nodes:] * (far_ref[...].astype(f32) + beyond_ref[...].astype(f32))
    ).astype(bf16)
    freq = freq_ref[...]

    def body(n, carry):
        start = pl.multiple_of(n * size, size)
        ends = cols_ref[pl.ds(start, size), :]
        node = lax.broadcasted_iota(i32, (size, 2 * nodes), 1)
        first = (node == ends[:, 0:1]).astype(f32)
        second = (node == ends[:, 1:2]).astype(f32)
        spread = (first - second).astype(bf16)
        drop = jnp.dot(spread, pot_ref[...], preferred_element_type=f32)
        flux = jnp.dot(self_ref[n], zb_ref[n], preferred_element_type=f32)
        part_ref[n] = res_ref[pl.ds(start, size), :] * z_ref[n] + turned(freq * flux - drop / freq)
        return carry

    lax.fori_loop(0, blocks, body, 0)


def couple_step(entries, row_ref, slot_ref, couple_ref, arrived_ref, acc_ref):
    step = pl.program_id(0)

    @pl.when(step == 0)
    def _():
        acc_ref[...] = jnp.zeros_like(acc_ref)

    for j in range(entries):
        e = step * entries + j
        row = row_ref[e]
        acc_ref[row] += jnp.dot(
            couple_ref[j], arrived_ref[slot_ref[e]], preferred_element_type=f32
        )


def image_of(part_ref, freq_ref, acc_ref, n):
    return STEP * (part_ref[n] + turned(freq_ref[...] * acc_ref[n]))


def middle_kernel(
    entries, row_ref, slot_ref, couple_ref, arrived_ref, part_ref, freq_ref,
    jacobi_ref, needs_ref, table_ref, ends_ref,
    w_ref, z_ref, zb_ref, send_ref, near_ref, far_ref, acc_ref,
):
    couple_step(entries, row_ref, slot_ref, couple_ref, arrived_ref, acc_ref)

    @pl.when(pl.program_id(0) == pl.num_programs(0) - 1)
    def _():
        for n in range(w_ref.shape[0]):
            w_ref[n] = image_of(part_ref, freq_ref, acc_ref, n)
        emit(
            lambda n: w_ref[n], jacobi_ref, needs_ref, table_ref, ends_ref,
            z_ref, zb_ref, send_ref, near_ref, far_ref,
        )


PAIRS = [(i, j) for j in range(ITERS + 1) for i in range(j + 1)]


def last_kernel(
    entries, row_ref, slot_ref, couple_ref, arrived_ref, part_ref, freq_ref,
    w0_ref, w1_ref, w2_ref, pay_ref, acc_ref,
):
    couple_step(entries, row_ref, slot_ref, couple_ref, arrived_ref, acc_ref)

    @pl.when(pl.program_id(0) == pl.num_programs(0) - 1)
    def _():
        blocks = acc_ref.shape[0]

        def body(n, sums):
            w = [w0_ref[n], w1_ref[n], w2_ref[n], image_of(part_ref, freq_ref, acc_ref, n)]
            fresh = []
            for at, (i, j) in enumerate(PAIRS):
                product = (w[i] * w[j]).reshape(-1, 8, 128)
                fresh.append(sums[at] + jnp.sum(product, axis=0))
            return tuple(fresh)

        sums = lax.fori_loop(0, blocks, body, tuple(jnp.zeros((8, 128), f32) for _ in PAIRS))
        rows = [jnp.sum(s, axis=0, keepdims=True) for s in sums]
        rows.append(jnp.zeros((16 - len(rows), 128), f32))
        pay_ref[...] = jnp.broadcast_to(jnp.concatenate(rows, axis=0)[None], pay_ref.shape)


def finish_kernel(pay_ref, beta_ref, z0_ref, z1_ref, z2_ref, out_ref, norm_ref):
    total = both_parts(jnp.sum(pay_ref[...], axis=0))
    gram = {}
    for at, (i, j) in enumerate(PAIRS):
        gram[i, j] = gram[j, i] = total[at : at + 1, :]
    order = list(range(1, ITERS + 1)) + [0]
    low = {}
    for i in range(ITERS + 1):
        for j in range(i + 1):
            value = gram[order[i], order[j]]
            for k in range(j):
                value = value - low[i, k] * low[j, k]
            low[i, j] = jnp.sqrt(jnp.maximum(value, 0.0)) if i == j else value / low[j, j]
    weights = [None] * ITERS
    for i in reversed(range(ITERS)):
        value = low[ITERS, i]
        for k in range(i + 1, ITERS):
            value = value - low[k, i] * weights[k]
        weights[i] = value / low[i, i]
    beta = beta_ref[0:1, :]
    norm_ref[...] = jnp.broadcast_to(low[ITERS, ITERS] * beta, norm_ref.shape)
    weights = [STEP * beta * weight for weight in weights]
    for n in range(out_ref.shape[0]):
        out_ref[n] = weights[0] * z0_ref[n] + weights[1] * z1_ref[n] + weights[2] * z2_ref[n]


def call(kernel, outs, ins, **more):
    return pl.pallas_call(
        kernel,
        out_shape=outs,
        in_specs=ins,
        out_specs=[VM] * len(outs),
        compiler_params=pltpu.CompilerParams(vmem_limit_bytes=LIMIT),
        **more,
    )


def on_device(
    right_side, resistance, omega, pcoef, branch_nodes, self_blocks, couple_list, couple_blocks,
    jacobi_ids, preconditioners,
):
    blocks, size, width = right_side.shape
    nodes = pcoef.shape[0]
    entries = couple_list.shape[1]
    peers = lax.axis_size("narrow")
    devices = peers * lax.axis_size("wide")
    group = lax.axis_index("wide")
    mine = lax.axis_index("narrow")
    node_rows = nodes // 128
    freq = jnp.tile(omega, 2 * CASES).reshape(1, width)
    ends = jnp.transpose(branch_nodes, (1, 0, 2)).reshape(2, blocks * size)
    ends_col = jnp.transpose(ends)
    res_col = resistance.reshape(blocks * size, 1)

    pay, slots = call(
        functools.partial(setup_kernel, peers, blocks),
        [whole((devices, 8 + node_rows, 128), f32), whole((1, entries), i32)],
        [VM] * 3,
    )(couple_list, right_side, pcoef.reshape(node_rows, 128))
    pay = lax.all_to_all(pay, AXES, 0, 0)
    slots = slots.reshape(entries)
    rows = couple_list[0]
    needs = lax.dynamic_slice(
        pay, (group * peers, 1, mine * CAP), (peers, 1, CAP)
    ).reshape(peers, CAP).astype(i32)
    next_dev = jnp.minimum(group * peers + mine + 1, devices - 1)
    next_pcoef = lax.dynamic_slice(pay, (next_dev, 8, 0), (1, node_rows, 128)).reshape(nodes)
    scale = jnp.concatenate([pcoef, next_pcoef]).reshape(2 * nodes, 1)

    vec = whole((blocks, size, width), f32)
    emitted = [
        vec,
        vec,
        whole((blocks, size, width), bf16),
        whole((peers, CAP, size, width), bf16),
        whole((nodes, width), bf16),
        whole((nodes, width), bf16),
    ]
    w, z, zb, send, near, far, beta = call(
        start_kernel,
        emitted + [whole((8, width), f32)],
        [VM, VM, SM, SM, VM, VM],
    )(pay, right_side, jacobi_ids, needs, preconditioners, ends)
    basis = [w]
    fields = [z]
    chunk = 16
    while entries % chunk:
        chunk //= 2
    constant = pl.BlockSpec(memory_space=pltpu.VMEM)
    for step in range(ITERS):
        arrived = lax.ppermute(far, "narrow", [(i, i + 1) for i in range(peers - 1)])
        beyond = lax.ppermute(near, "narrow", [(i + 1, i) for i in range(peers - 1)])
        incoming = lax.all_to_all(send, "narrow", 0, 0).reshape(peers * CAP, size, width)
        (part,) = call(
            local_kernel,
            [vec],
            [VM] * 11,
            scratch_shapes=[pltpu.VMEM((2 * nodes, width), bf16)],
        )(z, zb, self_blocks, res_col, freq, near, far, arrived, beyond, scale, ends_col)
        streamed = pl.BlockSpec((chunk, size, size), lambda i: (i, 0, 0))
        common = (rows, slots, couple_blocks, incoming, part, freq)
        specs = [SM, SM, streamed, constant, constant, constant]
        more = dict(
            grid=(entries // chunk,),
            scratch_shapes=[pltpu.VMEM((blocks, size, width), f32)],
        )
        if step + 1 < ITERS:
            w, z, zb, send, near, far = call(
                functools.partial(middle_kernel, chunk),
                emitted,
                specs + [SM, SM, constant, constant],
                **more,
            )(*common, jacobi_ids, needs, preconditioners, ends)
            basis.append(w)
            fields.append(z)
        else:
            (sums,) = call(
                functools.partial(last_kernel, chunk),
                [whole((devices, 16, 128), f32)],
                specs + [constant] * 3,
                **more,
            )(*common, *basis)
    sums = lax.all_to_all(sums, AXES, 0, 0)
    result, norms = call(
        finish_kernel, [vec, whole((8, width), f32)], [VM] * 5
    )(sums, beta, *fields)
    return result, norms[0].reshape(CASES, 2, F)[:, 0, :]


def solution(mesh):
    placed = (
        P(AXES, None, None),
        P(AXES, None),
        P(),
        P(AXES),
        P(AXES, None, None),
        P(AXES, None, None),
        P(None, AXES),
        P(AXES, None, None),
        P(AXES),
        P(),
    )
    return jax.shard_map(
        on_device,
        mesh=mesh,
        in_specs=placed,
        out_specs=(P(AXES, None, None), P()),
        check_vma=False,
    )
```

time: 731 us -> 247 us (0.34); the launches traced: 722 us -> 246 us
  other arithmetic: 215 us -> 0.68 us
  blocking collectives: 185 us -> 22.8 us
  local copies, waits for them, and re-layouts: 144 us -> 13.9 us
  Pallas kernels: 0 us -> 103 us
  waiting for transfers between devices: 101 us -> 52.2 us
  matrix products: 44.6 us -> 0 us
  starting transfers between devices: 17.5 us -> 52.6 us
  between operations: 14.4 us -> 0.78 us
    psum x4 -> x0, blocking collectives: 185 us -> none  [the longest x3 143 us: on_device(): lax.psum((local_dots, system_dot(image, image)), ('wide', 'narrow'))]
    scatter-add x9 -> x0, other arithmetic: 163 us -> none  [the longest x3 88.2 us: on_device(): flux = flux + jax.ops.segment_sum(coupled, row_block, block_count)]
    pallas_call x0 -> x9, Pallas kernels: none -> 103 us  [the longest x3 37.8 us: on_device(): call(local_kernel, [vec], [VM] * 11, scratch_shapes=[pltpu.VMEM((2 * node...]
    gather x10 -> x0, local copies, waits for them, and re-layouts: 78.6 us -> none  [the longest x3 31.6 us: on_device(): jnp.take(whole, flat_index, axis=0)]
    ppermute x6, waiting for transfers between devices: 101 us -> 43.6 us  [the longest x3 30.4 us: on_device(): lax.ppermute(near, 'narrow', [(i + 1, i) for i in range(peers - 1)])]
    dot_general x6 -> x0, local copies, waits for them, and re-layouts: 47.6 us -> none  [the longest x3 45.3 us: on_device(): jnp.einsum('eab,ebc->eac', couple_blocks, jnp.take(whole, flat_index, axi...]
    dot_general x9 -> x0, matrix products: 44.6 us -> none  [the longest x3 36.1 us: on_device(): jnp.einsum('eab,ebc->eac', couple_blocks, jnp.take(whole, flat_index, axi...]
    all_to_all x0 -> x4, starting transfers between devices: none -> 35.1 us  [the longest x3 27.8 us: on_device(): lax.all_to_all(send, 'narrow', 0, 0).reshape(peers * CAP, size, width)]
  transfers between devices with their start and end apart: 9 -> 10, of which waited for: 6 -> 7; matrix products, arithmetic and copies ran while one was open for 21% -> 3% of each run, Pallas kernels for 0% -> 15%
where the time goes in v1:
time: 247 us; the launch traced here: 246 us
  Pallas kernels  103 us (42%)
  starting transfers between devices  52.6 us (21%)
  waiting for transfers between devices  52.2 us (21%)
  blocking collectives  22.8 us (9%)
  local copies, waits for them, and re-layouts  13.9 us (6%)
    pallas_call x3, Pallas kernels, on_device(): call(local_kernel, [vec], [VM] * 11, scratch_shapes=[pltpu.VMEM((2 * node...  37.8 us
    pallas_call x2, Pallas kernels, on_device(): call(functools.partial(middle_kernel, chunk), emitted, specs + [SM, SM, c...  37.5 us
    ppermute x3, waiting for transfers between devices, on_device(): lax.ppermute(near, 'narrow', [(i + 1, i) for i in range(peers - 1)])  30.4 us
    all_to_all x3, starting transfers between devices, on_device(): lax.all_to_all(send, 'narrow', 0, 0).reshape(peers * CAP, size, width)  27.8 us
    all_to_all x1, blocking collectives, on_device(): sums = lax.all_to_all(sums, AXES, 0, 0)  22.8 us
    pallas_call x1, Pallas kernels, on_device(): call(functools.partial(last_kernel, chunk), [whole((devices, 16, 128), f3...  14.5 us
    ppermute x3, starting transfers between devices, on_device(): lax.ppermute(far, 'narrow', [(i, i + 1) for i in range(peers - 1)])  13.7 us
    ppermute x3, waiting for transfers between devices, on_device(): lax.ppermute(far, 'narrow', [(i, i + 1) for i in range(peers - 1)])  13.2 us
  transfers between devices with their start and end apart: 10, of which 7 were waited for; matrix products, arithmetic and copies ran while one was open for 3% of the time, Pallas kernels for 15%

profile of v1, /device:TPU:0, one launch (start us, length us, event | category | flops | bytes accessed | tf_op | source)
XLA Modules:
  0.0 246.1 jit_solution(12290042724973777946)
XLA Ops:
  0.6 0.0 copy-start.11
  0.6 0.0 copy-start.13
  0.7 0.0 copy-start.12
  0.7 2.2 shard_map.113
  2.9 7.3 %all-to-all-start = ((f32[32,16,128]{2,1,0:T(8,128)}), f32[32,16,128]{2,1,0:T(8,128)S(1)}, u32[]{:S(2)}, u32[]{:S(2)}) async-start(f32[32,16,128]{2,1,0:T(8,128)} %get-tuple-element.26), calls=%async_computation | async-start | bytes 524288 | tf_op jit(solution)/shard_map/all_to_all | solution.py:274
  10.2 1.1 copy.35
  11.3 0.0 copy-start
  11.3 1.0 copy.37.ends_ref
  12.3 8.6 %all-to-all-done.pay_ref = f32[32,16,128]{2,1,0:T(8,128)S(1)} async-done(((f32[32,16,128]{2,1,0:T(8,128)}), f32[32,16,128]{2,1,0:T(8,128)S(1)}, u32[]{:S(2)}, u32[]{:S(2)}) %all-to-all-start) | async-done | bytes 262176 | tf_op jit(solution)/shard_map/all_to_all | solution.py:274
  20.8 0.0 copy-start.4
  20.8 0.7 dynamic-slice_convert_fusion
  21.5 0.0 copy-done.4
  21.5 7.9 %shard_map.114 = (f32[16,128,128]{2,1,0:T(8,128)}, f32[16,128,128]{2,1,0:T(8,128)}, bf16[16,128,128]{2,1,0:T(8,128)(2,1)}, bf16[8,4,128,128]{3,2,1,0:T(8,128)(2,...) custom-call(f32[32,16,128]{2,1,0:T(8,128)} %copy-done.4, f32[16,128,128]{2,1,0:T(8,128)} %right_ref.3, ...), custom_call_target="tpu_custom_call" | custom-call | tf_op jit(solution)/shard_map/pallas_call | solution.py:293
  29.5 3.6 %all-to-all-start.1 = ((bf16[8,4,128,128]{3,2,1,0:T(8,128)(2,1)}), bf16[8,4,128,128]{3,2,1,0:T(8,128)(2,1)S(1)}, u32[]{:S(2)}, u32[]{:S(2)}) async-start(bf16[8,4,128,128]{3,2,1,0:T(8,128)(2,1)} %get-tuple-element.27), calls=%async_computation.1 | async-start | bytes 2097152 | tf_op jit(solution)/shard_map/all_to_all | solution.py:307
  33.0 1.3 collective-permute-start.1
  34.3 4.6 %collective-permute-start = (bf16[1024,128]{1,0:T(8,128)(2,1)}, bf16[1024,128]{1,0:T(8,128)(2,1)S(1)}, u32[]{:S(2)}, u32[]{:S(2)}) collective-permute-start(bf16[1024,128]{1,0:T(8,128)(2,1)} %get-tuple-element.31.far_ref), channel_id=1, source_target_pairs={{0,1},{1,2},{2,3},{3,4},{4,5},{5,6},{6,7},{8,9},{9,10},{10,11},{11... | collective-permute-start | bytes 786440 | tf_op jit(solution)/shard_map/ppermute | solution.py:305
  38.9 1.3 slice.9
  40.2 0.0 copy-done.13
  40.2 0.7 reshape_tile.3.freq_ref
  40.8 0.0 copy-done.12
  40.8 1.3 copy.38.res_ref
  42.2 0.7 dynamic-slice_bitcast_fusion
  42.8 0.0 copy-done.11
  42.8 1.4 copy.39.scale_ref
  44.2 6.5 %collective-permute-done.1.beyond_ref = bf16[1024,128]{1,0:T(8,128)(2,1)S(1)} collective-permute-done((bf16[1024,128]{1,0:T(8,128)(2,1)}, bf16[1024,128]{1,0:T(8,128)(2,1)S(1)}, u32[]{:S(2)}, u32[]{:S(2)}) %collective-permute-start.1) | collective-permute-done | bytes 262176 | tf_op jit(solution)/shard_map/ppermute | solution.py:306
  50.7 0.0 copy-start.5
  50.7 4.7 %collective-permute-done.arrived_ref = bf16[1024,128]{1,0:T(8,128)(2,1)S(1)} collective-permute-done((bf16[1024,128]{1,0:T(8,128)(2,1)}, bf16[1024,128]{1,0:T(8,128)(2,1)S(1)}, u32[]{:S(2)}, u32[]{:S(2)}) %collective-permute-start) | collective-permute-done | bytes 262176 | tf_op jit(solution)/shard_map/ppermute | solution.py:305
  55.4 0.0 copy-start.6
  55.4 0.0 copy-done
  55.4 0.0 copy-done.5
  55.4 0.7 copy-done.6
  56.1 12.6 %shard_map.115.part_ref = f32[16,128,128]{2,1,0:T(8,128)} custom-call(f32[16,128,128]{2,1,0:T(8,128)} %get-tuple-element.28.z_ref.z0_ref, bf16[16,128,128]{2,1,0:T(8,128)(2,1)} %get-tuple-element.29.zb_ref, bf16[16,128,128]{2,1,0:T(8,128)(2,1)} %self_ref.5, f32[2048,1]{1,0:T(8,128)} %copy.38.res_ref, f32[1,128]{1,0:T(1,128)} %reshape_tile.3.freq_ref, ...), custom_call_target="tpu_custom_call" | custom-call | tf_op jit(solution)/shard_map/pallas_call | solution.py:308
  68.7 0.0 all-to-all-done.1
  68.7 0.0 copy-start.1
  68.7 1.0 copy-done.1
  69.8 18.8 %shard_map.116 = (f32[16,128,128]{2,1,0:T(8,128)}, f32[16,128,128]{2,1,0:T(8,128)}, bf16[16,128,128]{2,1,0:T(8,128)(2,1)}, bf16[8,4,128,128]{3,2,1,0:T(8,128)(2,...) custom-call(s32[224]{0:T(256)} %bitcast.29, s32[224]{0:T(256)} %bitcast.32, bf16[224,128,128]{2,1,0:T(8,128)(2,1)} %couple_ref.5, ...), custom_call_target="tpu_custom_call" | custom-call | tf_op jit(solution)/shard_map/pallas_call | solution.py:322
  88.5 12.0 %all-to-all-start.2 = ((bf16[8,4,128,128]{3,2,1,0:T(8,128)(2,1)}), bf16[8,4,128,128]{3,2,1,0:T(8,128)(2,1)S(1)}, u32[]{:S(2)}, u32[]{:S(2)}) async-start(bf16[8,4,128,128]{3,2,1,0:T(8,128)(2,1)} %get-tuple-element.32), calls=%async_computation.2 | async-start | bytes 2097152 | tf_op jit(solution)/shard_map/all_to_all | solution.py:307
  100.5 1.3 collective-permute-start.3
  101.8 4.6 %collective-permute-start.2 = (bf16[1024,128]{1,0:T(8,128)(2,1)}, bf16[1024,128]{1,0:T(8,128)(2,1)S(1)}, u32[]{:S(2)}, u32[]{:S(2)}) collective-permute-start(bf16[1024,128]{1,0:T(8,128)(2,1)} %get-tuple-element.36.far_ref), channel_id=1, source_target_pairs={{0,1},{1,2},{2,3},{3,4},{4,5},{5,6},{6,7},{8,9},{9,10},{10,11},{11... | collective-permute-start | bytes 786440 | tf_op jit(solution)/shard_map/ppermute | solution.py:305
  106.4 11.9 %collective-permute-done.3.beyond_ref = bf16[1024,128]{1,0:T(8,128)(2,1)S(1)} collective-permute-done((bf16[1024,128]{1,0:T(8,128)(2,1)}, bf16[1024,128]{1,0:T(8,128)(2,1)S(1)}, u32[]{:S(2)}, u32[]{:S(2)}) %collective-permute-start.3) | collective-permute-done | bytes 262176 | tf_op jit(solution)/shard_map/ppermute | solution.py:306
  118.3 0.0 copy-start.8
  118.3 4.3 %collective-permute-done.2.arrived_ref = bf16[1024,128]{1,0:T(8,128)(2,1)S(1)} collective-permute-done((bf16[1024,128]{1,0:T(8,128)(2,1)}, bf16[1024,128]{1,0:T(8,128)(2,1)S(1)}, u32[]{:S(2)}, u32[]{:S(2)}) %collective-permute-start.2) | collective-permute-done | bytes 262176 | tf_op jit(solution)/shard_map/ppermute | solution.py:305
  122.6 0.0 copy-done.8
  122.6 0.7 copy-done.10
  123.3 12.6 %shard_map.117.part_ref = f32[16,128,128]{2,1,0:T(8,128)} custom-call(f32[16,128,128]{2,1,0:T(8,128)} %get-tuple-element.33.z_ref.z1_ref, bf16[16,128,128]{2,1,0:T(8,128)(2,1)} %get-tuple-element.34.zb_ref, bf16[16,128,128]{2,1,0:T(8,128)(2,1)} %self_ref.5, f32[2048,1]{1,0:T(8,128)} %copy.38.res_ref, f32[1,128]{1,0:T(1,128)} %reshape_tile.3.freq_ref, ...), custom_call_target="tpu_custom_call" | custom-call | tf_op jit(solution)/shard_map/pallas_call | solution.py:308
  135.9 0.0 all-to-all-done.2
  135.9 1.0 copy-done.3
  136.9 18.7 %shard_map.118 = (f32[16,128,128]{2,1,0:T(8,128)}, f32[16,128,128]{2,1,0:T(8,128)}, bf16[16,128,128]{2,1,0:T(8,128)(2,1)}, bf16[8,4,128,128]{3,2,1,0:T(8,128)(2,...) custom-call(s32[224]{0:T(256)} %bitcast.30, s32[224]{0:T(256)} %bitcast.33, bf16[224,128,128]{2,1,0:T(8,128)(2,1)} %couple_ref.5, ...), custom_call_target="tpu_custom_call" | custom-call | tf_op jit(solution)/shard_map/pallas_call | solution.py:322
  155.7 12.3 %all-to-all-start.3 = ((bf16[8,4,128,128]{3,2,1,0:T(8,128)(2,1)}), bf16[8,4,128,128]{3,2,1,0:T(8,128)(2,1)S(1)}, u32[]{:S(2)}, u32[]{:S(2)}) async-start(bf16[8,4,128,128]{3,2,1,0:T(8,128)(2,1)} %get-tuple-element.37), calls=%async_computation.3 | async-start | bytes 2097152 | tf_op jit(solution)/shard_map/all_to_all | solution.py:307
  167.9 1.3 collective-permute-start.5
  169.2 4.6 %collective-permute-start.4 = (bf16[1024,128]{1,0:T(8,128)(2,1)}, bf16[1024,128]{1,0:T(8,128)(2,1)S(1)}, u32[]{:S(2)}, u32[]{:S(2)}) collective-permute-start(bf16[1024,128]{1,0:T(8,128)(2,1)} %get-tuple-element.41.far_ref), channel_id=1, source_target_pairs={{0,1},{1,2},{2,3},{3,4},{4,5},{5,6},{6,7},{8,9},{9,10},{10,11},{11... | collective-permute-start | bytes 786440 | tf_op jit(solution)/shard_map/ppermute | solution.py:305
  173.8 11.9 %collective-permute-done.5.beyond_ref = bf16[1024,128]{1,0:T(8,128)(2,1)S(1)} collective-permute-done((bf16[1024,128]{1,0:T(8,128)(2,1)}, bf16[1024,128]{1,0:T(8,128)(2,1)S(1)}, u32[]{:S(2)}, u32[]{:S(2)}) %collective-permute-start.5) | collective-permute-done | bytes 262176 | tf_op jit(solution)/shard_map/ppermute | solution.py:306
  185.7 4.3 %collective-permute-done.4.arrived_ref = bf16[1024,128]{1,0:T(8,128)(2,1)S(1)} collective-permute-done((bf16[1024,128]{1,0:T(8,128)(2,1)}, bf16[1024,128]{1,0:T(8,128)(2,1)S(1)}, u32[]{:S(2)}, u32[]{:S(2)}) %collective-permute-start.4) | collective-permute-done | bytes 262176 | tf_op jit(solution)/shard_map/ppermute | solution.py:305
  190.0 0.0 copy-done.7
  190.0 0.7 copy-done.9
  190.7 12.6 %shard_map.119.part_ref = f32[16,128,128]{2,1,0:T(8,128)} custom-call(f32[16,128,128]{2,1,0:T(8,128)} %get-tuple-element.38.z_ref.z2_ref, bf16[16,128,128]{2,1,0:T(8,128)(2,1)} %get-tuple-element.39.zb_ref, bf16[16,128,128]{2,1,0:T(8,128)(2,1)} %self_ref.5, f32[2048,1]{1,0:T(8,128)} %copy.38.res_ref, f32[1,128]{1,0:T(1,128)} %reshape_tile.3.freq_ref, ...), custom_call_target="tpu_custom_call" | custom-call | tf_op jit(solution)/shard_map/pallas_call | solution.py:308
  203.3 0.0 all-to-all-done.3
  203.3 1.0 copy-done.2
  204.3 14.5 %shard_map.120 = f32[32,16,128]{2,1,0:T(8,128)} custom-call(s32[224]{0:T(256)} %bitcast.31, s32[224]{0:T(256)} %bitcast.34, bf16[224,128,128]{2,1,0:T(8,128)(2,1)} %couple_ref.5, bf16[32,128,128]{2,1,0:T(8,128)(2,1)} %bitcast.21, f32[16,128,128]{2,1,0:T(8,128)} %shard_map.119.part_ref, f32[1,128]{1,0:T(1,128)} %reshape_tile.3.freq_ref, ...), custom_call_target="tpu_custom_call" | custom-call | tf_op jit(solution)/shard_map/pallas_call | solution.py:331
  218.7 22.8 %all_to_all.25.pay_ref = f32[32,16,128]{2,1,0:T(8,128)} all-to-all(f32[32,16,128]{2,1,0:T(8,128)} %shard_map.120), channel_id=1, replica_groups=mesh['wide'=4,'narrow'=8] {'wide','narrow'}, dimensions={0} | all-to-all | bytes 524288 | tf_op jit(solution)/shard_map/all_to_all | solution.py:337
  241.5 3.3 %shard_map.121 = (f32[16,128,128]{2,1,0:T(8,128)}, f32[8,128]{1,0:T(8,128)}) custom-call(f32[32,16,128]{2,1,0:T(8,128)} %all_to_all.25.pay_ref, f32[8,128]{1,0:T(8,128)} %get-tuple-element.45.beta_ref, f32[16,128,128]{2,1,0:T(8,128)} %get-tuple-element.28.z_ref.z0_ref, f32[16,128,128]{2,1,0:T(8,128)} %get-tuple-element.33.z_ref.z1_ref, ...), custom_call_target="tpu_custom_call" | custom-call | tf_op jit(solution)/shard_map/pallas_call | solution.py:338
  244.8 0.7 slice_reduce_fusion
  245.5 0.1 reshape_squeeze.3
  245.6 0.6 slice.12
  (7 shorter events, 0.0 us)
Async XLA Ops:
  0.6 42.2 %copy-start.11 = (f32[1024]{0:T(1024)S(1)}, f32[1024]{0:T(1024)}, u32[]{:S(2)}) copy-start(f32[1024]{0:T(1024)} %param.13) | copy-start | bytes 12292
  0.6 39.5 %copy-start.13 = (f32[32]{0:T(128)S(1)}, f32[32]{0:T(128)}, u32[]{:S(2)}) copy-start(f32[32]{0:T(128)} %param.12) | copy-start | bytes 388
  0.7 40.2 %copy-start.12 = (f32[16,128]{1,0:T(8,128)S(1)}, f32[16,128]{1,0:T(8,128)}, u32[]{:S(2)}) copy-start(f32[16,128]{1,0:T(8,128)} %param.11) | copy-start | bytes 24580
  2.9 18.0 %all-to-all-start = ((f32[32,16,128]{2,1,0:T(8,128)}), f32[32,16,128]{2,1,0:T(8,128)S(1)}, u32[]{:S(2)}, u32[]{:S(2)}) async-start(f32[32,16,128]{2,1,0:T(8,128)} %get-tuple-element.26), calls=%async_computation | async-start | bytes 524288 | tf_op jit(solution)/shard_map/all_to_all | solution.py:274
  11.3 44.1 %copy-start = (s32[2,16,128]{0,2,1:T(8,128)}, s32[2,16,128]{0,2,1:T(8,128)S(1)}, u32[]{:S(2)}) copy-start(s32[2,16,128]{0,2,1:T(8,128)S(1)} %copy.35) | copy-start | bytes 49156
  20.8 0.7 copy-start.4
  29.5 39.2 %all-to-all-start.1 = ((bf16[8,4,128,128]{3,2,1,0:T(8,128)(2,1)}), bf16[8,4,128,128]{3,2,1,0:T(8,128)(2,1)S(1)}, u32[]{:S(2)}, u32[]{:S(2)}) async-start(bf16[8,4,128,128]{3,2,1,0:T(8,128)(2,1)} %get-tuple-element.27), calls=%async_computation.1 | async-start | bytes 2097152 | tf_op jit(solution)/shard_map/all_to_all | solution.py:307
  33.0 17.7 %collective-permute-start.1 = (bf16[1024,128]{1,0:T(8,128)(2,1)}, bf16[1024,128]{1,0:T(8,128)(2,1)S(1)}, u32[]{:S(2)}, u32[]{:S(2)}) collective-permute-start(bf16[1024,128]{1,0:T(8,128)(2,1)} %get-tuple-element.30.near_ref), channel_id=1, source_target_pairs={{1,0},{2,1},{3,2},{4,3},{5,4},{6,5},{7,6},{9,8},{10,9},{11,10},{12... | collective-permute-start | bytes 786440 | tf_op jit(solution)/shard_map/ppermute | solution.py:306
  34.3 21.1 %collective-permute-start = (bf16[1024,128]{1,0:T(8,128)(2,1)}, bf16[1024,128]{1,0:T(8,128)(2,1)S(1)}, u32[]{:S(2)}, u32[]{:S(2)}) collective-permute-start(bf16[1024,128]{1,0:T(8,128)(2,1)} %get-tuple-element.31.far_ref), channel_id=1, source_target_pairs={{0,1},{1,2},{2,3},{3,4},{4,5},{5,6},{6,7},{8,9},{9,10},{10,11},{11... | collective-permute-start | bytes 786440 | tf_op jit(solution)/shard_map/ppermute | solution.py:305
  50.7 4.7 %copy-start.5 = (bf16[1024,128]{1,0:T(8,128)(2,1)}, bf16[1024,128]{1,0:T(8,128)(2,1)S(1)}, u32[]{:S(2)}) copy-start(bf16[1024,128]{1,0:T(8,128)(2,1)S(1)} %collective-permute-done.1.beyond_ref) | copy-start | bytes 786436
  55.4 0.7 copy-start.6
  68.7 1.0 copy-start.1
  88.5 47.4 %all-to-all-start.2 = ((bf16[8,4,128,128]{3,2,1,0:T(8,128)(2,1)}), bf16[8,4,128,128]{3,2,1,0:T(8,128)(2,1)S(1)}, u32[]{:S(2)}, u32[]{:S(2)}) async-start(bf16[8,4,128,128]{3,2,1,0:T(8,128)(2,1)} %get-tuple-element.32), calls=%async_computation.2 | async-start | bytes 2097152 | tf_op jit(solution)/shard_map/all_to_all | solution.py:307
  100.5 17.8 %collective-permute-start.3 = (bf16[1024,128]{1,0:T(8,128)(2,1)}, bf16[1024,128]{1,0:T(8,128)(2,1)S(1)}, u32[]{:S(2)}, u32[]{:S(2)}) collective-permute-start(bf16[1024,128]{1,0:T(8,128)(2,1)} %get-tuple-element.35.near_ref), channel_id=1, source_target_pairs={{1,0},{2,1},{3,2},{4,3},{5,4},{6,5},{7,6},{9,8},{10,9},{11,10},{12... | collective-permute-start | bytes 786440 | tf_op jit(solution)/shard_map/ppermute | solution.py:306
  101.8 20.8 %collective-permute-start.2 = (bf16[1024,128]{1,0:T(8,128)(2,1)}, bf16[1024,128]{1,0:T(8,128)(2,1)S(1)}, u32[]{:S(2)}, u32[]{:S(2)}) collective-permute-start(bf16[1024,128]{1,0:T(8,128)(2,1)} %get-tuple-element.36.far_ref), channel_id=1, source_target_pairs={{0,1},{1,2},{2,3},{3,4},{4,5},{5,6},{6,7},{8,9},{9,10},{10,11},{11... | collective-permute-start | bytes 786440 | tf_op jit(solution)/shard_map/ppermute | solution.py:305
  118.3 4.3 %copy-start.8 = (bf16[1024,128]{1,0:T(8,128)(2,1)}, bf16[1024,128]{1,0:T(8,128)(2,1)S(1)}, u32[]{:S(2)}) copy-start(bf16[1024,128]{1,0:T(8,128)(2,1)S(1)} %collective-permute-done.3.beyond_ref) | copy-start | bytes 786436
  122.6 0.7 copy-start.10
  135.9 1.0 copy-start.3
  155.7 47.6 %all-to-all-start.3 = ((bf16[8,4,128,128]{3,2,1,0:T(8,128)(2,1)}), bf16[8,4,128,128]{3,2,1,0:T(8,128)(2,1)S(1)}, u32[]{:S(2)}, u32[]{:S(2)}) async-start(bf16[8,4,128,128]{3,2,1,0:T(8,128)(2,1)} %get-tuple-element.37), calls=%async_computation.3 | async-start | bytes 2097152 | tf_op jit(solution)/shard_map/all_to_all | solution.py:307
  167.9 17.8 %collective-permute-start.5 = (bf16[1024,128]{1,0:T(8,128)(2,1)}, bf16[1024,128]{1,0:T(8,128)(2,1)S(1)}, u32[]{:S(2)}, u32[]{:S(2)}) collective-permute-start(bf16[1024,128]{1,0:T(8,128)(2,1)} %get-tuple-element.40.near_ref), channel_id=1, source_target_pairs={{1,0},{2,1},{3,2},{4,3},{5,4},{6,5},{7,6},{9,8},{10,9},{11,10},{12... | collective-permute-start | bytes 786440 | tf_op jit(solution)/shard_map/ppermute | solution.py:306
  169.2 20.8 %collective-permute-start.4 = (bf16[1024,128]{1,0:T(8,128)(2,1)}, bf16[1024,128]{1,0:T(8,128)(2,1)S(1)}, u32[]{:S(2)}, u32[]{:S(2)}) collective-permute-start(bf16[1024,128]{1,0:T(8,128)(2,1)} %get-tuple-element.41.far_ref), channel_id=1, source_target_pairs={{0,1},{1,2},{2,3},{3,4},{4,5},{5,6},{6,7},{8,9},{9,10},{10,11},{11... | collective-permute-start | bytes 786440 | tf_op jit(solution)/shard_map/ppermute | solution.py:305
  185.7 4.3 %copy-start.7 = (bf16[1024,128]{1,0:T(8,128)(2,1)}, bf16[1024,128]{1,0:T(8,128)(2,1)S(1)}, u32[]{:S(2)}) copy-start(bf16[1024,128]{1,0:T(8,128)(2,1)S(1)} %collective-permute-done.5.beyond_ref) | copy-start | bytes 786436
  190.0 0.7 copy-start.9
  203.3 1.0 copy-start.2

commit v2 on v1

v2 whole, which is shorter than its diff:
```python
import functools
import jax
import jax.numpy as jnp
from jax import lax
from jax.experimental import pallas as pl
from jax.experimental.pallas import tpu as pltpu
from jax.sharding import PartitionSpec as P

F = 32
CASES = 2
ITERS = 3
CAP = 4
AXES = ("wide", "narrow")
STEP = 2.0**-8
LIMIT = 40 * 1024 * 1024
QUAD = 4
RUN = 17
f32 = jnp.float32
bf16 = jnp.bfloat16
i32 = jnp.int32
i16 = jnp.int16


def whole(shape, dtype):
    return jax.ShapeDtypeStruct(shape, dtype)


def kept(shape, dtype):
    return pltpu.HBM(shape, dtype)


def in_hbm(value):
    return pltpu.with_memory_space_constraint(value, pltpu.HBM)


def near_core(value):
    return pltpu.with_memory_space_constraint(value, pltpu.VMEM)


VM = pl.BlockSpec(memory_space=pltpu.VMEM)
SM = pl.BlockSpec(memory_space=pltpu.SMEM)
HB = pl.BlockSpec(memory_space=pl.ANY)


def lane_is_real(shape):
    lane = lax.broadcasted_iota(i32, shape, len(shape) - 1)
    return lax.rem(lane, 2 * F) < F


def both_parts(row):
    other = jnp.where(lane_is_real(row.shape), pltpu.roll(row, 128 - F, 1), pltpu.roll(row, F, 1))
    return row + other


def turned(values):
    return jnp.where(
        lane_is_real(values.shape),
        -pltpu.roll(values, 128 - F, 1),
        pltpu.roll(values, F, 1),
    )


def block_ranks(peers, blocks, lists_ref):
    keys = peers * blocks
    entries = lists_ref.shape[1]
    key = lists_ref[2:3, :] * blocks + lists_ref[1:2, :]
    one = (lax.broadcasted_iota(i32, (keys, entries), 0) == key).astype(f32)
    present = jnp.max(one, axis=1, keepdims=True)
    row = lax.broadcasted_iota(i32, (keys, keys), 0)
    col = lax.broadcasted_iota(i32, (keys, keys), 1)
    before = jnp.where((row // blocks == col // blocks) & (col <= row), 1.0, 0.0).astype(bf16)
    rank = jnp.dot(
        before,
        jnp.broadcast_to(present, (keys, 128)).astype(bf16),
        preferred_element_type=f32,
    )
    return one, present, rank


def setup_kernel(peers, blocks, lists_ref, right_ref, pcoef_ref, pay_ref):
    keys = peers * blocks
    _, present, rank = block_ranks(peers, blocks, lists_ref)
    lane = lax.broadcasted_iota(i32, (keys, 128), 1)
    name = lax.broadcasted_iota(i32, (keys, 128), 0)
    chosen = (
        (name // blocks == lane // CAP)
        & (rank == (lane % CAP + 1).astype(f32))
        & (present > 0.0)
    )
    needs = jnp.sum(jnp.where(chosen, (name % blocks).astype(f32), 0.0), axis=0, keepdims=True)
    held = jnp.sum(jnp.where(name // blocks == lane, present, 0.0), axis=0, keepdims=True)
    right = right_ref[...]
    squares = jnp.sum(jnp.sum(right * right, axis=0), axis=0, keepdims=True)
    rows = jnp.concatenate([squares, needs, held, jnp.zeros((5, 128), f32), pcoef_ref[...]], axis=0)
    pay_ref[...] = jnp.broadcast_to(rows[None], pay_ref.shape)


def order_kernel(peers, blocks, lists_ref, order_ref, slot_ref, row_ref):
    entries = lists_ref.shape[1]
    places = order_ref.shape[1]
    quads = row_ref.shape[1]
    one, _, rank = block_ranks(peers, blocks, lists_ref)
    place = jnp.sum(one * (rank[:, :1] - 1.0), axis=0, keepdims=True)
    slot = (lists_ref[2:3, :] * CAP).astype(f32) + place
    mine = (lax.broadcasted_iota(i32, (blocks, entries), 0) == lists_ref[0:1, :]).astype(f32)
    earlier = lax.broadcasted_iota(i32, (entries, entries), 0) < lax.broadcasted_iota(
        i32, (entries, entries), 1
    )
    seen = jnp.dot(
        mine.astype(bf16), jnp.where(earlier, 1.0, 0.0).astype(bf16), preferred_element_type=f32
    )
    turn = jnp.sum(mine * seen, axis=0, keepdims=True).astype(i32)
    count = jnp.sum(mine, axis=1, keepdims=True).astype(i32)
    groups = (count + QUAD - 1) // QUAD
    above = lax.broadcasted_iota(i32, (blocks, blocks), 1) < lax.broadcasted_iota(
        i32, (blocks, blocks), 0
    )
    base = jnp.dot(
        jnp.where(above, 1.0, 0.0).astype(bf16),
        jnp.broadcast_to(groups.astype(f32), (blocks, 128)).astype(bf16),
        preferred_element_type=f32,
    )[:, :1]
    start = jnp.sum(mine * base, axis=0, keepdims=True).astype(i32)
    goal = (start + turn // QUAD) * QUAD + turn % QUAD
    found = (lax.broadcasted_iota(i32, (places, entries), 0) == goal).astype(f32).astype(bf16)
    number = lax.broadcasted_iota(i32, (1, entries), 1).astype(f32)
    facts = jnp.concatenate(
        [number, slot, jnp.ones((1, entries), f32), jnp.zeros((5, entries), f32)], axis=0
    )
    table = lax.dot_general(
        facts.astype(bf16), found, (((1,), (1,)), ((), ())), preferred_element_type=f32
    )
    order_ref[...] = table[0:1, :].astype(i32)
    slot_ref[...] = jnp.where(table[2:3, :] > 0.5, table[1:2, :], float(peers * CAP)).astype(i32)
    quad = lax.broadcasted_iota(i32, (blocks, quads), 1).astype(f32)
    inside = (quad >= base) & (quad < base + groups.astype(f32))
    name = lax.broadcasted_iota(i32, (blocks, quads), 0)
    row_ref[...] = jnp.sum(jnp.where(inside, name.astype(f32), 0.0), axis=0, keepdims=True).astype(i32)


def prepare_kernel(order_ref, couple_ref, sorted_ref, held_ref, sems):
    places = sorted_ref.shape[0]
    piece = RUN * QUAD
    runs = places // piece

    def out(step):
        here = pl.ds(step * piece, piece)
        return pltpu.make_async_copy(held_ref.at[here], sorted_ref.at[here], sems.at[runs])

    for step in range(runs):

        def fetch(i, carry, step=step):
            p = step * piece + i
            pltpu.make_async_copy(
                couple_ref.at[order_ref[0, p]], held_ref.at[p], sems.at[step]
            ).start()
            return carry

        lax.fori_loop(0, piece, fetch, 0)
    for step in range(runs):
        here = held_ref.at[pl.ds(step * piece, piece)]
        pltpu.make_async_copy(here, here, sems.at[step]).wait()
        out(step).start()
    pltpu.make_async_copy(held_ref, sorted_ref, sems.at[runs]).wait()


def signs(node, first, second):
    one = jnp.ones(node.shape, bf16)
    return jnp.where(node == first, one, jnp.where(node == second, -one, jnp.zeros_like(one)))


def charges(ends_ref, zb_ref, start, chunk):
    blocks, size, width = zb_ref.shape
    branches = blocks * size
    node = lax.broadcasted_iota(i32, (16, branches), 0).astype(i16)
    groups = []
    for g in range(chunk // 16):
        row = node + jnp.full((16, branches), start + 16 * g, i32).astype(i16)
        groups.append(signs(row, ends_ref[:16, :], ends_ref[16:, :]))
    return jnp.dot(
        jnp.concatenate(groups, axis=0),
        zb_ref[...].reshape(branches, width),
        preferred_element_type=f32,
    ).astype(bf16)


def emit(
    plan, w_of, ends_ref, jacobi_ref, needs_ref, place_ref, table_ref,
    z_ref, send_ref, own_ref, right_ref, left_ref, extra_refs, zv_ref, zb_ref, sv_ref, sems,
):
    blocks, size, width = zb_ref.shape
    peers, base = sv_ref.shape[:2]
    extra = plan[1] - base
    nodes = right_ref.shape[0] - extra * size
    for n in range(blocks):
        z = jnp.dot(table_ref[jacobi_ref[n]], w_of(n).astype(bf16), preferred_element_type=f32)
        zv_ref[n] = z
        zb_ref[n] = z.astype(bf16)
    save = pltpu.make_async_copy(zv_ref, z_ref, sems.at[0])
    save.start()
    for j in range(peers):
        for s in range(base):
            sv_ref[j, s] = zb_ref[needs_ref[j, s]]
    pack = pltpu.make_async_copy(sv_ref, send_ref, sems.at[1])
    pack.start()
    mine = place_ref[0]
    for s in range(CAP):
        own_ref[s] = zb_ref[needs_ref[mine, s]]
    for distance in range(1, peers):
        for s in range(base, plan[distance]):
            for side in range(2):
                peer = jnp.clip(mine + (distance if side == 0 else -distance), 0, peers - 1)
                block = zb_ref[needs_ref[peer, s]]
                if distance == 1:
                    out = right_ref if side == 0 else left_ref
                    out[pl.ds(nodes + (s - base) * size, size), :] = block
                else:
                    extra_refs[2 * (distance - 2) + side][s - base] = block
    chunk = 512
    while nodes % chunk:
        chunk //= 2
    for part, out in ((0, left_ref), (1, right_ref)):

        def body(step, carry, part=part, out=out):
            start = pl.multiple_of(step * chunk, chunk)
            out[pl.ds(start, chunk), :] = charges(ends_ref, zb_ref, start + part * nodes, chunk)
            return carry

        lax.fori_loop(0, nodes // chunk, body, 0)
    save.wait()
    pack.wait()


def start_kernel(
    plan, pay_ref, side_ref, ends_ref, jacobi_ref, needs_ref, place_ref, table_ref,
    w_ref, beta_ref, z_ref, send_ref, own_ref, right_ref, left_ref, *rest,
):
    extra_refs, (zv_ref, zb_ref, sv_ref, sems) = rest[:-4], rest[-4:]
    total = jnp.sum(pay_ref[:, 0, :], axis=0, keepdims=True)
    beta = jnp.sqrt(both_parts(total))
    beta_ref[...] = jnp.broadcast_to(beta, beta_ref.shape)
    w_ref[...] = side_ref[...] / beta[None]
    emit(
        plan, lambda n: w_ref[n], ends_ref, jacobi_ref, needs_ref, place_ref, table_ref,
        z_ref, send_ref, own_ref, right_ref, left_ref, extra_refs, zv_ref, zb_ref, sv_ref, sems,
    )


def local_kernel(z_ref, self_ref, res_ref, freq_ref, part_ref):
    freq = freq_ref[...]
    for n in range(z_ref.shape[0]):
        z = z_ref[n]
        flux = jnp.dot(self_ref[n], z.astype(bf16), preferred_element_type=f32)
        part_ref[n] = res_ref[n] * z + turned(freq * flux)


def node_drop(cols_ref, scale_ref, left_ref, right_ref, arrived_ref, beyond_ref, drop_ref):
    nodes = scale_ref.shape[1] // 2
    blocks, size, width = drop_ref.shape
    charge = jnp.concatenate(
        [
            left_ref[:nodes].astype(f32) + arrived_ref[:nodes].astype(f32),
            right_ref[:nodes].astype(f32) + beyond_ref[:nodes].astype(f32),
        ],
        axis=0,
    ).astype(bf16)
    group = 4
    while blocks % group:
        group //= 2
    chunk = group * size

    def body(step, carry):
        start = pl.multiple_of(step * chunk, chunk)
        node = lax.broadcasted_iota(i32, (16, 2 * nodes), 1).astype(i16)
        plus = scale_ref[...]
        none = jnp.zeros_like(plus)
        rows = []
        for g in range(chunk // 16):
            ends = cols_ref[pl.ds(start + 16 * g, 16), :]
            rows.append(
                jnp.where(
                    node == ends[:, 0:1], plus, jnp.where(node == ends[:, 1:2], -plus, none)
                )
            )
        drop = jnp.dot(jnp.concatenate(rows, axis=0), charge, preferred_element_type=f32)
        drop_ref[pl.ds(step * group, group)] = drop.reshape(group, size, width)
        return carry

    lax.fori_loop(0, blocks // group, body, 0)


def couple(
    plan, row_ref, slot_ref, place_ref, sorted_ref, incoming_ref, own_ref, arrived_ref, beyond_ref,
    extra_refs, cols_ref, scale_ref, left_ref, right_ref, drop_ref, acc_ref, source_ref, held_ref,
    sems,
):
    places = held_ref.shape[0]
    piece = RUN * QUAD
    runs = places // piece

    def copy(step):
        here = pl.ds(step * piece, piece)
        return pltpu.make_async_copy(sorted_ref.at[here], held_ref.at[here], sems.at[step])

    for step in range(runs):
        copy(step).start()
    peers, base, size, width = incoming_ref.shape
    extra = plan[1] - base
    nodes = arrived_ref.shape[0] - extra * size
    mine = place_ref[0]
    for j in range(peers):
        for s in range(base):
            source_ref[j * CAP + s] = incoming_ref[j, s]
    source_ref[peers * CAP] = jnp.zeros((size, width), bf16)
    for s in range(base, CAP):
        source_ref[mine * CAP + s] = own_ref[s]
    for distance in range(1, peers):
        for s in range(base, plan[distance]):
            for side in range(2):
                peer = mine + (-distance if side == 0 else distance)
                there = (peer >= 0) & (peer < peers)
                slot = jnp.where(there, peer * CAP + s, peers * CAP + 1)
                if distance == 1:
                    source = arrived_ref if side == 0 else beyond_ref
                    block = source[pl.ds(nodes + (s - base) * size, size), :]
                else:
                    block = extra_refs[2 * (distance - 2) + side][s - base]
                source_ref[slot] = block
    acc_ref[...] = jnp.zeros_like(acc_ref)
    node_drop(cols_ref, scale_ref, left_ref, right_ref, arrived_ref, beyond_ref, drop_ref)

    def body(step, carry):
        copy(step).wait()
        for u in range(RUN):
            quad = step * RUN + u
            left = jnp.concatenate([held_ref[quad * QUAD + i] for i in range(QUAD)], axis=1)
            right = jnp.concatenate(
                [source_ref[slot_ref[0, quad * QUAD + i]] for i in range(QUAD)], axis=0
            )
            acc_ref[row_ref[0, quad]] += jnp.dot(left, right, preferred_element_type=f32)
        return carry

    lax.fori_loop(0, runs, body, 0)


def image_of(part_ref, freq_ref, acc_ref, drop_ref, n):
    freq = freq_ref[...]
    return STEP * (part_ref[n] + turned(freq * acc_ref[n] - drop_ref[n] / freq))


def split(plan, rest):
    count = extras(plan)
    return rest[:count], rest[count:]


def extras(plan):
    return 2 * sum(1 for slots in plan[2:] if slots > plan[0])


def middle_kernel(
    plan, row_ref, slot_ref, place_ref, sorted_ref, incoming_ref, own_in_ref, arrived_ref,
    beyond_ref, *rest,
):
    come, rest = split(plan, rest)
    part_ref, freq_ref, cols_ref, scale_ref, left_in_ref, right_in_ref = rest[:6]
    ends_ref, jacobi_ref, needs_ref, table_ref = rest[6:10]
    w_ref, z_ref, send_ref, own_ref, right_ref, left_ref = rest[10:16]
    go, rest = split(plan, rest[16:])
    drop_ref, acc_ref, source_ref, held_ref, run_sems, wv_ref, zv_ref, zb_ref, sv_ref, sems = rest
    couple(
        plan, row_ref, slot_ref, place_ref, sorted_ref, incoming_ref, own_in_ref, arrived_ref,
        beyond_ref, come, cols_ref, scale_ref, left_in_ref, right_in_ref, drop_ref, acc_ref,
        source_ref, held_ref, run_sems,
    )
    for n in range(wv_ref.shape[0]):
        wv_ref[n] = image_of(part_ref, freq_ref, acc_ref, drop_ref, n)
    save = pltpu.make_async_copy(wv_ref, w_ref, sems.at[2])
    save.start()
    emit(
        plan, lambda n: wv_ref[n], ends_ref, jacobi_ref, needs_ref, place_ref, table_ref,
        z_ref, send_ref, own_ref, right_ref, left_ref, go, zv_ref, zb_ref, sv_ref, sems,
    )
    save.wait()


PAIRS = [(i, j) for j in range(ITERS + 1) for i in range(j + 1)]


def last_kernel(
    plan, row_ref, slot_ref, place_ref, sorted_ref, incoming_ref, own_ref, arrived_ref,
    beyond_ref, *rest,
):
    come, rest = split(plan, rest)
    part_ref, freq_ref, cols_ref, scale_ref, left_ref, right_ref = rest[:6]
    w0_ref, w1_ref, w2_ref, pay_ref, drop_ref, acc_ref, source_ref, held_ref, sems = rest[6:]
    couple(
        plan, row_ref, slot_ref, place_ref, sorted_ref, incoming_ref, own_ref, arrived_ref,
        beyond_ref, come, cols_ref, scale_ref, left_ref, right_ref, drop_ref, acc_ref, source_ref,
        held_ref, sems,
    )
    blocks = acc_ref.shape[0]

    def body(n, sums):
        w = [w0_ref[n], w1_ref[n], w2_ref[n], image_of(part_ref, freq_ref, acc_ref, drop_ref, n)]
        fresh = []
        for at, (i, j) in enumerate(PAIRS):
            product = (w[i] * w[j]).reshape(-1, 8, 128)
            fresh.append(sums[at] + jnp.sum(product, axis=0))
        return tuple(fresh)

    sums = lax.fori_loop(0, blocks, body, tuple(jnp.zeros((8, 128), f32) for _ in PAIRS))
    rows = [jnp.sum(s, axis=0, keepdims=True) for s in sums]
    rows.append(jnp.zeros((16 - len(rows), 128), f32))
    pay_ref[...] = jnp.broadcast_to(jnp.concatenate(rows, axis=0)[None], pay_ref.shape)


def finish_kernel(pay_ref, beta_ref, z0_ref, z1_ref, z2_ref, out_ref, norm_ref):
    total = both_parts(jnp.sum(pay_ref[...], axis=0))
    gram = {}
    for at, (i, j) in enumerate(PAIRS):
        gram[i, j] = gram[j, i] = total[at : at + 1, :]
    order = list(range(1, ITERS + 1)) + [0]
    low = {}
    for i in range(ITERS + 1):
        for j in range(i + 1):
            value = gram[order[i], order[j]]
            for k in range(j):
                value = value - low[i, k] * low[j, k]
            low[i, j] = jnp.sqrt(jnp.maximum(value, 0.0)) if i == j else value / low[j, j]
    weights = [None] * ITERS
    for i in reversed(range(ITERS)):
        value = low[ITERS, i]
        for k in range(i + 1, ITERS):
            value = value - low[k, i] * weights[k]
        weights[i] = value / low[i, i]
    beta = beta_ref[0:1, :]
    norm_ref[...] = jnp.broadcast_to(low[ITERS, ITERS] * beta, norm_ref.shape)
    weights = [STEP * beta * weight for weight in weights]
    for n in range(out_ref.shape[0]):
        out_ref[n] = weights[0] * z0_ref[n] + weights[1] * z1_ref[n] + weights[2] * z2_ref[n]


def call(kernel, outs, ins, places=None, **more):
    return pl.pallas_call(
        kernel,
        out_shape=outs,
        in_specs=ins,
        out_specs=places or [VM] * len(outs),
        compiler_params=pltpu.CompilerParams(vmem_limit_bytes=LIMIT),
        **more,
    )


def iterate(
    plan, pay, right_side, jacobi_ids, needs, place, table, ends, ends_col, selfs, res, scale,
    freq, order, sorted_blocks,
):
    slots, rows = order
    peers = needs.shape[0]
    devices = pay.shape[0]
    blocks, size, width = right_side.shape
    nodes = scale.shape[1] // 2
    base = plan[0]
    far = [d for d in range(2, peers) if plan[d] > base]
    halo = kept((nodes + (plan[1] - base) * size, width), bf16)
    vec = kept((blocks, size, width), f32)
    emitted = [
        vec,
        kept((peers, base, size, width), bf16),
        kept((CAP, size, width), bf16),
        halo,
        halo,
    ] + [kept((plan[d] - base, size, width), bf16) for d in far for side in range(2)]
    spots = [HB, HB] + [VM] * (len(emitted) - 2)
    buffers = [
        pltpu.VMEM((blocks, size, width), f32),
        pltpu.VMEM((blocks, size, width), bf16),
        pltpu.VMEM((peers, base, size, width), bf16),
        pltpu.SemaphoreType.DMA((3,)),
    ]
    places = sorted_blocks.shape[0]
    coupling = [
        pltpu.VMEM((blocks, size, width), f32),
        pltpu.VMEM((blocks, size, width), f32),
        pltpu.VMEM((peers * CAP + 2, size, width), bf16),
        pltpu.VMEM((places, size, size), bf16),
        pltpu.SemaphoreType.DMA((places // (RUN * QUAD),)),
    ]
    w, beta, z, send, own, right, left, *go = call(
        functools.partial(start_kernel, plan),
        [vec, whole((8, width), f32)] + emitted,
        [VM, VM, VM, SM, SM, SM, VM],
        [VM, VM] + spots,
        scratch_shapes=buffers,
    )(near_core(pay), right_side, ends, jacobi_ids, needs, place, table)
    basis = [w]
    fields = [z]
    for step in range(ITERS):

        def moved(value, distance):
            route = [(i, i + distance) for i in range(peers) if 0 <= i + distance < peers]
            return near_core(lax.ppermute(value, "narrow", route))

        arrived = moved(right, 1)
        beyond = moved(left, -1)
        come = []
        for at, d in enumerate(far):
            come += [moved(go[2 * at], d), moved(go[2 * at + 1], -d)]
        incoming = near_core(lax.all_to_all(send, "narrow", 0, 0))
        (part,) = call(local_kernel, [vec], [VM] * 4)(in_hbm(z), selfs, res, freq)
        common = (
            rows, slots, place, in_hbm(sorted_blocks), incoming, in_hbm(own), arrived, beyond, *come,
            in_hbm(part), freq, ends_col, scale, in_hbm(left), in_hbm(right),
        )
        specs = [SM, SM, SM, HB] + [VM] * (10 + len(come))
        if step + 1 < ITERS:
            w, z, send, own, right, left, *go = call(
                functools.partial(middle_kernel, plan),
                [vec] + emitted,
                specs + [VM, SM, SM, VM],
                [HB] + spots,
                scratch_shapes=coupling + [pltpu.VMEM((blocks, size, width), f32)] + buffers,
            )(*common, ends, jacobi_ids, needs, table)
            basis.append(w)
            fields.append(z)
        else:
            (sums,) = call(
                functools.partial(last_kernel, plan),
                [whole((devices, 16, 128), f32)],
                specs + [VM] * 3,
                scratch_shapes=coupling,
            )(*common, *map(in_hbm, basis))
    sums = near_core(lax.all_to_all(sums, AXES, 0, 0))
    return call(finish_kernel, [vec, whole((8, width), f32)], [VM] * 5)(sums, beta, *map(in_hbm, fields))


def on_device(
    right_side, resistance, omega, pcoef, branch_nodes, self_blocks, couple_list, couple_blocks,
    jacobi_ids, preconditioners,
):
    blocks, size, width = right_side.shape
    nodes = pcoef.shape[0]
    entries = couple_list.shape[1]
    peers = lax.axis_size("narrow")
    devices = peers * lax.axis_size("wide")
    group = lax.axis_index("wide")
    mine = lax.axis_index("narrow")
    node_rows = nodes // 128
    freq = jnp.tile(omega, 2 * CASES).reshape(1, width)
    pairs = jnp.transpose(branch_nodes, (1, 0, 2)).reshape(2, blocks * size)
    pairs = jnp.where(pairs[0] == pairs[1], -1, pairs)
    ends = jnp.repeat(pairs.astype(i16), 16, axis=0)
    ends_col = jnp.transpose(pairs).astype(i16)
    quads = (entries + (QUAD - 1) * blocks) // QUAD
    quads = -(-quads // RUN) * RUN

    (pay,) = call(
        functools.partial(setup_kernel, peers, blocks),
        [whole((devices, 8 + node_rows, 128), f32)],
        [VM] * 3,
    )(couple_list, in_hbm(right_side), pcoef.reshape(node_rows, 128))
    pay = lax.all_to_all(pay, AXES, 0, 0)
    order, slots, rows = call(
        functools.partial(order_kernel, peers, blocks),
        [whole((1, quads * QUAD), i32), whole((1, quads * QUAD), i32), whole((1, quads), i32)],
        [VM],
    )(couple_list)
    (sorted_blocks,) = call(
        prepare_kernel,
        [kept((quads * QUAD, size, size), bf16)],
        [SM, HB],
        [HB],
        scratch_shapes=[
            pltpu.VMEM((quads * QUAD, size, size), bf16),
            pltpu.SemaphoreType.DMA((quads // RUN + 1,)),
        ],
    )(order, in_hbm(couple_blocks))
    needs = lax.dynamic_slice(
        pay, (group * peers, 1, mine * CAP), (peers, 1, CAP)
    ).reshape(peers, CAP).astype(i32)
    next_dev = jnp.minimum(group * peers + mine + 1, devices - 1)
    next_pcoef = lax.dynamic_slice(pay, (next_dev, 8, 0), (1, node_rows, 128)).reshape(nodes)
    scale = jnp.concatenate([pcoef, next_pcoef]).astype(bf16)
    scale = jnp.broadcast_to(scale[None], (16, 2 * nodes))
    shared = (
        pay, in_hbm(right_side), jacobi_ids, needs, mine.reshape(1), in_hbm(preconditioners),
        in_hbm(ends), in_hbm(ends_col), in_hbm(self_blocks),
        in_hbm(resistance.reshape(blocks, size, 1)), in_hbm(scale), freq, (slots, rows),
        sorted_blocks,
    )
    full = (CAP,) * peers
    near = (1,) + tuple(max(1, CAP // distance) for distance in range(1, peers))
    place = jnp.arange(devices) % peers
    reach = jnp.abs(place[:, None] - jnp.arange(peers)[None, :])
    allowed = jnp.where(reach == 0, CAP, jnp.asarray(near, f32)[reach])
    fits = jnp.all(pay[:, 2, :peers] <= allowed)
    result, norms = lax.cond(
        fits, lambda given: iterate(near, *given), lambda given: iterate(full, *given), shared
    )
    return result, norms[0].reshape(CASES, 2, F)[:, 0, :]


def solution(mesh):
    placed = (
        P(AXES, None, None),
        P(AXES, None),
        P(),
        P(AXES),
        P(AXES, None, None),
        P(AXES, None, None),
        P(None, AXES),
        P(AXES, None, None),
        P(AXES),
        P(),
    )
    return jax.shard_map(
        on_device,
        mesh=mesh,
        in_specs=placed,
        out_specs=(P(AXES, None, None), P()),
        check_vma=False,
    )
```

time: 247 us -> 173 us (0.70)
  waiting for transfers between devices: 52.2 us -> 12.1 us
  Pallas kernels: 103 us -> 68.2 us
  starting transfers between devices: 52.6 us -> 62.2 us
  blocking collectives: 22.8 us -> 16.7 us
  local copies, waits for them, and re-layouts: 13.9 us -> 9.17 us
    pallas_call x8 -> x10, Pallas kernels: 101 us -> 66 us  [the longest x2 26.1 us: iterate(): call(functools.partial(middle_kernel, plan), [vec] + emitted, specs + [VM...]
    ppermute x6 -> x12, waiting for transfers between devices: 43.6 us -> 12 us  [moved(): return near_core(lax.ppermute(value, 'narrow', route))]
    ppermute x6 -> x12, starting transfers between devices: 17.6 us -> 36.1 us  [moved(): return near_core(lax.ppermute(value, 'narrow', route))]
    all_to_all x3, starting transfers between devices: 27.8 us -> 18.8 us  [iterate(): incoming = near_core(lax.all_to_all(send, 'narrow', 0, 0))]
    all_to_all x1, waiting for transfers between devices: 8.56 us -> 0.01 us  [on_device(): pay = lax.all_to_all(pay, AXES, 0, 0)]
    all_to_all x1, blocking collectives: 22.8 us -> 16.7 us  [iterate(): sums = near_core(lax.all_to_all(sums, AXES, 0, 0))]
    reshape x4 -> x1, local copies, waits for them, and re-layouts: 4.37 us -> 1.35 us  [on_device(): resistance.reshape(blocks, size, 1)]
    unnamed x28 -> x17, local copies, waits for them, and re-layouts: 5.17 us -> 2.82 us
  transfers between devices with their start and end apart: 10 -> 16, of which waited for: 7 -> 6; matrix products, arithmetic and copies ran while one was open for 3% -> 3% of each run, Pallas kernels for 15% -> 12%
where the time goes in v2:
time: 173 us; the launch traced here: 172 us
  Pallas kernels  68.2 us (39%)
  starting transfers between devices  62.2 us (36%)
  blocking collectives  16.7 us (10%)
  waiting for transfers between devices  12.1 us (7%)
  local copies, waits for them, and re-layouts  9.17 us (5%)
    ppermute x12, starting transfers between devices, moved(): return near_core(lax.ppermute(value, 'narrow', route))  36.1 us
    pallas_call x2, Pallas kernels, iterate(): call(functools.partial(middle_kernel, plan), [vec] + emitted, specs + [VM...  26.1 us
    all_to_all x3, starting transfers between devices, iterate(): incoming = near_core(lax.all_to_all(send, 'narrow', 0, 0))  18.8 us
    all_to_all x1, blocking collectives, iterate(): sums = near_core(lax.all_to_all(sums, AXES, 0, 0))  16.7 us
    ppermute x12, waiting for transfers between devices, moved(): return near_core(lax.ppermute(value, 'narrow', route))  12 us
    pallas_call x3, Pallas kernels, iterate(): part, = call(local_kernel, [vec], [VM] * 4)(in_hbm(z), selfs, res, freq)  11 us
    pallas_call x1, Pallas kernels, iterate(): call(functools.partial(last_kernel, plan), [whole((devices, 16, 128), f32...  11 us
    pallas_call x1, Pallas kernels, on_device(): call(prepare_kernel, [kept((quads * QUAD, size, size), bf16)], [SM, HB],...  8.3 us
  transfers between devices with their start and end apart: 16, of which 6 were waited for; matrix products, arithmetic and copies ran while one was open for 3% of the time, Pallas kernels for 12%

profile of v2, /device:TPU:0, one launch (start us, length us, event | category | flops | bytes accessed | tf_op | source)
XLA Modules:
  0.0 171.9 jit_solution(17256401029021201369)
XLA Ops:
  0.6 0.0 copy-start.3
  0.6 0.0 copy-start
  0.7 0.7 copy-done
  1.3 0.7 copy-done.1
  2.0 2.2 %shard_map.124 = f32[32,16,128]{2,1,0:T(8,128)} custom-call(s32[3,224]{1,0:T(4,128)S(1)} %copy-done.1, f32[16,128,128]{2,1,0:T(8,128)} %right_ref.1, f32[8,128]{1,0:T(8,128)S(1)} %bitcast.33), custom_call_target="tpu_custom_call" | custom-call | tf_op jit(solution)/shard_map/pallas_call | solution.py:557
  4.2 7.3 %all-to-all-start.8 = ((f32[32,16,128]{2,1,0:T(8,128)}), f32[32,16,128]{2,1,0:T(8,128)S(1)}, u32[]{:S(2)}, u32[]{:S(2)}) async-start(f32[32,16,128]{2,1,0:T(8,128)} %shard_map.124), calls=%async_computation.8 | async-start | bytes 524288 | tf_op jit(solution)/shard_map/all_to_all | solution.py:562
  11.5 0.7 convert.8
  12.2 0.7 copy-done.2
  12.9 0.5 shard_map.125
  13.5 0.7 copy.62
  14.2 0.1 compare_select_fusion
  14.3 0.1 reshape.130
  14.4 1.9 %gather_fusion = f32[256]{0:T(256)S(1)} fusion(f32[8]{0:T(128)S(1)} %copy-done.3, s32[1024]{0:T(1024)S(1)} %pad_clamp_fusion), kind=kCustom, calls=%fused_computation | custom fusion | bytes 3072 | tf_op jit(solution)/shard_map/gather | solution.py:595
  16.3 0.0 copy-start.6
  16.3 0.0 copy-start.7
  16.3 0.0 copy-start.8
  16.3 0.1 reshape.129
  16.4 0.5 copy.55
  16.9 8.3 %shard_map.126 = bf16[272,128,128]{2,1,0:T(8,128)(2,1)} custom-call(s32[1,272]{1,0:T(1,128)S(1)} %get-tuple-element.210.order_ref, bf16[224,128,128]{2,1,0:T(8,128)(2,1)} %couple_ref.1), custom_call_target="tpu_custom_call" | custom-call | tf_op jit(solution)/shard_map/pallas_call | solution.py:568
  25.2 0.0 all-to-all-done.8
  25.3 0.7 fusion.1
  26.7 145.2 %conditional.1 = (f32[16,128,128]{2,1,0:T(8,128)}, f32[2,32]{1,0:T(2,128)}) conditional(s32[]{:T(128)} %convert_element_type.33, (s32[]{:T(128)}, s16[2,2048]{1,0:T(2,128)(2,1)S(1)}, s32[]{:T(128)}, f32[32,16,128]{2,1,0:T(8,128)S(1)}, f32[16,128,128]{2,1,0:T(8,128)}, /*index=5*/s32[16]{0:T(128)S(1)}, bf16[8,128,128]{2,1,0:T(8,128)(2,1)}, ...), branch_computations={%region_1.2_spmd, %region_2.3_spmd} | conditional | flops 39 | bytes 17048662 | solution.py:597
  26.9 0.3 copy.47
  27.3 0.1 convert_bitcast_fusion.1
  27.4 0.1 copy.48.needs_ref.rest_10_
  27.4 0.6 broadcast_in_dim.32
  28.1 5.9 %branch_1_fun.8 = (f32[16,128,128]{2,1,0:T(8,128)}, f32[8,128]{1,0:T(8,128)S(1)}, f32[16,128,128]{2,1,0:T(8,128)}, bf16[8,1,128,128]{3,2,1,0:T(8,128)(2,1)}, bf1...) custom-call(f32[32,16,128]{2,1,0:T(8,128)S(1)} %get-tuple-element.16, ...), custom_call_target="tpu_custom_call" | custom-call | tf_op jit(solution)/shard_map/cond/branch_1_fun/pallas_call | solution.py:489
  34.0 5.9 %all-to-all-start.4 = ((bf16[8,1,128,128]{3,2,1,0:T(8,128)(2,1)}), bf16[8,1,128,128]{3,2,1,0:T(8,128)(2,1)S(1)}, u32[]{:S(2)}, u32[]{:S(2)}) async-start(bf16[8,1,128,128]{3,2,1,0:T(8,128)(2,1)} %get-tuple-element.171), calls=%async_computation.4 | async-start | bytes 524288 | tf_op jit(solution)/shard_map/cond/branch_1_fun/all_to_all | solution.py:509
  39.9 3.9 %collective-permute-start.6 = (bf16[1408,128]{1,0:T(8,128)(2,1)}, bf16[1408,128]{1,0:T(8,128)(2,1)S(1)}, u32[]{:S(2)}, u32[]{:S(2)}) collective-permute-start(bf16[1408,128]{1,0:T(8,128)(2,1)} %get-tuple-element.173.rest_7_), channel_id=1, source_target_pairs={{0,1},{1,2},{2,3},{3,4},{4,5},{5,6},{6,7},{8,9},{9,10},{10,11},{11... | collective-permute-start | bytes 1081352 | tf_op jit(solution)/shard_map/cond/branch_1_fun/ppermute | solution.py:502
  43.9 1.3 collective-permute-start.7
  45.2 5.4 %collective-permute-start.8 = (bf16[1,128,128]{2,1,0:T(8,128)(2,1)}, bf16[1,128,128]{2,1,0:T(8,128)(2,1)S(1)}, u32[]{:S(2)}, u32[]{:S(2)}) collective-permute-start(bf16[1,128,128]{2,1,0:T(8,128)(2,1)} %get-tuple-element.175), channel_id=1, source_target_pairs={{0,2},{1,3},{2,4},{3,5},{4,6},{5,7},{8,10},{9,11},{10,12},{11,13},... | collective-permute-start | bytes 98312 | tf_op jit(solution)/shard_map/cond/branch_1_fun/ppermute | solution.py:502
  50.6 1.3 collective-permute-start.9
  51.9 0.1 reshape_tile.6.freq_ref.rest_3_
  52.0 1.4 copy.49.res_ref
  53.4 3.7 %branch_1_fun.9.rest_2_ = f32[16,128,128]{2,1,0:T(8,128)} custom-call(f32[16,128,128]{2,1,0:T(8,128)} %get-tuple-element.177.z_ref.z0_ref, bf16[16,128,128]{2,1,0:T(8,128)(2,1)} %get-tuple-element.178.self_ref, f32[16,128,1]{2,1,0:T(8,128)} %copy.49.res_ref, f32[1,128]{1,0:T(1,128)S(1)} %reshape_tile.6.freq_ref.rest_3_), custom_call_target="tpu_custom_call" | custom-call | tf_op jit(solution)/shard_map/cond/branch_1_fun/pallas_call | solution.py:510
  57.1 0.0 collective-permute-done.8.rest_0_
  57.1 0.4 collective-permute-done.9.rest_1_
  57.5 2.8 %collective-permute-done.6.arrived_ref = bf16[1408,128]{1,0:T(8,128)(2,1)S(1)} collective-permute-done((bf16[1408,128]{1,0:T(8,128)(2,1)}, bf16[1408,128]{1,0:T(8,128)(2,1)S(1)}, u32[]{:S(2)}, u32[]{:S(2)}) %collective-permute-start.6) | collective-permute-done | bytes 360480 | tf_op jit(solution)/shard_map/cond/branch_1_fun/ppermute | solution.py:502
  60.3 0.0 collective-permute-done.7.beyond_ref
  60.3 0.0 all-to-all-done.4.incoming_ref
  60.3 0.6 broadcast_in_dim.34.rest_5_
  61.0 13.0 %branch_1_fun.10 = (f32[16,128,128]{2,1,0:T(8,128)}, f32[16,128,128]{2,1,0:T(8,128)}, bf16[8,1,128,128]{3,2,1,0:T(8,128)(2,1)}, bf16[4,128,128]{2,1,0:T(8,128)(2...) custom-call(s32[1,68]{1,0:T(1,128)S(1)} %get-tuple-element.161.row_r, ...), custom_call_target="tpu_custom_call" | custom-call | tf_op jit(solution)/shard_map/cond/branch_1_fun/pallas_call | solution.py:517
  74.0 6.6 %all-to-all-start.5 = ((bf16[8,1,128,128]{3,2,1,0:T(8,128)(2,1)}), bf16[8,1,128,128]{3,2,1,0:T(8,128)(2,1)S(1)}, u32[]{:S(2)}, u32[]{:S(2)}) async-start(bf16[8,1,128,128]{3,2,1,0:T(8,128)(2,1)} %get-tuple-element.183), calls=%async_computation.5 | async-start | bytes 524288 | tf_op jit(solution)/shard_map/cond/branch_1_fun/all_to_all | solution.py:509
  80.6 3.9 %collective-permute-start.10 = (bf16[1408,128]{1,0:T(8,128)(2,1)}, bf16[1408,128]{1,0:T(8,128)(2,1)S(1)}, u32[]{:S(2)}, u32[]{:S(2)}) collective-permute-start(bf16[1408,128]{1,0:T(8,128)(2,1)} %get-tuple-element.185.rest_7_), channel_id=1, source_target_pairs={{0,1},{1,2},{2,3},{3,4},{4,5},{5,6},{6,7},{8,9},{9,10},{10,11},{11... | collective-permute-start | bytes 1081352 | tf_op jit(solution)/shard_map/cond/branch_1_fun/ppermute | solution.py:502
  84.5 1.3 collective-permute-start.11
  85.8 5.4 %collective-permute-start.12 = (bf16[1,128,128]{2,1,0:T(8,128)(2,1)}, bf16[1,128,128]{2,1,0:T(8,128)(2,1)S(1)}, u32[]{:S(2)}, u32[]{:S(2)}) collective-permute-start(bf16[1,128,128]{2,1,0:T(8,128)(2,1)} %get-tuple-element.187), channel_id=1, source_target_pairs={{0,2},{1,3},{2,4},{3,5},{4,6},{5,7},{8,10},{9,11},{10,12},{11,13},... | collective-permute-start | bytes 98312 | tf_op jit(solution)/shard_map/cond/branch_1_fun/ppermute | solution.py:502
  91.3 1.3 collective-permute-start.13
  92.6 3.7 %branch_1_fun.11.rest_2_ = f32[16,128,128]{2,1,0:T(8,128)} custom-call(f32[16,128,128]{2,1,0:T(8,128)} %get-tuple-element.189.z_ref.z1_ref, bf16[16,128,128]{2,1,0:T(8,128)(2,1)} %get-tuple-element.178.self_ref, f32[16,128,1]{2,1,0:T(8,128)} %copy.49.res_ref, f32[1,128]{1,0:T(1,128)S(1)} %reshape_tile.6.freq_ref.rest_3_), custom_call_target="tpu_custom_call" | custom-call | tf_op jit(solution)/shard_map/cond/branch_1_fun/pallas_call | solution.py:510
  96.2 1.4 collective-permute-done.13.rest_1_
  97.6 3.1 %collective-permute-done.10.arrived_ref = bf16[1408,128]{1,0:T(8,128)(2,1)S(1)} collective-permute-done((bf16[1408,128]{1,0:T(8,128)(2,1)}, bf16[1408,128]{1,0:T(8,128)(2,1)S(1)}, u32[]{:S(2)}, u32[]{:S(2)}) %collective-permute-start.10) | collective-permute-done | bytes 360480 | tf_op jit(solution)/shard_map/cond/branch_1_fun/ppermute | solution.py:502
  100.8 13.0 %branch_1_fun.12 = (f32[16,128,128]{2,1,0:T(8,128)}, f32[16,128,128]{2,1,0:T(8,128)}, bf16[8,1,128,128]{3,2,1,0:T(8,128)(2,1)}, bf16[4,128,128]{2,1,0:T(8,128)(2...) custom-call(s32[1,68]{1,0:T(1,128)S(1)} %get-tuple-element.161.row_r, ...), custom_call_target="tpu_custom_call" | custom-call | tf_op jit(solution)/shard_map/cond/branch_1_fun/pallas_call | solution.py:517
  113.8 6.3 %all-to-all-start.6 = ((bf16[8,1,128,128]{3,2,1,0:T(8,128)(2,1)}), bf16[8,1,128,128]{3,2,1,0:T(8,128)(2,1)S(1)}, u32[]{:S(2)}, u32[]{:S(2)}) async-start(bf16[8,1,128,128]{3,2,1,0:T(8,128)(2,1)} %get-tuple-element.190), calls=%async_computation.6 | async-start | bytes 524288 | tf_op jit(solution)/shard_map/cond/branch_1_fun/all_to_all | solution.py:509
  120.1 3.9 %collective-permute-start.14 = (bf16[1408,128]{1,0:T(8,128)(2,1)}, bf16[1408,128]{1,0:T(8,128)(2,1)S(1)}, u32[]{:S(2)}, u32[]{:S(2)}) collective-permute-start(bf16[1408,128]{1,0:T(8,128)(2,1)} %get-tuple-element.192.rest_7_), channel_id=1, source_target_pairs={{0,1},{1,2},{2,3},{3,4},{4,5},{5,6},{6,7},{8,9},{9,10},{10,11},{11... | collective-permute-start | bytes 1081352 | tf_op jit(solution)/shard_map/cond/branch_1_fun/ppermute | solution.py:502
  124.0 1.3 collective-permute-start.15
  125.3 5.4 %collective-permute-start.16 = (bf16[1,128,128]{2,1,0:T(8,128)(2,1)}, bf16[1,128,128]{2,1,0:T(8,128)(2,1)S(1)}, u32[]{:S(2)}, u32[]{:S(2)}) collective-permute-start(bf16[1,128,128]{2,1,0:T(8,128)(2,1)} %get-tuple-element.194), channel_id=1, source_target_pairs={{0,2},{1,3},{2,4},{3,5},{4,6},{5,7},{8,10},{9,11},{10,12},{11,13},... | collective-permute-start | bytes 98312 | tf_op jit(solution)/shard_map/cond/branch_1_fun/ppermute | solution.py:502
  130.8 1.6 collective-permute-start.17
  132.3 3.7 %branch_1_fun.13.rest_2_ = f32[16,128,128]{2,1,0:T(8,128)} custom-call(f32[16,128,128]{2,1,0:T(8,128)} %get-tuple-element.196.z_ref.z2_ref, bf16[16,128,128]{2,1,0:T(8,128)(2,1)} %get-tuple-element.178.self_ref, f32[16,128,1]{2,1,0:T(8,128)} %copy.49.res_ref, f32[1,128]{1,0:T(1,128)S(1)} %reshape_tile.6.freq_ref.rest_3_), custom_call_target="tpu_custom_call" | custom-call | tf_op jit(solution)/shard_map/cond/branch_1_fun/pallas_call | solution.py:510
  136.0 1.2 collective-permute-done.17.rest_1_
  137.2 3.1 %collective-permute-done.14.arrived_ref = bf16[1408,128]{1,0:T(8,128)(2,1)S(1)} collective-permute-done((bf16[1408,128]{1,0:T(8,128)(2,1)}, bf16[1408,128]{1,0:T(8,128)(2,1)S(1)}, u32[]{:S(2)}, u32[]{:S(2)}) %collective-permute-start.14) | collective-permute-done | bytes 360480 | tf_op jit(solution)/shard_map/cond/branch_1_fun/ppermute | solution.py:502
  140.3 11.0 %branch_1_fun.14 = f32[32,16,128]{2,1,0:T(8,128)S(1)} custom-call(s32[1,68]{1,0:T(1,128)S(1)} %get-tuple-element.161.row_ref, s32[1,272]{1,0:T(1,128)S(1)} %get-tuple-element.162.slot_ref, s32[1]{0:T(128)} %bitcast.5.place_ref, bf16[272,128,128]{2,1,0:T(8,128)(2,1)} %get-tuple-element.164.sorted_ref, ...), custom_call_target="tpu_custom_call" | custom-call | tf_op jit(solution)/shard_map/cond/branch_1_fun/pallas_call | solution.py:527
  151.3 16.7 %all_to_all.38.pay_ref = f32[32,16,128]{2,1,0:T(8,128)S(1)} all-to-all(f32[32,16,128]{2,1,0:T(8,128)S(1)} %branch_1_fun.14), channel_id=1, replica_groups=mesh['wide'=4,'narrow'=8] {'wide','narrow'}, dimensions={0} | all-to-all | bytes 524288 | tf_op jit(solution)/shard_map/cond/branch_1_fun/all_to_all | solution.py:533
  168.0 3.2 %branch_1_fun.15 = (f32[16,128,128]{2,1,0:T(8,128)}, f32[8,128]{1,0:T(8,128)S(1)}) custom-call(f32[32,16,128]{2,1,0:T(8,128)S(1)} %all_to_all.38.pay_ref, f32[8,128]{1,0:T(8,128)S(1)} %get-tuple-element.200.beta_ref, f32[16,128,128]{2,1,0:T(8,128)} %get-tuple-element.177.z_ref.z0_ref, f32[16,128,128]{2,1,0:T(8,128)} %get-tuple-element.189.z_ref.z1_ref, ...), custom_call_target="tpu_custom_call" | custom-call | tf_op jit(solution)/shard_map/cond/branch_1_fun/pallas_call | solution.py:534
  171.2 0.1 reshape_squeeze.6
  171.3 0.6 slice.31
  (26 shorter events, 0.2 us)
Async XLA Ops:
  0.6 13.7 %copy-start.3 = (f32[8]{0:T(128)S(1)}, f32[8]{0:T(128)}, u32[]{:S(2)}) copy-start(f32[8]{0:T(128)} %constant.57.clone) | copy-start | bytes 100
  0.6 0.7 copy-start
  1.3 0.7 copy-start.1
  4.2 21.0 %all-to-all-start.8 = ((f32[32,16,128]{2,1,0:T(8,128)}), f32[32,16,128]{2,1,0:T(8,128)S(1)}, u32[]{:S(2)}, u32[]{:S(2)}) async-start(f32[32,16,128]{2,1,0:T(8,128)} %shard_map.124), calls=%async_computation.8 | async-start | bytes 524288 | tf_op jit(solution)/shard_map/all_to_all | solution.py:562
  12.2 0.7 copy-start.2
  16.3 10.4 %copy-start.6 = (f32[16,128]{1,0:T(8,128)S(1)}, f32[16,128]{1,0:T(8,128)}, u32[]{:S(2)}) copy-start(f32[16,128]{1,0:T(8,128)} %param.14) | copy-start | bytes 24580
  16.3 10.4 %copy-start.7 = (s32[16]{0:T(128)S(1)}, s32[16]{0:T(128)}, u32[]{:S(2)}) copy-start(s32[16]{0:T(128)} %param.21) | copy-start | bytes 196
  16.3 10.4 %copy-start.8 = (f32[32]{0:T(128)S(1)}, f32[32]{0:T(128)}, u32[]{:S(2)}) copy-start(f32[32]{0:T(128)} %param.15) | copy-start | bytes 388
  26.9 34.0 %copy-start.5 = (s16[2048,2]{1,0:T(8,128)(2,1)}, s16[2048,2]{1,0:T(8,128)(2,1)S(1)}, u32[]{:S(2)}) copy-start(s16[2048,2]{1,0:T(8,128)(2,1)S(1)} %get-tuple-element.181.rest_4_) | copy-start | bytes 24580 | tf_op jit(solution)/shard_map/cond
  34.0 26.3 %all-to-all-start.4 = ((bf16[8,1,128,128]{3,2,1,0:T(8,128)(2,1)}), bf16[8,1,128,128]{3,2,1,0:T(8,128)(2,1)S(1)}, u32[]{:S(2)}, u32[]{:S(2)}) async-start(bf16[8,1,128,128]{3,2,1,0:T(8,128)(2,1)} %get-tuple-element.171), calls=%async_computation.4 | async-start | bytes 524288 | tf_op jit(solution)/shard_map/cond/branch_1_fun/all_to_all | solution.py:509
  39.9 20.4 %collective-permute-start.6 = (bf16[1408,128]{1,0:T(8,128)(2,1)}, bf16[1408,128]{1,0:T(8,128)(2,1)S(1)}, u32[]{:S(2)}, u32[]{:S(2)}) collective-permute-start(bf16[1408,128]{1,0:T(8,128)(2,1)} %get-tuple-element.173.rest_7_), channel_id=1, source_target_pairs={{0,1},{1,2},{2,3},{3,4},{4,5},{5,6},{6,7},{8,9},{9,10},{10,11},{11... | collective-permute-start | bytes 1081352 | tf_op jit(solution)/shard_map/cond/branch_1_fun/ppermute | solution.py:502
  43.9 16.4 %collective-permute-start.7 = (bf16[1408,128]{1,0:T(8,128)(2,1)}, bf16[1408,128]{1,0:T(8,128)(2,1)S(1)}, u32[]{:S(2)}, u32[]{:S(2)}) collective-permute-start(bf16[1408,128]{1,0:T(8,128)(2,1)} %get-tuple-element.174.rest_6_), channel_id=1, source_target_pairs={{1,0},{2,1},{3,2},{4,3},{5,4},{6,5},{7,6},{9,8},{10,9},{11,10},{12... | collective-permute-start | bytes 1081352 | tf_op jit(solution)/shard_map/cond/branch_1_fun/ppermute | solution.py:502
  45.2 11.9 %collective-permute-start.8 = (bf16[1,128,128]{2,1,0:T(8,128)(2,1)}, bf16[1,128,128]{2,1,0:T(8,128)(2,1)S(1)}, u32[]{:S(2)}, u32[]{:S(2)}) collective-permute-start(bf16[1,128,128]{2,1,0:T(8,128)(2,1)} %get-tuple-element.175), channel_id=1, source_target_pairs={{0,2},{1,3},{2,4},{3,5},{4,6},{5,7},{8,10},{9,11},{10,12},{11,13},... | collective-permute-start | bytes 98312 | tf_op jit(solution)/shard_map/cond/branch_1_fun/ppermute | solution.py:502
  50.6 6.9 %collective-permute-start.9 = (bf16[1,128,128]{2,1,0:T(8,128)(2,1)}, bf16[1,128,128]{2,1,0:T(8,128)(2,1)S(1)}, u32[]{:S(2)}, u32[]{:S(2)}) collective-permute-start(bf16[1,128,128]{2,1,0:T(8,128)(2,1)} %get-tuple-element.176), channel_id=1, source_target_pairs={{2,0},{3,1},{4,2},{5,3},{6,4},{7,5},{10,8},{11,9},{12,10},{13,11},... | collective-permute-start | bytes 98312 | tf_op jit(solution)/shard_map/cond/branch_1_fun/ppermute | solution.py:502
  74.0 26.8 %all-to-all-start.5 = ((bf16[8,1,128,128]{3,2,1,0:T(8,128)(2,1)}), bf16[8,1,128,128]{3,2,1,0:T(8,128)(2,1)S(1)}, u32[]{:S(2)}, u32[]{:S(2)}) async-start(bf16[8,1,128,128]{3,2,1,0:T(8,128)(2,1)} %get-tuple-element.183), calls=%async_computation.5 | async-start | bytes 524288 | tf_op jit(solution)/shard_map/cond/branch_1_fun/all_to_all | solution.py:509
  80.6 20.2 %collective-permute-start.10 = (bf16[1408,128]{1,0:T(8,128)(2,1)}, bf16[1408,128]{1,0:T(8,128)(2,1)S(1)}, u32[]{:S(2)}, u32[]{:S(2)}) collective-permute-start(bf16[1408,128]{1,0:T(8,128)(2,1)} %get-tuple-element.185.rest_7_), channel_id=1, source_target_pairs={{0,1},{1,2},{2,3},{3,4},{4,5},{5,6},{6,7},{8,9},{9,10},{10,11},{11... | collective-permute-start | bytes 1081352 | tf_op jit(solution)/shard_map/cond/branch_1_fun/ppermute | solution.py:502
  84.5 16.2 %collective-permute-start.11 = (bf16[1408,128]{1,0:T(8,128)(2,1)}, bf16[1408,128]{1,0:T(8,128)(2,1)S(1)}, u32[]{:S(2)}, u32[]{:S(2)}) collective-permute-start(bf16[1408,128]{1,0:T(8,128)(2,1)} %get-tuple-element.186.rest_6_), channel_id=1, source_target_pairs={{1,0},{2,1},{3,2},{4,3},{5,4},{6,5},{7,6},{9,8},{10,9},{11,10},{12... | collective-permute-start | bytes 1081352 | tf_op jit(solution)/shard_map/cond/branch_1_fun/ppermute | solution.py:502
  85.8 10.4 %collective-permute-start.12 = (bf16[1,128,128]{2,1,0:T(8,128)(2,1)}, bf16[1,128,128]{2,1,0:T(8,128)(2,1)S(1)}, u32[]{:S(2)}, u32[]{:S(2)}) collective-permute-start(bf16[1,128,128]{2,1,0:T(8,128)(2,1)} %get-tuple-element.187), channel_id=1, source_target_pairs={{0,2},{1,3},{2,4},{3,5},{4,6},{5,7},{8,10},{9,11},{10,12},{11,13},... | collective-permute-start | bytes 98312 | tf_op jit(solution)/shard_map/cond/branch_1_fun/ppermute | solution.py:502
  91.3 6.4 %collective-permute-start.13 = (bf16[1,128,128]{2,1,0:T(8,128)(2,1)}, bf16[1,128,128]{2,1,0:T(8,128)(2,1)S(1)}, u32[]{:S(2)}, u32[]{:S(2)}) collective-permute-start(bf16[1,128,128]{2,1,0:T(8,128)(2,1)} %get-tuple-element.188), channel_id=1, source_target_pairs={{2,0},{3,1},{4,2},{5,3},{6,4},{7,5},{10,8},{11,9},{12,10},{13,11},... | collective-permute-start | bytes 98312 | tf_op jit(solution)/shard_map/cond/branch_1_fun/ppermute | solution.py:502
  113.8 26.5 %all-to-all-start.6 = ((bf16[8,1,128,128]{3,2,1,0:T(8,128)(2,1)}), bf16[8,1,128,128]{3,2,1,0:T(8,128)(2,1)S(1)}, u32[]{:S(2)}, u32[]{:S(2)}) async-start(bf16[8,1,128,128]{3,2,1,0:T(8,128)(2,1)} %get-tuple-element.190), calls=%async_computation.6 | async-start | bytes 524288 | tf_op jit(solution)/shard_map/cond/branch_1_fun/all_to_all | solution.py:509
  120.1 20.2 %collective-permute-start.14 = (bf16[1408,128]{1,0:T(8,128)(2,1)}, bf16[1408,128]{1,0:T(8,128)(2,1)S(1)}, u32[]{:S(2)}, u32[]{:S(2)}) collective-permute-start(bf16[1408,128]{1,0:T(8,128)(2,1)} %get-tuple-element.192.rest_7_), channel_id=1, source_target_pairs={{0,1},{1,2},{2,3},{3,4},{4,5},{5,6},{6,7},{8,9},{9,10},{10,11},{11... | collective-permute-start | bytes 1081352 | tf_op jit(solution)/shard_map/cond/branch_1_fun/ppermute | solution.py:502
  124.0 16.3 %collective-permute-start.15 = (bf16[1408,128]{1,0:T(8,128)(2,1)}, bf16[1408,128]{1,0:T(8,128)(2,1)S(1)}, u32[]{:S(2)}, u32[]{:S(2)}) collective-permute-start(bf16[1408,128]{1,0:T(8,128)(2,1)} %get-tuple-element.193.rest_6_), channel_id=1, source_target_pairs={{1,0},{2,1},{3,2},{4,3},{5,4},{6,5},{7,6},{9,8},{10,9},{11,10},{12... | collective-permute-start | bytes 1081352 | tf_op jit(solution)/shard_map/cond/branch_1_fun/ppermute | solution.py:502
  125.3 10.7 %collective-permute-start.16 = (bf16[1,128,128]{2,1,0:T(8,128)(2,1)}, bf16[1,128,128]{2,1,0:T(8,128)(2,1)S(1)}, u32[]{:S(2)}, u32[]{:S(2)}) collective-permute-start(bf16[1,128,128]{2,1,0:T(8,128)(2,1)} %get-tuple-element.194), channel_id=1, source_target_pairs={{0,2},{1,3},{2,4},{3,5},{4,6},{5,7},{8,10},{9,11},{10,12},{11,13},... | collective-permute-start | bytes 98312 | tf_op jit(solution)/shard_map/cond/branch_1_fun/ppermute | solution.py:502
  130.8 6.4 %collective-permute-start.17 = (bf16[1,128,128]{2,1,0:T(8,128)(2,1)}, bf16[1,128,128]{2,1,0:T(8,128)(2,1)S(1)}, u32[]{:S(2)}, u32[]{:S(2)}) collective-permute-start(bf16[1,128,128]{2,1,0:T(8,128)(2,1)} %get-tuple-element.195), channel_id=1, source_target_pairs={{2,0},{3,1},{4,2},{5,3},{6,4},{7,5},{10,8},{11,9},{12,10},{13,11},... | collective-permute-start | bytes 98312 | tf_op jit(solution)/shard_map/cond/branch_1_fun/ppermute | solution.py:502

commit v3 on v2

v3 whole, which is shorter than its diff:
```python
import functools
import jax
import jax.numpy as jnp
import numpy as np
from jax import lax
from jax.experimental import pallas as pl
from jax.experimental.pallas import tpu as pltpu
from jax.sharding import PartitionSpec as P

F = 32
CASES = 2
ITERS = 3
CAP = 4
AXES = ("wide", "narrow")
STEP = 2.0**-8
LIMIT = 40 * 1024 * 1024
QUAD = 4
RUN = 17
WEIGHT = 64
NODE_ROW = 128
PAD = 2
f32 = jnp.float32
bf16 = jnp.bfloat16
i32 = jnp.int32
i16 = jnp.int16


def whole(shape, dtype):
    return jax.ShapeDtypeStruct(shape, dtype)


def kept(shape, dtype):
    return pltpu.HBM(shape, dtype)


def in_hbm(value):
    return pltpu.with_memory_space_constraint(value, pltpu.HBM)


def near_core(value):
    return pltpu.with_memory_space_constraint(value, pltpu.VMEM)


VM = pl.BlockSpec(memory_space=pltpu.VMEM)
SM = pl.BlockSpec(memory_space=pltpu.SMEM)
HB = pl.BlockSpec(memory_space=pl.ANY)


def lane_is_real(shape):
    lane = lax.broadcasted_iota(i32, shape, len(shape) - 1)
    return lax.rem(lane, 2 * F) < F


def both_parts(row):
    other = jnp.where(lane_is_real(row.shape), pltpu.roll(row, 128 - F, 1), pltpu.roll(row, F, 1))
    return row + other


def turned(values):
    return jnp.where(
        lane_is_real(values.shape),
        -pltpu.roll(values, 128 - F, 1),
        pltpu.roll(values, F, 1),
    )


def block_ranks(peers, blocks, lists_ref):
    keys = peers * blocks
    entries = lists_ref.shape[1]
    key = lists_ref[2:3, :] * blocks + lists_ref[1:2, :]
    one = (lax.broadcasted_iota(i32, (keys, entries), 0) == key).astype(f32)
    present = jnp.max(one, axis=1, keepdims=True)
    row = lax.broadcasted_iota(i32, (keys, keys), 0)
    col = lax.broadcasted_iota(i32, (keys, keys), 1)
    before = jnp.where((row // blocks == col // blocks) & (col <= row), 1.0, 0.0).astype(bf16)
    rank = jnp.dot(
        before,
        jnp.broadcast_to(present, (keys, 128)).astype(bf16),
        preferred_element_type=f32,
    )
    return one, present, rank


def setup_kernel(peers, blocks, lists_ref, right_ref, pay_ref):
    keys = peers * blocks
    _, present, rank = block_ranks(peers, blocks, lists_ref)
    lane = lax.broadcasted_iota(i32, (keys, 128), 1)
    name = lax.broadcasted_iota(i32, (keys, 128), 0)
    chosen = (
        (name // blocks == lane // CAP)
        & (rank == (lane % CAP + 1).astype(f32))
        & (present > 0.0)
    )
    needs = jnp.sum(jnp.where(chosen, (name % blocks).astype(f32), 0.0), axis=0, keepdims=True)
    held = jnp.sum(jnp.where(name // blocks == lane, present, 0.0), axis=0, keepdims=True)
    right = right_ref[...]
    squares = jnp.sum(jnp.sum(right * right, axis=0), axis=0, keepdims=True)
    rows = jnp.concatenate([squares, needs, held, jnp.zeros((5, 128), f32)], axis=0)
    pay_ref[...] = jnp.broadcast_to(rows[None], pay_ref.shape)


def order_kernel(peers, blocks, lists_ref, order_ref, slot_ref, row_ref):
    entries = lists_ref.shape[1]
    places = order_ref.shape[1]
    quads = row_ref.shape[1]
    one, _, rank = block_ranks(peers, blocks, lists_ref)
    place = jnp.sum(one * (rank[:, :1] - 1.0), axis=0, keepdims=True)
    slot = (lists_ref[2:3, :] * CAP).astype(f32) + place
    mine = (lax.broadcasted_iota(i32, (blocks, entries), 0) == lists_ref[0:1, :]).astype(f32)
    earlier = lax.broadcasted_iota(i32, (entries, entries), 0) < lax.broadcasted_iota(
        i32, (entries, entries), 1
    )
    seen = jnp.dot(
        mine.astype(bf16), jnp.where(earlier, 1.0, 0.0).astype(bf16), preferred_element_type=f32
    )
    turn = jnp.sum(mine * seen, axis=0, keepdims=True).astype(i32)
    count = jnp.sum(mine, axis=1, keepdims=True).astype(i32)
    groups = (count + QUAD - 1) // QUAD
    above = lax.broadcasted_iota(i32, (blocks, blocks), 1) < lax.broadcasted_iota(
        i32, (blocks, blocks), 0
    )
    base = jnp.dot(
        jnp.where(above, 1.0, 0.0).astype(bf16),
        jnp.broadcast_to(groups.astype(f32), (blocks, 128)).astype(bf16),
        preferred_element_type=f32,
    )[:, :1]
    start = jnp.sum(mine * base, axis=0, keepdims=True).astype(i32)
    goal = (start + turn // QUAD) * QUAD + turn % QUAD
    found = (lax.broadcasted_iota(i32, (places, entries), 0) == goal).astype(f32).astype(bf16)
    number = lax.broadcasted_iota(i32, (1, entries), 1).astype(f32)
    facts = jnp.concatenate(
        [number, slot, jnp.ones((1, entries), f32), jnp.zeros((5, entries), f32)], axis=0
    )
    table = lax.dot_general(
        facts.astype(bf16), found, (((1,), (1,)), ((), ())), preferred_element_type=f32
    )
    order_ref[...] = table[0:1, :].astype(i32)
    slot_ref[...] = jnp.where(table[2:3, :] > 0.5, table[1:2, :], float(peers * CAP)).astype(i32)
    quad = lax.broadcasted_iota(i32, (blocks, quads), 1).astype(f32)
    inside = (quad >= base) & (quad < base + groups.astype(f32))
    name = lax.broadcasted_iota(i32, (blocks, quads), 0)
    row_ref[...] = jnp.sum(jnp.where(inside, name.astype(f32), 0.0), axis=0, keepdims=True).astype(i32)


def signs(node, first, second):
    one = jnp.ones(node.shape, bf16)
    return jnp.where(node == first, one, jnp.where(node == second, -one, jnp.zeros_like(one)))


def charges(ends_ref, zb_ref, start, chunk):
    blocks, size, width = zb_ref.shape
    branches = blocks * size
    node = lax.broadcasted_iota(i32, (16, branches), 0).astype(i16)
    groups = []
    for g in range(chunk // 16):
        row = node + jnp.full((16, branches), start + 16 * g, i32).astype(i16)
        groups.append(signs(row, ends_ref[:16, :], ends_ref[16:, :]))
    return jnp.dot(
        jnp.concatenate(groups, axis=0),
        zb_ref[...].reshape(branches, width),
        preferred_element_type=f32,
    ).astype(bf16)


def emit(
    plan, w_of, ends_ref, jacobi_ref, needs_ref, place_ref, table_ref, rows_ref,
    z_ref, zb_out_ref, right_ref, left_ref, zv_ref, zb_ref, both_ref, sems,
):
    blocks, size, width = zb_ref.shape
    peers = needs_ref.shape[0]
    base = plan[0]
    node_rows = rows_ref.shape[0]
    nodes = right_ref.shape[0] - (plan[1] - base) * size - node_rows
    for n in range(blocks):
        z = jnp.dot(table_ref[jacobi_ref[n]], w_of(n).astype(bf16), preferred_element_type=f32)
        zv_ref[n] = z
        zb_ref[n] = z.astype(bf16)
    pack = pltpu.make_async_copy(zb_ref, zb_out_ref, sems.at[1])
    pack.start()
    save = pltpu.make_async_copy(zv_ref, z_ref, sems.at[0])
    save.start()
    mine = place_ref[0]
    left_ref[pl.ds(nodes, node_rows), :] = rows_ref[...]
    right_ref[pl.ds(nodes, node_rows), :] = rows_ref[...]
    for s in range(base, plan[1]):
        for out, step in ((right_ref, 1), (left_ref, -1)):
            peer = jnp.clip(mine + step, 0, peers - 1)
            there = nodes + node_rows + (s - base) * size
            out[pl.ds(there, size), :] = zb_ref[needs_ref[peer, s]]
    chunk = nodes if base < CAP else 128

    def body(step, carry):
        start = pl.multiple_of(step * chunk, chunk)
        both_ref[pl.ds(start, chunk), :] = charges(ends_ref, zb_ref, start, chunk)
        return carry

    lax.fori_loop(0, 2 * nodes // chunk, body, 0)
    left_ref[pl.ds(0, nodes), :] = both_ref[pl.ds(0, nodes), :]
    right_ref[pl.ds(0, nodes), :] = both_ref[pl.ds(nodes, nodes), :]
    save.wait()
    pack.wait()


def pack_kernel(plan, needs_ref, place_ref, zb_ref, send_ref, own_ref, *extra_refs):
    peers, base = send_ref.shape[:2]
    mine = place_ref[0]
    for j in range(peers):
        for s in range(base):
            send_ref[j, s] = zb_ref[needs_ref[j, s]]
    for s in range(CAP):
        own_ref[s] = zb_ref[needs_ref[mine, s]]
    at = 0
    for distance in range(2, peers):
        if plan[distance] > base:
            for step in (distance, -distance):
                peer = jnp.clip(mine + step, 0, peers - 1)
                for s in range(base, plan[distance]):
                    extra_refs[at][s - base] = zb_ref[needs_ref[peer, s]]
                at += 1


def start_kernel(
    plan, pay_ref, side_ref, ends_ref, jacobi_ref, needs_ref, place_ref, table_ref, rows_ref,
    w_ref, beta_ref, z_ref, zb_out_ref, right_ref, left_ref, zv_ref, zb_ref, both_ref, sems,
):
    total = jnp.sum(pay_ref[:, 0, :], axis=0, keepdims=True)
    beta = jnp.sqrt(both_parts(total))
    beta_ref[...] = jnp.broadcast_to(beta, beta_ref.shape)
    w_ref[...] = side_ref[...] / beta[None]
    emit(
        plan, lambda n: w_ref[n], ends_ref, jacobi_ref, needs_ref, place_ref, table_ref, rows_ref,
        z_ref, zb_out_ref, right_ref, left_ref, zv_ref, zb_ref, both_ref, sems,
    )


def local_kernel(z_ref, self_ref, res_ref, freq_ref, part_ref):
    freq = freq_ref[...]
    for n in range(z_ref.shape[0]):
        z = z_ref[n]
        flux = jnp.dot(self_ref[n], z.astype(bf16), preferred_element_type=f32)
        part_ref[n] = freq * flux - turned(res_ref[n] * z)


def drop_kernel(
    part_ref, freq_ref, cols_ref, rows_ref, left_ref, right_ref, arrived_ref, beyond_ref, out_ref,
    charge_ref, plus_ref,
):
    node_rows = rows_ref.shape[0]
    group, size, width = out_ref.shape
    nodes = NODE_ROW * node_rows // PAD

    @pl.when(pl.program_id(0) == 0)
    def _():
        charge_ref[:nodes] = (
            left_ref[:nodes].astype(f32) + arrived_ref[:nodes].astype(f32)
        ).astype(bf16)
        charge_ref[nodes:] = (
            right_ref[:nodes].astype(f32) + beyond_ref[:nodes].astype(f32)
        ).astype(bf16)
        own = rows_ref[...].astype(f32)
        next_rows = beyond_ref[pl.ds(nodes, node_rows), :].astype(f32)
        lanes = [own[i : i + 1, :] for i in range(nodes // NODE_ROW)]
        lanes += [next_rows[i : i + 1, :] for i in range(nodes // NODE_ROW)]
        row = jnp.concatenate(lanes, axis=1)
        plus_ref[...] = jnp.broadcast_to(row, (16, 2 * nodes)).astype(bf16)

    plus = plus_ref[...]
    node = lax.broadcasted_iota(i32, (16, 2 * nodes), 1).astype(i16)
    none = jnp.zeros_like(plus)
    rows = []
    for g in range(group * size // 16):
        ends = cols_ref[pl.ds(16 * g, 16), :]
        rows.append(
            jnp.where(node == ends[:, 0:1], plus, jnp.where(node == ends[:, 1:2], -plus, none))
        )
    drop = jnp.dot(jnp.concatenate(rows, axis=0), charge_ref[...], preferred_element_type=f32)
    out_ref[...] = part_ref[...] - (drop / freq_ref[...]).reshape(group, size, width)


def couple(
    plan, order_ref, row_ref, slot_ref, place_ref, blocks_ref, incoming_ref, own_ref, arrived_ref,
    beyond_ref, extra_refs, acc_ref, source_ref, held_ref, sems, later,
):
    places = held_ref.shape[0]
    piece = RUN * QUAD
    runs = places // piece

    def copy(step):
        here = pl.ds(step * piece, piece)
        source = held_ref if order_ref is not None else blocks_ref
        return pltpu.make_async_copy(source.at[here], held_ref.at[here], sems.at[step])

    for step in range(runs):
        if order_ref is None:
            copy(step).start()
            continue

        def fetch(i, carry, step=step):
            p = step * piece + i
            pltpu.make_async_copy(
                blocks_ref.at[order_ref[0, p]], held_ref.at[p], sems.at[step]
            ).start()
            return carry

        lax.fori_loop(0, piece, fetch, 0, unroll=4)
    for fetched in later:
        fetched.start()
    peers, base, size, width = incoming_ref.shape
    extra = plan[1] - base
    head = arrived_ref.shape[0] - extra * size
    mine = place_ref[0]
    for j in range(peers):
        for s in range(base):
            source_ref[j * CAP + s] = incoming_ref[j, s]
    source_ref[peers * CAP] = jnp.zeros((size, width), bf16)
    for s in range(base, CAP):
        source_ref[mine * CAP + s] = own_ref[s]
    for distance in range(1, peers):
        for s in range(base, plan[distance]):
            for side in range(2):
                peer = mine + (-distance if side == 0 else distance)
                there = (peer >= 0) & (peer < peers)
                slot = jnp.where(there, peer * CAP + s, peers * CAP + 1)
                if distance == 1:
                    source = arrived_ref if side == 0 else beyond_ref
                    block = source[pl.ds(head + (s - base) * size, size), :]
                else:
                    block = extra_refs[2 * (distance - 2) + side][s - base]
                source_ref[slot] = block
    acc_ref[...] = jnp.zeros_like(acc_ref)

    def body(step, carry):
        copy(step).wait()
        for u in range(RUN):
            quad = step * RUN + u
            left = jnp.concatenate([held_ref[quad * QUAD + i] for i in range(QUAD)], axis=1)
            right = jnp.concatenate(
                [source_ref[slot_ref[0, quad * QUAD + i]] for i in range(QUAD)], axis=0
            )
            acc_ref[row_ref[0, quad]] += jnp.dot(left, right, preferred_element_type=f32)
        return carry

    lax.fori_loop(0, runs, body, 0)
    for fetched in later:
        fetched.wait()


def image_of(part_ref, freq_ref, acc_ref, n):
    return STEP * turned(part_ref[n] + freq_ref[...] * acc_ref[n])


def split(plan, rest):
    count = extras(plan)
    return rest[:count], rest[count:]


def extras(plan):
    return 2 * sum(1 for slots in plan[2:] if slots > plan[0])


def middle_kernel(
    plan, first, row_ref, slot_ref, place_ref, blocks_ref, incoming_ref, own_ref, arrived_ref,
    beyond_ref, *rest,
):
    come, rest = split(plan, rest)
    part_ref, freq_ref, ends_ref, jacobi_ref, needs_ref, table_ref, rows_ref = rest[:7]
    rest = rest[7:]
    order_ref = None
    if first:
        order_ref, rest = rest[0], rest[1:]
    w_ref, z_ref, zb_out_ref, right_ref, left_ref = rest[:5]
    rest = rest[5:]
    if first:
        sorted_ref, rest = rest[0], rest[1:]
    acc_ref, source_ref, held_ref, run_sems, wv_ref, zv_ref, zb_ref, both_ref, sems = rest
    bring = pltpu.make_async_copy(part_ref, zv_ref, sems.at[0])
    couple(
        plan, order_ref, row_ref, slot_ref, place_ref, blocks_ref, incoming_ref, own_ref,
        arrived_ref, beyond_ref, come, acc_ref, source_ref, held_ref, run_sems, [bring],
    )
    if first:
        keep = pltpu.make_async_copy(held_ref, sorted_ref, sems.at[3])
        keep.start()
    for n in range(wv_ref.shape[0]):
        wv_ref[n] = image_of(zv_ref, freq_ref, acc_ref, n)
    save = pltpu.make_async_copy(wv_ref, w_ref, sems.at[2])
    save.start()
    emit(
        plan, lambda n: wv_ref[n], ends_ref, jacobi_ref, needs_ref, place_ref, table_ref, rows_ref,
        z_ref, zb_out_ref, right_ref, left_ref, zv_ref, zb_ref, both_ref, sems,
    )
    save.wait()
    if first:
        keep.wait()


PAIRS = [(i, j) for j in range(ITERS + 1) for i in range(j + 1)]


def last_kernel(
    plan, row_ref, slot_ref, place_ref, blocks_ref, incoming_ref, own_ref, arrived_ref,
    beyond_ref, *rest,
):
    come, rest = split(plan, rest)
    part_ref, freq_ref, w0_ref, w1_ref, w2_ref, pay_ref = rest[:6]
    acc_ref, source_ref, held_ref, run_sems, store_ref, sems = rest[6:]
    bring = [
        pltpu.make_async_copy(source, store_ref.at[at], sems.at[at])
        for at, source in enumerate((part_ref, w0_ref, w1_ref, w2_ref))
    ]
    couple(
        plan, None, row_ref, slot_ref, place_ref, blocks_ref, incoming_ref, own_ref,
        arrived_ref, beyond_ref, come, acc_ref, source_ref, held_ref, run_sems, bring,
    )
    blocks = acc_ref.shape[0]

    def body(n, sums):
        w = [store_ref[1 + k, n] for k in range(ITERS)]
        w.append(image_of(store_ref.at[0], freq_ref, acc_ref, n))
        fresh = []
        for at, (i, j) in enumerate(PAIRS):
            product = (w[i] * w[j]).reshape(-1, 8, 128)
            fresh.append(sums[at] + jnp.sum(product, axis=0))
        return tuple(fresh)

    sums = lax.fori_loop(0, blocks, body, tuple(jnp.zeros((8, 128), f32) for _ in PAIRS))
    rows = [jnp.sum(s, axis=0, keepdims=True) for s in sums]
    rows = [both_parts(row) for row in rows]
    real = lane_is_real((1, 128))
    rows = [jnp.where(real, rows[k], rows[k + 1]) for k in range(0, len(rows), 2)]
    rows.append(jnp.zeros((8 - len(rows), 128), f32))
    pay_ref[...] = jnp.broadcast_to(jnp.concatenate(rows, axis=0)[None], pay_ref.shape)


def finish_kernel(pay_ref, beta_ref, z0_ref, z1_ref, z2_ref, out_ref, norm_ref):
    total = jnp.sum(pay_ref[...], axis=0)
    real = lane_is_real(total.shape)
    even = jnp.where(real, total, pltpu.roll(total, F, 1))
    odd = jnp.where(real, pltpu.roll(total, 128 - F, 1), total)
    gram = {}
    for at, (i, j) in enumerate(PAIRS):
        half = at // 2
        gram[i, j] = gram[j, i] = (odd if at % 2 else even)[half : half + 1, :]
    order = list(range(1, ITERS + 1)) + [0]
    low = {}
    for i in range(ITERS + 1):
        for j in range(i + 1):
            value = gram[order[i], order[j]]
            for k in range(j):
                value = value - low[i, k] * low[j, k]
            low[i, j] = jnp.sqrt(jnp.maximum(value, 0.0)) if i == j else value / low[j, j]
    weights = [None] * ITERS
    for i in reversed(range(ITERS)):
        value = low[ITERS, i]
        for k in range(i + 1, ITERS):
            value = value - low[k, i] * weights[k]
        weights[i] = value / low[i, i]
    beta = beta_ref[0:1, :]
    norm_ref[...] = jnp.broadcast_to(low[ITERS, ITERS] * beta, norm_ref.shape)
    weights = [STEP * beta * weight for weight in weights]
    for n in range(out_ref.shape[0]):
        out_ref[n] = weights[0] * z0_ref[n] + weights[1] * z1_ref[n] + weights[2] * z2_ref[n]


def call(kernel, outs, ins, places=None, **more):
    return pl.pallas_call(
        kernel,
        out_shape=outs,
        in_specs=ins,
        out_specs=places or [VM] * len(outs),
        compiler_params=pltpu.CompilerParams(vmem_limit_bytes=LIMIT),
        **more,
    )


def iterate(
    plan, pay, right_side, jacobi_ids, needs, place, table, ends, ends_col, selfs, res, scale,
    freq, tables, couple_blocks,
):
    order, slots, rows = tables
    peers = needs.shape[0]
    devices = pay.shape[0]
    blocks, size, width = right_side.shape
    nodes = NODE_ROW * scale.shape[0] // PAD
    base = plan[0]
    far = [d for d in range(2, peers) if plan[d] > base]
    halo = kept((nodes + scale.shape[0] + (plan[1] - base) * size, width), bf16)
    vec = kept((blocks, size, width), f32)
    emitted = [vec, kept((blocks, size, width), bf16), halo, halo]
    packed = [
        kept((peers, base, size, width), bf16),
        kept((CAP, size, width), bf16),
    ] + [kept((plan[d] - base, size, width), bf16) for d in far for side in range(2)]
    spots = [HB, HB, VM, VM]
    buffers = [
        pltpu.VMEM((blocks, size, width), f32),
        pltpu.VMEM((blocks, size, width), bf16),
        pltpu.VMEM((2 * nodes, width), bf16),
        pltpu.SemaphoreType.DMA((4,)),
    ]
    places = order.shape[1]
    coupling = [
        pltpu.VMEM((blocks, size, width), f32),
        pltpu.VMEM((peers * CAP + 2, size, width), bf16),
        pltpu.VMEM((places, size, size), bf16),
        pltpu.SemaphoreType.DMA((places // (RUN * QUAD),)),
    ]
    w, beta, z, zb, right, left = call(
        functools.partial(start_kernel, plan),
        [vec, whole((8, width), f32)] + emitted,
        [VM, VM, VM, SM, SM, SM, VM, VM],
        [VM, VM] + spots,
        scratch_shapes=buffers,
    )(near_core(pay), right_side, ends, jacobi_ids, needs, place, table, scale)
    basis = [w]
    fields = [z]
    for step in range(ITERS):

        def moved(value, distance):
            route = [(i, i + distance) for i in range(peers) if 0 <= i + distance < peers]
            return near_core(lax.ppermute(value, "narrow", route))

        arrived = moved(right, 1)
        beyond = moved(left, -1)
        send, own, *go = call(functools.partial(pack_kernel, plan), packed, [SM, SM, VM])(
            needs, place, in_hbm(zb)
        )
        come = []
        for at, d in enumerate(far):
            come += [moved(go[2 * at], d), moved(go[2 * at + 1], -d)]
        incoming = near_core(lax.all_to_all(send, "narrow", 0, 0))
        later, send = lax.optimization_barrier((z, send))
        (part,) = call(local_kernel, [vec], [VM] * 4)(in_hbm(later), selfs, res, freq)
        parts = 2 if base < CAP else blocks
        half = blocks // parts
        block = pl.BlockSpec((half, size, width), lambda i: (i, 0, 0))
        (part,) = call(
            drop_kernel,
            [vec],
            [block, VM, pl.BlockSpec((half * size, 2), lambda i: (i, 0))] + [VM] * 5,
            [block],
            grid=(parts,),
            scratch_shapes=[
                pltpu.VMEM((2 * nodes, width), bf16),
                pltpu.VMEM((16, 2 * nodes), bf16),
            ],
            cost_estimate=pl.CostEstimate(
                flops=WEIGHT * blocks * size * nodes * width,
                bytes_accessed=WEIGHT * blocks * size * width,
                transcendentals=0,
            ),
        )(in_hbm(part), freq, ends_col, scale, in_hbm(left), in_hbm(right), arrived, beyond)
        first = step == 0
        held = couple_blocks if first else sorted_blocks
        common = (
            rows, slots, place, in_hbm(held), incoming, in_hbm(own), arrived, beyond, *come,
            in_hbm(part), freq,
        )
        specs = [SM, SM, SM, HB] + [VM] * (4 + len(come)) + [HB, VM]
        if step + 1 < ITERS:
            w, z, zb, right, left, *copies = call(
                functools.partial(middle_kernel, plan, first),
                [vec] + emitted + ([kept((places, size, size), bf16)] if first else []),
                specs + [VM, SM, SM, VM, VM] + ([SM] if first else []),
                [HB] + spots + ([HB] if first else []),
                scratch_shapes=coupling + [pltpu.VMEM((blocks, size, width), f32)] + buffers,
            )(*common, ends, jacobi_ids, needs, table, scale, *([order] if first else []))
            if first:
                (sorted_blocks,) = copies
            basis.append(w)
            fields.append(z)
        else:
            (sums,) = call(
                functools.partial(last_kernel, plan),
                [whole((devices, 8, 128), f32)],
                specs + [HB] * 3,
                scratch_shapes=coupling
                + [
                    pltpu.VMEM((ITERS + 1, blocks, size, width), f32),
                    pltpu.SemaphoreType.DMA((ITERS + 1,)),
                ],
            )(*common, *map(in_hbm, basis))
    sums = near_core(lax.all_to_all(sums, AXES, 0, 0))
    return call(finish_kernel, [vec, whole((8, width), f32)], [VM] * 5)(
        sums, beta, *map(in_hbm, fields)
    )


def on_device(
    right_side, resistance, omega, pcoef, branch_nodes, self_blocks, couple_list, couple_blocks,
    jacobi_ids, preconditioners,
):
    blocks, size, width = right_side.shape
    nodes = pcoef.shape[0]
    entries = couple_list.shape[1]
    peers = lax.axis_size("narrow")
    devices = peers * lax.axis_size("wide")
    group = lax.axis_index("wide")
    mine = lax.axis_index("narrow")
    node_rows = nodes // NODE_ROW
    freq = jnp.tile(omega, 2 * CASES).reshape(1, width)
    pairs = jnp.transpose(branch_nodes, (1, 0, 2)).reshape(2, blocks * size)
    pairs = jnp.where(pairs[0] == pairs[1], -1, pairs)
    ends = jnp.repeat(pairs.astype(i16), 16, axis=0)
    ends_col = jnp.transpose(pairs).astype(i16)
    quads = (entries + (QUAD - 1) * blocks) // QUAD
    quads = -(-quads // RUN) * RUN

    (pay,) = call(
        functools.partial(setup_kernel, peers, blocks),
        [whole((devices, 8, 128), f32)],
        [VM] * 2,
    )(couple_list, in_hbm(right_side))
    pay = lax.all_to_all(pay, AXES, 0, 0)
    order, slots, rows = call(
        functools.partial(order_kernel, peers, blocks),
        [whole((1, quads * QUAD), i32), whole((1, quads * QUAD), i32), whole((1, quads), i32)],
        [VM],
    )(couple_list)
    needs = lax.dynamic_slice(
        pay, (group * peers, 1, mine * CAP), (peers, 1, CAP)
    ).reshape(peers, CAP).astype(i32)
    rows16 = jnp.pad(pcoef.astype(bf16).reshape(node_rows, 128), ((0, node_rows), (0, 0)))
    shared = (
        pay, in_hbm(right_side), jacobi_ids, needs, mine.reshape(1), in_hbm(preconditioners),
        in_hbm(ends), in_hbm(ends_col), in_hbm(self_blocks),
        in_hbm(resistance.reshape(blocks, size, 1)), in_hbm(rows16), freq, (order, slots, rows),
        in_hbm(couple_blocks),
    )
    full = (CAP,) * peers
    near = (2,) + tuple(max(2, CAP // distance) for distance in range(1, peers))
    reach = np.abs(np.arange(devices)[:, None] % peers - np.arange(peers)[None, :])
    allowed = np.where(reach == 0, CAP, np.asarray(near)[reach]).astype(np.float32)
    fits = jnp.all(pay[:, 2, :peers] <= allowed)
    result, norms = lax.cond(
        fits, lambda given: iterate(near, *given), lambda given: iterate(full, *given), shared
    )
    return result, norms[0].reshape(CASES, 2, F)[:, 0, :]


def solution(mesh):
    placed = (
        P(AXES, None, None),
        P(AXES, None),
        P(),
        P(AXES),
        P(AXES, None, None),
        P(AXES, None, None),
        P(None, AXES),
        P(AXES, None, None),
        P(AXES),
        P(),
    )
    return jax.shard_map(
        on_device,
        mesh=mesh,
        in_specs=placed,
        out_specs=(P(AXES, None, None), P()),
        check_vma=False,
    )
```

time: 173 us -> 161 us (0.931)
  starting transfers between devices: 62.2 us -> 39.8 us
  Pallas kernels: 68.2 us -> 75.6 us
  waiting for transfers between devices: 12.1 us -> 19.1 us
  blocking collectives: 16.7 us -> 13.5 us
    ppermute x12 -> x6, starting transfers between devices: 36.1 us -> 13.3 us  [moved(): return near_core(lax.ppermute(value, 'narrow', route))]
    all_to_all x3, waiting for transfers between devices: 0.01 us -> 9.5 us  [iterate(): incoming = near_core(lax.all_to_all(send, 'narrow', 0, 0))]
    pallas_call x8 -> x13, Pallas kernels: 58.6 us -> 66.3 us  [the longest x2 21.8 us: iterate(): call(functools.partial(middle_kernel, plan, first), [vec] + emitted + ([k...]
    ppermute x12 -> x6, waiting for transfers between devices: 12 us -> 5.07 us  [moved(): return near_core(lax.ppermute(value, 'narrow', route))]
    all_to_all x1, waiting for transfers between devices: 0.01 us -> 4.58 us  [on_device(): pay = lax.all_to_all(pay, AXES, 0, 0)]
    all_to_all x1, blocking collectives: 16.7 us -> 13.5 us  [iterate(): sums = near_core(lax.all_to_all(sums, AXES, 0, 0))]
    gather x2 -> x0, local copies, waits for them, and re-layouts: 1.95 us -> none  [on_device(): allowed = jnp.where(reach == 0, CAP, jnp.asarray(near, f32)[reach])]
  transfers between devices with their start and end apart: 16 -> 10, of which waited for: 6 -> 6; matrix products, arithmetic and copies ran while one was open for 3% -> 3% of each run, Pallas kernels for 12% -> 22%
where the time goes in v3:
time: 161 us; the launch traced here: 159 us
  Pallas kernels  75.6 us (47%)
  starting transfers between devices  39.8 us (25%)
  waiting for transfers between devices  19.1 us (12%)
  blocking collectives  13.5 us (8%)
  local copies, waits for them, and re-layouts  7.58 us (5%)
  other arithmetic  2.2 us (1%)
    pallas_call x2, Pallas kernels, iterate(): call(functools.partial(middle_kernel, plan, first), [vec] + emitted + ([k...  21.8 us
    all_to_all x3, starting transfers between devices, iterate(): incoming = near_core(lax.all_to_all(send, 'narrow', 0, 0))  19.1 us
    pallas_call x3, Pallas kernels, iterate(): call(drop_kernel, [vec], [block, VM, pl.BlockSpec((half * size, 2), lambd...  15.4 us
    all_to_all x1, blocking collectives, iterate(): sums = near_core(lax.all_to_all(sums, AXES, 0, 0))  13.5 us
    ppermute x6, starting transfers between devices, moved(): return near_core(lax.ppermute(value, 'narrow', route))  13.3 us
    pallas_call x3, Pallas kernels, iterate(): part, = call(local_kernel, [vec], [VM] * 4)(in_hbm(later), selfs, res, freq)  13 us
    all_to_all x3, waiting for transfers between devices, iterate(): incoming = near_core(lax.all_to_all(send, 'narrow', 0, 0))  9.5 us
    pallas_call x1, Pallas kernels, iterate(): call(functools.partial(last_kernel, plan), [whole((devices, 8, 128), f32)...  8.1 us
  transfers between devices with their start and end apart: 10, of which 6 were waited for; matrix products, arithmetic and copies ran while one was open for 3% of the time, Pallas kernels for 22%

profile of v3, /device:TPU:0, one launch (start us, length us, event | category | flops | bytes accessed | tf_op | source)
XLA Modules:
  0.0 159.4 jit_solution(13769895305190325111)
XLA Ops:
  0.6 0.0 copy-start
  0.6 0.7 copy-done
  1.3 2.1 %shard_map.124 = f32[32,8,128]{2,1,0:T(8,128)} custom-call(s32[3,224]{1,0:T(4,128)S(1)} %copy-done, f32[16,128,128]{2,1,0:T(8,128)} %right_ref.1), custom_call_target="tpu_custom_call" | custom-call | tf_op jit(solution)/shard_map/pallas_call | solution.py:609
  3.5 7.3 %all-to-all-start.8 = ((f32[32,8,128]{2,1,0:T(8,128)}), f32[32,8,128]{2,1,0:T(8,128)S(1)}, u32[]{:S(2)}, u32[]{:S(2)}) async-start(f32[32,8,128]{2,1,0:T(8,128)} %shard_map.124), calls=%async_computation.8 | async-start | bytes 262144 | tf_op jit(solution)/shard_map/all_to_all | solution.py:614
  10.8 0.0 copy-start.1
  10.8 0.7 copy-done.1
  11.5 0.5 shard_map.125
  12.0 0.7 convert_element_type.30
  12.7 0.7 copy.78
  13.4 0.5 copy.73
  13.9 4.6 %all-to-all-done.8 = f32[32,8,128]{2,1,0:T(8,128)S(1)} async-done(((f32[32,8,128]{2,1,0:T(8,128)}), f32[32,8,128]{2,1,0:T(8,128)S(1)}, u32[]{:S(2)}, u32[]{:S(2)}) %all-to-all-start.8) | async-done | bytes 131104 | tf_op jit(solution)/shard_map/all_to_all | solution.py:614
  18.5 1.4 compare_reduce_fusion
  20.5 138.9 %conditional.1 = (f32[16,128,128]{2,1,0:T(8,128)}, f32[2,32]{1,0:T(2,128)}) conditional(s32[]{:T(128)} %convert_element_type.28, (s32[]{:T(128)}, s32[]{:T(128)}, f32[32,8,128]{2,1,0:T(8,128)S(1)}, s16[2,2048]{1,0:T(2,128)(2,1)S(1)}, bf16[1024]{0:T(1024)(128)(2,1)S(1)}, /*index=5*/f32[16,128,128]{2,1,0:T(8,128)}, s32[16]{0:T(128)}, ...), branch_computations={%region_1.2_spmd, %region_2.3_spmd} | conditional | flops 51539607552 | bytes 66882944 | solution.py:635
  20.8 0.0 copy-start.3
  20.8 0.2 copy.62
  21.0 0.1 convert_bitcast_fusion.1
  21.1 0.1 copy.64.needs_ref.rest_4_
  21.2 0.6 pad.7.rows_ref.rest_6_
  21.8 0.7 broadcast_in_dim.12
  22.4 5.5 %branch_1_fun.14 = (f32[16,128,128]{2,1,0:T(8,128)}, f32[8,128]{1,0:T(8,128)S(1)}, f32[16,128,128]{2,1,0:T(8,128)}, bf16[16,128,128]{2,1,0:T(8,128)(2,1)}, bf16[...) custom-call(f32[32,8,128]{2,1,0:T(8,128)S(1)} %get-tuple-element.183.pay_ref, ...), custom_call_target="tpu_custom_call" | custom-call | tf_op jit(solution)/shard_map/cond/branch_1_fun/pallas_call | solution.py:508
  28.0 3.2 %collective-permute-start.6 = (bf16[1296,128]{1,0:T(8,128)(2,1)}, bf16[1296,128]{1,0:T(8,128)(2,1)S(1)}, u32[]{:S(2)}, u32[]{:S(2)}) collective-permute-start(bf16[1296,128]{1,0:T(8,128)(2,1)} %get-tuple-element.193.right_ref), channel_id=1, source_target_pairs={{0,1},{1,2},{2,3},{3,4},{4,5},{5,6},{6,7},{8,9},{9,10},{10,11},{11... | collective-permute-start | bytes 995336 | tf_op jit(solution)/shard_map/cond/branch_1_fun/ppermute | solution.py:521
  31.1 1.3 collective-permute-start.7
  32.4 2.0 %branch_1_fun.15 = (bf16[8,2,128,128]{3,2,1,0:T(8,128)(2,1)}, bf16[4,128,128]{2,1,0:T(8,128)(2,1)}) custom-call(s32[8,4]{1,0:T(8,128)S(1)} %copy.64.needs_ref.rest_4_, s32[1]{0:T(128)} %bitcast.6.place_ref, bf16[16,128,128]{2,1,0:T(8,128)(2,1)} %get-tuple-element.190.zb_ref), custom_call_target="tpu_custom_call" | custom-call | tf_op jit(solution)/shard_map/cond/branch_1_fun/pallas_call | solution.py:525
  34.4 4.9 %all-to-all-start.4 = ((bf16[8,2,128,128]{3,2,1,0:T(8,128)(2,1)}), bf16[8,2,128,128]{3,2,1,0:T(8,128)(2,1)S(1)}, u32[]{:S(2)}, u32[]{:S(2)}) async-start(bf16[8,2,128,128]{3,2,1,0:T(8,128)(2,1)} %get-tuple-element.191), calls=%async_computation.4 | async-start | bytes 1048576 | tf_op jit(solution)/shard_map/cond/branch_1_fun/all_to_all | solution.py:531
  39.3 0.7 tile.9
  40.0 0.1 reshape_tile.6.freq_ref.rest_1_
  40.1 2.1 %copy.65.res_ref = f32[16,128,1]{2,1,0:T(8,128)} copy(f32[16,128,1]{1,0,2:T(8,128)} %bitcast.37) | data formatting | bytes 16384 | tf_op jit(solution)/shard_map/reshape | solution.py:627
  42.1 4.3 %branch_1_fun.16.part_ref = f32[16,128,128]{2,1,0:T(8,128)} custom-call(f32[16,128,128]{2,1,0:T(8,128)} %get-tuple-element.196.z_ref.z0_ref, bf16[16,128,128]{2,1,0:T(8,128)(2,1)} %get-tuple-element.197.self_ref, f32[16,128,1]{2,1,0:T(8,128)} %copy.65.res_ref, f32[1,128]{1,0:T(1,128)S(1)} %reshape_tile.6.freq_ref.rest_1_), custom_call_target="tpu_custom_call" | custom-call | tf_op jit(solution)/shard_map/cond/branch_1_fun/pallas_call | solution.py:533
  46.5 3.2 %collective-permute-done.6.arrived_ref = bf16[1296,128]{1,0:T(8,128)(2,1)S(1)} collective-permute-done((bf16[1296,128]{1,0:T(8,128)(2,1)}, bf16[1296,128]{1,0:T(8,128)(2,1)S(1)}, u32[]{:S(2)}, u32[]{:S(2)}) %collective-permute-start.6) | collective-permute-done | bytes 331808 | tf_op jit(solution)/shard_map/cond/branch_1_fun/ppermute | solution.py:521
  49.7 0.0 collective-permute-done.7.beyond_ref
  49.7 0.0 copy-done.3
  49.7 0.0 copy-start.5
  49.7 5.1 %branch_1_fun.17.rest_0_ = f32[16,128,128]{2,1,0:T(8,128)} custom-call(f32[16,128,128]{2,1,0:T(8,128)} %branch_1_fun.16.part_ref, f32[1,128]{1,0:T(1,128)S(1)} %reshape_tile.6.freq_ref.rest_1_, s16[2048,2]{1,0:T(8,128)(2,1)} %copy-done.3, bf16[16,128]{1,0:T(8,128)(2,1)} %pad.7.rows_ref.rest_6_, bf16[1296,128]{1,0:T(8,128)(2,1)} %get-tuple-element.194.left_ref, ...), custom_call_target="tpu_custom_call" | custom-call | flops 17179869184 | bytes 16777216 | tf_op jit(solution)/shard_map/cond/branch_1_fun/pallas_call | solution.py:537
  54.8 1.0 all-to-all-done.4.incoming_ref
  55.8 0.0 copy-done.5
  55.8 11.9 %branch_1_fun.18 = (f32[16,128,128]{2,1,0:T(8,128)}, f32[16,128,128]{2,1,0:T(8,128)}, bf16[16,128,128]{2,1,0:T(8,128)(2,1)}, bf16[1296,128]{1,0:T(8,128)(2,1)}, ...) custom-call(s32[1,68]{1,0:T(1,128)S(1)} %get-tuple-element.179.row_ref, ...), custom_call_target="tpu_custom_call" | custom-call | tf_op jit(solution)/shard_map/cond/branch_1_fun/pallas_call | solution.py:561
  67.7 3.4 %collective-permute-start.8 = (bf16[1296,128]{1,0:T(8,128)(2,1)}, bf16[1296,128]{1,0:T(8,128)(2,1)S(1)}, u32[]{:S(2)}, u32[]{:S(2)}) collective-permute-start(bf16[1296,128]{1,0:T(8,128)(2,1)} %get-tuple-element.206.right_ref), channel_id=1, source_target_pairs={{0,1},{1,2},{2,3},{3,4},{4,5},{5,6},{6,7},{8,9},{9,10},{10,11},{11... | collective-permute-start | bytes 995336 | tf_op jit(solution)/shard_map/cond/branch_1_fun/ppermute | solution.py:521
  71.0 1.3 collective-permute-start.9
  72.3 1.9 %branch_1_fun.19 = (bf16[8,2,128,128]{3,2,1,0:T(8,128)(2,1)}, bf16[4,128,128]{2,1,0:T(8,128)(2,1)}) custom-call(s32[8,4]{1,0:T(8,128)S(1)} %copy.64.needs_ref.rest_4_, s32[1]{0:T(128)} %bitcast.6.place_ref, bf16[16,128,128]{2,1,0:T(8,128)(2,1)} %get-tuple-element.203.zb_ref), custom_call_target="tpu_custom_call" | custom-call | tf_op jit(solution)/shard_map/cond/branch_1_fun/pallas_call | solution.py:525
  74.3 6.4 %all-to-all-start.5 = ((bf16[8,2,128,128]{3,2,1,0:T(8,128)(2,1)}), bf16[8,2,128,128]{3,2,1,0:T(8,128)(2,1)S(1)}, u32[]{:S(2)}, u32[]{:S(2)}) async-start(bf16[8,2,128,128]{3,2,1,0:T(8,128)(2,1)} %get-tuple-element.204), calls=%async_computation.5 | async-start | bytes 1048576 | tf_op jit(solution)/shard_map/cond/branch_1_fun/all_to_all | solution.py:531
  80.7 4.4 %branch_1_fun.20.part_ref = f32[16,128,128]{2,1,0:T(8,128)} custom-call(f32[16,128,128]{2,1,0:T(8,128)} %get-tuple-element.209.z_ref.z1_ref, bf16[16,128,128]{2,1,0:T(8,128)(2,1)} %get-tuple-element.197.self_ref, f32[16,128,1]{2,1,0:T(8,128)} %copy.65.res_ref, f32[1,128]{1,0:T(1,128)S(1)} %reshape_tile.6.freq_ref.rest_1_), custom_call_target="tpu_custom_call" | custom-call | tf_op jit(solution)/shard_map/cond/branch_1_fun/pallas_call | solution.py:533
  85.0 1.9 %collective-permute-done.8.arrived_ref = bf16[1296,128]{1,0:T(8,128)(2,1)S(1)} collective-permute-done((bf16[1296,128]{1,0:T(8,128)(2,1)}, bf16[1296,128]{1,0:T(8,128)(2,1)S(1)}, u32[]{:S(2)}, u32[]{:S(2)}) %collective-permute-start.8) | collective-permute-done | bytes 331808 | tf_op jit(solution)/shard_map/cond/branch_1_fun/ppermute | solution.py:521
  86.9 0.0 collective-permute-done.9.beyond_ref
  86.9 5.1 %branch_1_fun.21.rest_0_ = f32[16,128,128]{2,1,0:T(8,128)} custom-call(f32[16,128,128]{2,1,0:T(8,128)} %branch_1_fun.20.part_ref, f32[1,128]{1,0:T(1,128)S(1)} %reshape_tile.6.freq_ref.rest_1_, s16[2048,2]{1,0:T(8,128)(2,1)} %copy-done.3, bf16[16,128]{1,0:T(8,128)(2,1)} %pad.7.rows_ref.rest_6_, bf16[1296,128]{1,0:T(8,128)(2,1)} %get-tuple-element.207.left_ref, ...), custom_call_target="tpu_custom_call" | custom-call | flops 17179869184 | bytes 16777216 | tf_op jit(solution)/shard_map/cond/branch_1_fun/pallas_call | solution.py:537
  92.0 4.0 %all-to-all-done.5.incoming_ref = bf16[8,2,128,128]{3,2,1,0:T(8,128)(2,1)S(1)} async-done(((bf16[8,2,128,128]{3,2,1,0:T(8,128)(2,1)}), bf16[8,2,128,128]{3,2,1,0:T(8,128)(2,1)S(1)}, u32[]{:S(2)}, u32[]{:S(2)}) %all-to-all-start.5) | async-done | bytes 524320 | tf_op jit(solution)/shard_map/cond/branch_1_fun/all_to_all | solution.py:531
  96.0 9.9 %branch_1_fun.22 = (f32[16,128,128]{2,1,0:T(8,128)}, f32[16,128,128]{2,1,0:T(8,128)}, bf16[16,128,128]{2,1,0:T(8,128)(2,1)}, bf16[1296,128]{1,0:T(8,128)(2,1)}, bf16[1296,128]{1,0:T(8,128)(2,1)}) custom-call(s32[1,68]{1,0:T(1,128)S(1)} %get-tuple-element.179.row_ref, s32[1,272]{1,0:T(1,128)S(1)} %get-tuple-element.180.slot_ref, s32[1]{0:T(128)} %bitcast.6.place_ref, ...), custom_call_target="tpu_custom_call" | custom-call | tf_op jit(solution)/shard_map/cond/branch_1_fun/pallas_call | solution.py:561
  106.0 2.7 %collective-permute-start.10 = (bf16[1296,128]{1,0:T(8,128)(2,1)}, bf16[1296,128]{1,0:T(8,128)(2,1)S(1)}, u32[]{:S(2)}, u32[]{:S(2)}) collective-permute-start(bf16[1296,128]{1,0:T(8,128)(2,1)} %get-tuple-element.213.right_ref), channel_id=1, source_target_pairs={{0,1},{1,2},{2,3},{3,4},{4,5},{5,6},{6,7},{8,9},{9,10},{10,11},{11... | collective-permute-start | bytes 995336 | tf_op jit(solution)/shard_map/cond/branch_1_fun/ppermute | solution.py:521
  108.7 1.6 collective-permute-start.11
  110.2 2.0 %branch_1_fun.23 = (bf16[8,2,128,128]{3,2,1,0:T(8,128)(2,1)}, bf16[4,128,128]{2,1,0:T(8,128)(2,1)}) custom-call(s32[8,4]{1,0:T(8,128)S(1)} %copy.64.needs_ref.rest_4_, s32[1]{0:T(128)} %bitcast.6.place_ref, bf16[16,128,128]{2,1,0:T(8,128)(2,1)} %get-tuple-element.210.zb_ref), custom_call_target="tpu_custom_call" | custom-call | tf_op jit(solution)/shard_map/cond/branch_1_fun/pallas_call | solution.py:525
  112.2 7.8 %all-to-all-start.6 = ((bf16[8,2,128,128]{3,2,1,0:T(8,128)(2,1)}), bf16[8,2,128,128]{3,2,1,0:T(8,128)(2,1)S(1)}, u32[]{:S(2)}, u32[]{:S(2)}) async-start(bf16[8,2,128,128]{3,2,1,0:T(8,128)(2,1)} %get-tuple-element.211), calls=%async_computation.6 | async-start | bytes 1048576 | tf_op jit(solution)/shard_map/cond/branch_1_fun/all_to_all | solution.py:531
  120.0 4.3 %branch_1_fun.24.part_ref = f32[16,128,128]{2,1,0:T(8,128)} custom-call(f32[16,128,128]{2,1,0:T(8,128)} %get-tuple-element.216.z_ref.z2_ref, bf16[16,128,128]{2,1,0:T(8,128)(2,1)} %get-tuple-element.197.self_ref, f32[16,128,1]{2,1,0:T(8,128)} %copy.65.res_ref, f32[1,128]{1,0:T(1,128)S(1)} %reshape_tile.6.freq_ref.rest_1_), custom_call_target="tpu_custom_call" | custom-call | tf_op jit(solution)/shard_map/cond/branch_1_fun/pallas_call | solution.py:533
  124.3 0.0 collective-permute-done.10.arrived_ref
  124.3 0.0 collective-permute-done.11.beyond_ref
  124.3 5.1 %branch_1_fun.25.rest_0_ = f32[16,128,128]{2,1,0:T(8,128)} custom-call(f32[16,128,128]{2,1,0:T(8,128)} %branch_1_fun.24.part_ref, f32[1,128]{1,0:T(1,128)S(1)} %reshape_tile.6.freq_ref.rest_1_, s16[2048,2]{1,0:T(8,128)(2,1)} %copy-done.3, bf16[16,128]{1,0:T(8,128)(2,1)} %pad.7.rows_ref.rest_6_, bf16[1296,128]{1,0:T(8,128)(2,1)} %get-tuple-element.214.left_ref, ...), custom_call_target="tpu_custom_call" | custom-call | flops 17179869184 | bytes 16777216 | tf_op jit(solution)/shard_map/cond/branch_1_fun/pallas_call | solution.py:537
  129.5 4.5 %all-to-all-done.6.incoming_ref = bf16[8,2,128,128]{3,2,1,0:T(8,128)(2,1)S(1)} async-done(((bf16[8,2,128,128]{3,2,1,0:T(8,128)(2,1)}), bf16[8,2,128,128]{3,2,1,0:T(8,128)(2,1)S(1)}, u32[]{:S(2)}, u32[]{:S(2)}) %all-to-all-start.6) | async-done | bytes 524320 | tf_op jit(solution)/shard_map/cond/branch_1_fun/all_to_all | solution.py:531
  134.0 8.1 %branch_1_fun.26 = f32[32,8,128]{2,1,0:T(8,128)S(1)} custom-call(s32[1,68]{1,0:T(1,128)S(1)} %get-tuple-element.179.row_ref, s32[1,272]{1,0:T(1,128)S(1)} %get-tuple-element.180.slot_ref, s32[1]{0:T(128)} %bitcast.6.place_ref, bf16[272,128,128]{2,1,0:T(8,128)(2,1)} %get-tuple-element.202.blocks_ref, ...), custom_call_target="tpu_custom_call" | custom-call | tf_op jit(solution)/shard_map/cond/branch_1_fun/pallas_call | solution.py:573
  142.1 13.5 %all_to_all.38.pay_ref = f32[32,8,128]{2,1,0:T(8,128)S(1)} all-to-all(f32[32,8,128]{2,1,0:T(8,128)S(1)} %branch_1_fun.26), channel_id=1, replica_groups=mesh['wide'=4,'narrow'=8] {'wide','narrow'}, dimensions={0} | all-to-all | bytes 262144 | tf_op jit(solution)/shard_map/cond/branch_1_fun/all_to_all | solution.py:583
  155.6 3.2 %branch_1_fun.27 = (f32[16,128,128]{2,1,0:T(8,128)}, f32[8,128]{1,0:T(8,128)S(1)}) custom-call(f32[32,8,128]{2,1,0:T(8,128)S(1)} %all_to_all.38.pay_ref, f32[8,128]{1,0:T(8,128)S(1)} %get-tuple-element.220.beta_ref, f32[16,128,128]{2,1,0:T(8,128)} %get-tuple-element.196.z_ref.z0_ref, f32[16,128,128]{2,1,0:T(8,128)} %get-tuple-element.209.z_ref.z1_ref, ...), custom_call_target="tpu_custom_call" | custom-call | tf_op jit(solution)/shard_map/cond/branch_1_fun/pallas_call | solution.py:584
  158.8 0.1 reshape_squeeze.6
  158.9 0.6 slice.29
  (3 shorter events, 0.0 us)
Async XLA Ops:
  0.6 0.7 copy-start
  3.5 15.0 %all-to-all-start.8 = ((f32[32,8,128]{2,1,0:T(8,128)}), f32[32,8,128]{2,1,0:T(8,128)S(1)}, u32[]{:S(2)}, u32[]{:S(2)}) async-start(f32[32,8,128]{2,1,0:T(8,128)} %shard_map.124), calls=%async_computation.8 | async-start | bytes 262144 | tf_op jit(solution)/shard_map/all_to_all | solution.py:614
  10.8 0.7 copy-start.1
  20.8 28.9 %copy-start.3 = (s16[2048,2]{1,0:T(8,128)(2,1)}, s16[2048,2]{1,0:T(8,128)(2,1)S(1)}, u32[]{:S(2)}) copy-start(s16[2048,2]{1,0:T(8,128)(2,1)S(1)} %get-tuple-element.200.cols_ref) | copy-start | bytes 24580 | tf_op jit(solution)/shard_map/cond
  28.0 21.7 %collective-permute-start.6 = (bf16[1296,128]{1,0:T(8,128)(2,1)}, bf16[1296,128]{1,0:T(8,128)(2,1)S(1)}, u32[]{:S(2)}, u32[]{:S(2)}) collective-permute-start(bf16[1296,128]{1,0:T(8,128)(2,1)} %get-tuple-element.193.right_ref), channel_id=1, source_target_pairs={{0,1},{1,2},{2,3},{3,4},{4,5},{5,6},{6,7},{8,9},{9,10},{10,11},{11... | collective-permute-start | bytes 995336 | tf_op jit(solution)/shard_map/cond/branch_1_fun/ppermute | solution.py:521
  31.1 18.6 %collective-permute-start.7 = (bf16[1296,128]{1,0:T(8,128)(2,1)}, bf16[1296,128]{1,0:T(8,128)(2,1)S(1)}, u32[]{:S(2)}, u32[]{:S(2)}) collective-permute-start(bf16[1296,128]{1,0:T(8,128)(2,1)} %get-tuple-element.194.left_ref), channel_id=1, source_target_pairs={{1,0},{2,1},{3,2},{4,3},{5,4},{6,5},{7,6},{9,8},{10,9},{11,10},{12... | collective-permute-start | bytes 995336 | tf_op jit(solution)/shard_map/cond/branch_1_fun/ppermute | solution.py:521
  34.4 21.4 %all-to-all-start.4 = ((bf16[8,2,128,128]{3,2,1,0:T(8,128)(2,1)}), bf16[8,2,128,128]{3,2,1,0:T(8,128)(2,1)S(1)}, u32[]{:S(2)}, u32[]{:S(2)}) async-start(bf16[8,2,128,128]{3,2,1,0:T(8,128)(2,1)} %get-tuple-element.191), calls=%async_computation.4 | async-start | bytes 1048576 | tf_op jit(solution)/shard_map/cond/branch_1_fun/all_to_all | solution.py:531
  49.7 6.1 %copy-start.5 = (s32[16]{0:T(128)S(1)}, s32[16]{0:T(128)}, u32[]{:S(2)}) copy-start(s32[16]{0:T(128)} %get-tuple-element.187.jacobi_ref.rest_3_) | copy-start | bytes 196 | tf_op jit(solution)/shard_map/cond
  67.7 19.3 %collective-permute-start.8 = (bf16[1296,128]{1,0:T(8,128)(2,1)}, bf16[1296,128]{1,0:T(8,128)(2,1)S(1)}, u32[]{:S(2)}, u32[]{:S(2)}) collective-permute-start(bf16[1296,128]{1,0:T(8,128)(2,1)} %get-tuple-element.206.right_ref), channel_id=1, source_target_pairs={{0,1},{1,2},{2,3},{3,4},{4,5},{5,6},{6,7},{8,9},{9,10},{10,11},{11... | collective-permute-start | bytes 995336 | tf_op jit(solution)/shard_map/cond/branch_1_fun/ppermute | solution.py:521
  71.0 15.9 %collective-permute-start.9 = (bf16[1296,128]{1,0:T(8,128)(2,1)}, bf16[1296,128]{1,0:T(8,128)(2,1)S(1)}, u32[]{:S(2)}, u32[]{:S(2)}) collective-permute-start(bf16[1296,128]{1,0:T(8,128)(2,1)} %get-tuple-element.207.left_ref), channel_id=1, source_target_pairs={{1,0},{2,1},{3,2},{4,3},{5,4},{6,5},{7,6},{9,8},{10,9},{11,10},{12... | collective-permute-start | bytes 995336 | tf_op jit(solution)/shard_map/cond/branch_1_fun/ppermute | solution.py:521
  74.3 21.8 %all-to-all-start.5 = ((bf16[8,2,128,128]{3,2,1,0:T(8,128)(2,1)}), bf16[8,2,128,128]{3,2,1,0:T(8,128)(2,1)S(1)}, u32[]{:S(2)}, u32[]{:S(2)}) async-start(bf16[8,2,128,128]{3,2,1,0:T(8,128)(2,1)} %get-tuple-element.204), calls=%async_computation.5 | async-start | bytes 1048576 | tf_op jit(solution)/shard_map/cond/branch_1_fun/all_to_all | solution.py:531
  106.0 18.3 %collective-permute-start.10 = (bf16[1296,128]{1,0:T(8,128)(2,1)}, bf16[1296,128]{1,0:T(8,128)(2,1)S(1)}, u32[]{:S(2)}, u32[]{:S(2)}) collective-permute-start(bf16[1296,128]{1,0:T(8,128)(2,1)} %get-tuple-element.213.right_ref), channel_id=1, source_target_pairs={{0,1},{1,2},{2,3},{3,4},{4,5},{5,6},{6,7},{8,9},{9,10},{10,11},{11... | collective-permute-start | bytes 995336 | tf_op jit(solution)/shard_map/cond/branch_1_fun/ppermute | solution.py:521
  108.7 15.7 %collective-permute-start.11 = (bf16[1296,128]{1,0:T(8,128)(2,1)}, bf16[1296,128]{1,0:T(8,128)(2,1)S(1)}, u32[]{:S(2)}, u32[]{:S(2)}) collective-permute-start(bf16[1296,128]{1,0:T(8,128)(2,1)} %get-tuple-element.214.left_ref), channel_id=1, source_target_pairs={{1,0},{2,1},{3,2},{4,3},{5,4},{6,5},{7,6},{9,8},{10,9},{11,10},{12... | collective-permute-start | bytes 995336 | tf_op jit(solution)/shard_map/cond/branch_1_fun/ppermute | solution.py:521
  112.2 21.8 %all-to-all-start.6 = ((bf16[8,2,128,128]{3,2,1,0:T(8,128)(2,1)}), bf16[8,2,128,128]{3,2,1,0:T(8,128)(2,1)S(1)}, u32[]{:S(2)}, u32[]{:S(2)}) async-start(bf16[8,2,128,128]{3,2,1,0:T(8,128)(2,1)} %get-tuple-element.211), calls=%async_computation.6 | async-start | bytes 1048576 | tf_op jit(solution)/shard_map/cond/branch_1_fun/all_to_all | solution.py:531

commit v4 on v3

--- a/solution.py
+++ b/solution.py
@@ -241,45 +241,44 @@
         part_ref[n] = freq * flux - turned(res_ref[n] * z)
 
 
-def drop_kernel(
-    part_ref, freq_ref, cols_ref, rows_ref, left_ref, right_ref, arrived_ref, beyond_ref, out_ref,
-    charge_ref, plus_ref,
-):
+def charge_kernel(rows_ref, left_ref, right_ref, arrived_ref, beyond_ref, charge_ref, plus_ref):
     node_rows = rows_ref.shape[0]
-    group, size, width = out_ref.shape
     nodes = NODE_ROW * node_rows // PAD
-
-    @pl.when(pl.program_id(0) == 0)
-    def _():
-        charge_ref[:nodes] = (
-            left_ref[:nodes].astype(f32) + arrived_ref[:nodes].astype(f32)
-        ).astype(bf16)
-        charge_ref[nodes:] = (
-            right_ref[:nodes].astype(f32) + beyond_ref[:nodes].astype(f32)
-        ).astype(bf16)
-        own = rows_ref[...].astype(f32)
-        next_rows = beyond_ref[pl.ds(nodes, node_rows), :].astype(f32)
-        lanes = [own[i : i + 1, :] for i in range(nodes // NODE_ROW)]
-        lanes += [next_rows[i : i + 1, :] for i in range(nodes // NODE_ROW)]
-        row = jnp.concatenate(lanes, axis=1)
-        plus_ref[...] = jnp.broadcast_to(row, (16, 2 * nodes)).astype(bf16)
-
-    plus = plus_ref[...]
-    node = lax.broadcasted_iota(i32, (16, 2 * nodes), 1).astype(i16)
-    none = jnp.zeros_like(plus)
-    rows = []
-    for g in range(group * size // 16):
-        ends = cols_ref[pl.ds(16 * g, 16), :]
-        rows.append(
-            jnp.where(node == ends[:, 0:1], plus, jnp.where(node == ends[:, 1:2], -plus, none))
-        )
-    drop = jnp.dot(jnp.concatenate(rows, axis=0), charge_ref[...], preferred_element_type=f32)
-    out_ref[...] = part_ref[...] - (drop / freq_ref[...]).reshape(group, size, width)
+    charge_ref[:nodes] = (left_ref[...].astype(f32) + arrived_ref[:nodes].astype(f32)).astype(bf16)
+    charge_ref[nodes:] = (right_ref[...].astype(f32) + beyond_ref[:nodes].astype(f32)).astype(bf16)
+    own = rows_ref[...].astype(f32)
+    next_rows = beyond_ref[pl.ds(nodes, node_rows), :].astype(f32)
+    lanes = [own[i : i + 1, :] for i in range(nodes // NODE_ROW)]
+    lanes += [next_rows[i : i + 1, :] for i in range(nodes // NODE_ROW)]
+    row = jnp.concatenate(lanes, axis=1)
+    plus_ref[...] = jnp.broadcast_to(row, (16, 2 * nodes)).astype(bf16)
+
+
+def drop_into(acc_ref, group, freq_ref, cols_ref, charge_ref, plus_ref):
+    blocks, size, width = acc_ref.shape
+    scale = 1.0 / (freq_ref[...] * freq_ref[...])
+
+    def body(step, carry):
+        start = pl.multiple_of(step * group * size, group * size)
+        plus = plus_ref[...]
+        node = lax.broadcasted_iota(i32, plus.shape, 1).astype(i16)
+        none = jnp.zeros_like(plus)
+        rows = []
+        for g in range(group * size // 16):
+            ends = cols_ref[pl.ds(start + 16 * g, 16), :]
+            rows.append(
+                jnp.where(node == ends[:, 0:1], plus, jnp.where(node == ends[:, 1:2], -plus, none))
+            )
+        drop = jnp.dot(jnp.concatenate(rows, axis=0), charge_ref[...], preferred_element_type=f32)
+        acc_ref[pl.ds(step * group, group)] = -(drop * scale).reshape(group, size, width)
+        return carry
+
+    lax.fori_loop(0, blocks // group, body, 0)
 
 
 def couple(
     plan, order_ref, row_ref, slot_ref, place_ref, blocks_ref, incoming_ref, own_ref, arrived_ref,
-    beyond_ref, extra_refs, acc_ref, source_ref, held_ref, sems, later,
+    beyond_ref, extra_refs, drop_refs, acc_ref, source_ref, held_ref, sems, later,
 ):
     places = held_ref.shape[0]
     piece = RUN * QUAD
@@ -327,7 +326,7 @@
                 else:
                     block = extra_refs[2 * (distance - 2) + side][s - base]
                 source_ref[slot] = block
-    acc_ref[...] = jnp.zeros_like(acc_ref)
+    drop_into(acc_ref, acc_ref.shape[0] // 2 if base < CAP else 1, *drop_refs)
 
     def body(step, carry):
         copy(step).wait()
@@ -363,8 +362,9 @@
     beyond_ref, *rest,
 ):
     come, rest = split(plan, rest)
-    part_ref, freq_ref, ends_ref, jacobi_ref, needs_ref, table_ref, rows_ref = rest[:7]
-    rest = rest[7:]
+    part_ref, freq_ref, cols_ref, charge_ref, plus_ref = rest[:5]
+    ends_ref, jacobi_ref, needs_ref, table_ref, rows_ref = rest[5:10]
+    rest = rest[10:]
     order_ref = None
     if first:
         order_ref, rest = rest[0], rest[1:]
@@ -376,7 +376,8 @@
     bring = pltpu.make_async_copy(part_ref, zv_ref, sems.at[0])
     couple(
         plan, order_ref, row_ref, slot_ref, place_ref, blocks_ref, incoming_ref, own_ref,
-        arrived_ref, beyond_ref, come, acc_ref, source_ref, held_ref, run_sems, [bring],
+        arrived_ref, beyond_ref, come, (freq_ref, cols_ref, charge_ref, plus_ref), acc_ref,
+        source_ref, held_ref, run_sems, [bring],
     )
     if first:
         keep = pltpu.make_async_copy(held_ref, sorted_ref, sems.at[3])
@@ -402,15 +403,17 @@
     beyond_ref, *rest,
 ):
     come, rest = split(plan, rest)
-    part_ref, freq_ref, w0_ref, w1_ref, w2_ref, pay_ref = rest[:6]
-    acc_ref, source_ref, held_ref, run_sems, store_ref, sems = rest[6:]
+    part_ref, freq_ref, cols_ref, charge_ref, plus_ref = rest[:5]
+    w0_ref, w1_ref, w2_ref, pay_ref = rest[5:9]
+    acc_ref, source_ref, held_ref, run_sems, store_ref, sems = rest[9:]
     bring = [
         pltpu.make_async_copy(source, store_ref.at[at], sems.at[at])
         for at, source in enumerate((part_ref, w0_ref, w1_ref, w2_ref))
     ]
     couple(
         plan, None, row_ref, slot_ref, place_ref, blocks_ref, incoming_ref, own_ref,
-        arrived_ref, beyond_ref, come, acc_ref, source_ref, held_ref, run_sems, bring,
+        arrived_ref, beyond_ref, come, (freq_ref, cols_ref, charge_ref, plus_ref), acc_ref,
+        source_ref, held_ref, run_sems, bring,
     )
     blocks = acc_ref.shape[0]
 
@@ -456,7 +459,8 @@
             value = value - low[k, i] * weights[k]
         weights[i] = value / low[i, i]
     beta = beta_ref[0:1, :]
-    norm_ref[...] = jnp.broadcast_to(low[ITERS, ITERS] * beta, norm_ref.shape)
+    norm = low[ITERS, ITERS] * beta
+    norm_ref[...] = jnp.concatenate([norm, pltpu.roll(norm, 2 * F, 1)], axis=0)[:, :F]
     weights = [STEP * beta * weight for weight in weights]
     for n in range(out_ref.shape[0]):
         out_ref[n] = weights[0] * z0_ref[n] + weights[1] * z1_ref[n] + weights[2] * z2_ref[n]
@@ -531,32 +535,25 @@
         incoming = near_core(lax.all_to_all(send, "narrow", 0, 0))
         later, send = lax.optimization_barrier((z, send))
         (part,) = call(local_kernel, [vec], [VM] * 4)(in_hbm(later), selfs, res, freq)
-        parts = 2 if base < CAP else blocks
-        half = blocks // parts
-        block = pl.BlockSpec((half, size, width), lambda i: (i, 0, 0))
-        (part,) = call(
-            drop_kernel,
-            [vec],
-            [block, VM, pl.BlockSpec((half * size, 2), lambda i: (i, 0))] + [VM] * 5,
-            [block],
-            grid=(parts,),
-            scratch_shapes=[
-                pltpu.VMEM((2 * nodes, width), bf16),
-                pltpu.VMEM((16, 2 * nodes), bf16),
-            ],
+        head = pl.BlockSpec((nodes, width), lambda i: (0, 0))
+        charge, plus = call(
+            charge_kernel,
+            [kept((2 * nodes, width), bf16), kept((16, 2 * nodes), bf16)],
+            [VM, head, head, VM, VM],
+            grid=(1,),
             cost_estimate=pl.CostEstimate(
                 flops=WEIGHT * blocks * size * nodes * width,
                 bytes_accessed=WEIGHT * blocks * size * width,
                 transcendentals=0,
             ),
-        )(in_hbm(part), freq, ends_col, scale, in_hbm(left), in_hbm(right), arrived, beyond)
+        )(scale, in_hbm(left), in_hbm(right), arrived, beyond)
         first = step == 0
         held = couple_blocks if first else sorted_blocks
         common = (
             rows, slots, place, in_hbm(held), incoming, in_hbm(own), arrived, beyond, *come,
-            in_hbm(part), freq,
+            in_hbm(part), freq, ends_col, in_hbm(charge), in_hbm(plus),
         )
-        specs = [SM, SM, SM, HB] + [VM] * (4 + len(come)) + [HB, VM]
+        specs = [SM, SM, SM, HB] + [VM] * (4 + len(come)) + [HB] + [VM] * 4
         if step + 1 < ITERS:
             w, z, zb, right, left, *copies = call(
                 functools.partial(middle_kernel, plan, first),
@@ -581,7 +578,7 @@
                 ],
             )(*common, *map(in_hbm, basis))
     sums = near_core(lax.all_to_all(sums, AXES, 0, 0))
-    return call(finish_kernel, [vec, whole((8, width), f32)], [VM] * 5)(
+    return call(finish_kernel, [vec, whole((CASES, F), f32)], [VM] * 5)(
         sums, beta, *map(in_hbm, fields)
     )
 
@@ -610,7 +607,7 @@
         functools.partial(setup_kernel, peers, blocks),
         [whole((devices, 8, 128), f32)],
         [VM] * 2,
-    )(couple_list, in_hbm(right_side))
+    )(in_hbm(couple_list), in_hbm(right_side))
     pay = lax.all_to_all(pay, AXES, 0, 0)
     order, slots, rows = call(
         functools.partial(order_kernel, peers, blocks),
@@ -632,10 +629,9 @@
     reach = np.abs(np.arange(devices)[:, None] % peers - np.arange(peers)[None, :])
     allowed = np.where(reach == 0, CAP, np.asarray(near)[reach]).astype(np.float32)
     fits = jnp.all(pay[:, 2, :peers] <= allowed)
-    result, norms = lax.cond(
+    return lax.cond(
         fits, lambda given: iterate(near, *given), lambda given: iterate(full, *given), shared
     )
-    return result, norms[0].reshape(CASES, 2, F)[:, 0, :]
 
 
 def solution(mesh):

time: 161 us -> 154 us (0.957)
  waiting for transfers between devices: 19.1 us -> 30.1 us
  starting transfers between devices: 39.8 us -> 32.7 us
  Pallas kernels: 75.6 us -> 70.5 us
  blocking collectives: 13.5 us -> 9.59 us
  local copies, waits for them, and re-layouts: 7.58 us -> 5.96 us
    pallas_call x4, Pallas kernels: 18.6 us -> 9.2 us  [the longest x3 6.02 us: iterate(): call(charge_kernel, [kept((2 * nodes, width), bf16), kept((16, 2 * nodes)...]
    ppermute x6, waiting for transfers between devices: 5.07 us -> 13.4 us  [moved(): return near_core(lax.ppermute(value, 'narrow', route))]
    all_to_all x3, starting transfers between devices: 19.1 us -> 13 us  [iterate(): incoming = near_core(lax.all_to_all(send, 'narrow', 0, 0))]
    all_to_all x1, blocking collectives: 13.5 us -> 9.59 us  [iterate(): sums = near_core(lax.all_to_all(sums, AXES, 0, 0))]
    pallas_call x2, Pallas kernels: 21.8 us -> 25.2 us  [iterate(): call(functools.partial(middle_kernel, plan, first), [vec] + emitted + ([k...]
    all_to_all x3, waiting for transfers between devices: 9.5 us -> 12.1 us  [iterate(): incoming = near_core(lax.all_to_all(send, 'narrow', 0, 0))]
  transfers between devices with their start and end apart: 10 -> 10, of which waited for: 6 -> 7; matrix products, arithmetic and copies ran while one was open for 3% -> 3% of each run, Pallas kernels for 22% -> 17%
where the time goes in v4:
time: 154 us; the launch traced here: 153 us
  Pallas kernels  70.5 us (46%)
  starting transfers between devices  32.7 us (21%)
  waiting for transfers between devices  30.1 us (20%)
  blocking collectives  9.59 us (6%)
  local copies, waits for them, and re-layouts  5.96 us (4%)
  other arithmetic  2.2 us (1%)
    pallas_call x2, Pallas kernels, iterate(): call(functools.partial(middle_kernel, plan, first), [vec] + emitted + ([k...  25.2 us
    ppermute x6, waiting for transfers between devices, moved(): return near_core(lax.ppermute(value, 'narrow', route))  13.4 us
    pallas_call x3, Pallas kernels, iterate(): part, = call(local_kernel, [vec], [VM] * 4)(in_hbm(later), selfs, res, freq)  13 us
    all_to_all x3, starting transfers between devices, iterate(): incoming = near_core(lax.all_to_all(send, 'narrow', 0, 0))  13 us
    ppermute x6, starting transfers between devices, moved(): return near_core(lax.ppermute(value, 'narrow', route))  12.4 us
    all_to_all x3, waiting for transfers between devices, iterate(): incoming = near_core(lax.all_to_all(send, 'narrow', 0, 0))  12.1 us
    all_to_all x1, blocking collectives, iterate(): sums = near_core(lax.all_to_all(sums, AXES, 0, 0))  9.59 us
    pallas_call x1, Pallas kernels, iterate(): call(functools.partial(last_kernel, plan), [whole((devices, 8, 128), f32)...  9.03 us
  transfers between devices with their start and end apart: 10, of which 7 were waited for; matrix products, arithmetic and copies ran while one was open for 3% of the time, Pallas kernels for 17%

profile of v4, /device:TPU:0, one launch (start us, length us, event | category | flops | bytes accessed | tf_op | source)
XLA Modules:
  0.0 152.7 jit_solution(7301317309223511623)
XLA Ops:
  0.6 2.2 %shard_map.138 = f32[32,8,128]{2,1,0:T(8,128)} custom-call(s32[3,224]{1,0:T(4,128)} %lists_ref.3, f32[16,128,128]{2,1,0:T(8,128)} %right_ref.1), custom_call_target="tpu_custom_call" | custom-call | tf_op jit(solution)/shard_map/pallas_call | solution.py:606
  2.8 7.3 %all-to-all-start.8 = ((f32[32,8,128]{2,1,0:T(8,128)}), f32[32,8,128]{2,1,0:T(8,128)S(1)}, u32[]{:S(2)}, u32[]{:S(2)}) async-start(f32[32,8,128]{2,1,0:T(8,128)} %shard_map.138), calls=%async_computation.8 | async-start | bytes 262144 | tf_op jit(solution)/shard_map/all_to_all | solution.py:611
  10.1 0.0 copy-start
  10.1 0.7 copy-done
  10.8 0.5 shard_map.139
  11.3 0.7 convert_element_type.25
  12.0 0.7 copy.72
  12.8 0.5 copy.63
  13.2 4.6 %all-to-all-done.8 = f32[32,8,128]{2,1,0:T(8,128)S(1)} async-done(((f32[32,8,128]{2,1,0:T(8,128)}), f32[32,8,128]{2,1,0:T(8,128)S(1)}, u32[]{:S(2)}, u32[]{:S(2)}) %all-to-all-start.8) | async-done | bytes 131104 | tf_op jit(solution)/shard_map/all_to_all | solution.py:611
  17.8 1.4 compare_reduce_fusion
  19.9 0.1 dynamic-slice_convert_fusion
  20.0 132.7 %conditional.1 = ((f32[16,128,128]{2,1,0:T(8,128)}, f32[2,32]{1,0:T(2,128)})) conditional(s32[]{:T(128)} %convert_element_type.21, (f32[32,8,128]{2,1,0:T(8,128)S(1)}, f32[16,128,128]{2,1,0:T(8,128)}, s16[2,2048]{1,0:T(2,128)(2,1)S(1)}, s32[16]{0:T(128)}, s32[8,1,4]{2,1,0:T(1,128)S(1)}, /*index=5*/s32[]{:T(128)}, bf16[8,128,128]{2,1,0:T(8,128)(2,1)}, ...), branch_computations={%region_1.2_spmd, %region_2.3_spmd} | conditional | flops 51539607552 | bytes 66617616 | solution.py:632
  20.1 0.0 copy-start.2
  20.1 0.6 pad.6.rows_ref.rest_9_
  20.7 0.7 broadcast_in_dim.15
  21.4 5.5 %branch_1_fun.14 = (f32[16,128,128]{2,1,0:T(8,128)}, f32[8,128]{1,0:T(8,128)S(1)}, f32[16,128,128]{2,1,0:T(8,128)}, bf16[16,128,128]{2,1,0:T(8,128)(2,1)}, bf16[...) custom-call(f32[32,8,128]{2,1,0:T(8,128)S(1)} %get-tuple-element.117.pay_ref, ...), custom_call_target="tpu_custom_call" | custom-call | tf_op jit(solution)/shard_map/cond/branch_1_fun/pallas_call | solution.py:512
  26.9 3.2 %collective-permute-start.6 = (bf16[1296,128]{1,0:T(8,128)(2,1)}, bf16[1296,128]{1,0:T(8,128)(2,1)S(1)}, u32[]{:S(2)}, u32[]{:S(2)}) collective-permute-start(bf16[1296,128]{1,0:T(8,128)(2,1)} %get-tuple-element.126.right_ref), channel_id=1, source_target_pairs={{0,1},{1,2},{2,3},{3,4},{4,5},{5,6},{6,7},{8,9},{9,10},{10,11},{11... | collective-permute-start | bytes 995336 | tf_op jit(solution)/shard_map/cond/branch_1_fun/ppermute | solution.py:525
  30.1 1.3 collective-permute-start.7
  31.4 1.9 %branch_1_fun.15 = (bf16[8,2,128,128]{3,2,1,0:T(8,128)(2,1)}, bf16[4,128,128]{2,1,0:T(8,128)(2,1)}) custom-call(s32[8,4]{1,0:T(8,128)S(1)} %bitcast.37, s32[1]{0:T(128)} %bitcast.5.place_ref, bf16[16,128,128]{2,1,0:T(8,128)(2,1)} %get-tuple-element.123.zb_ref), custom_call_target="tpu_custom_call" | custom-call | tf_op jit(solution)/shard_map/cond/branch_1_fun/pallas_call | solution.py:529
  33.3 4.9 %all-to-all-start.4 = ((bf16[8,2,128,128]{3,2,1,0:T(8,128)(2,1)}), bf16[8,2,128,128]{3,2,1,0:T(8,128)(2,1)S(1)}, u32[]{:S(2)}, u32[]{:S(2)}) async-start(bf16[8,2,128,128]{3,2,1,0:T(8,128)(2,1)} %get-tuple-element.124), calls=%async_computation.4 | async-start | bytes 1048576 | tf_op jit(solution)/shard_map/cond/branch_1_fun/all_to_all | solution.py:535
  38.3 0.7 tile.8
  38.9 0.1 reshape_tile.5.freq_ref.rest_1_
  39.0 2.1 %copy.55.res_ref = f32[16,128,1]{2,1,0:T(8,128)} copy(f32[16,128,1]{1,0,2:T(8,128)} %bitcast.45) | data formatting | bytes 16384 | tf_op jit(solution)/shard_map/reshape | solution.py:624
  41.1 4.3 %branch_1_fun.16.rest_0_ = f32[16,128,128]{2,1,0:T(8,128)} custom-call(f32[16,128,128]{2,1,0:T(8,128)} %get-tuple-element.129.z_ref.z0_ref, bf16[16,128,128]{2,1,0:T(8,128)(2,1)} %get-tuple-element.205.self_ref, f32[16,128,1]{2,1,0:T(8,128)} %copy.55.res_ref, f32[1,128]{1,0:T(1,128)S(1)} %reshape_tile.5.freq_ref.rest_1_), custom_call_target="tpu_custom_call" | custom-call | tf_op jit(solution)/shard_map/cond/branch_1_fun/pallas_call | solution.py:537
  45.4 0.0 copy-start.4
  45.4 3.3 %collective-permute-done.6.arrived_ref = bf16[1296,128]{1,0:T(8,128)(2,1)S(1)} collective-permute-done((bf16[1296,128]{1,0:T(8,128)(2,1)}, bf16[1296,128]{1,0:T(8,128)(2,1)S(1)}, u32[]{:S(2)}, u32[]{:S(2)}) %collective-permute-start.6) | collective-permute-done | bytes 331808 | tf_op jit(solution)/shard_map/cond/branch_1_fun/ppermute | solution.py:525
  48.7 0.0 collective-permute-done.7.beyond_ref
  48.7 2.0 %branch_1_fun.17 = (bf16[2048,128]{1,0:T(8,128)(2,1)}, bf16[16,2048]{1,0:T(8,128)(2,1)}) custom-call(bf16[16,128]{1,0:T(8,128)(2,1)} %pad.6.rows_ref.rest_9_, bf16[1296,128]{1,0:T(8,128)(2,1)} %get-tuple-element.127.left_ref, bf16[1296,128]{1,0:T(8,128)(2,1)} %get-tuple-element.126.right_ref, bf16[1296,128]{1,0:T(8,128)(2,1)S(1)} %collective-permute-done.6.arrived_ref, ...), custom_call_target="tpu_custom_call" | custom-call | flops 17179869184 | bytes 16777216 | tf_op jit(solution)/shard_map/cond/branch_1_fun/pallas_call | solution.py:539
  50.7 0.0 copy-done.2
  50.7 4.1 %all-to-all-done.4.incoming_ref = bf16[8,2,128,128]{3,2,1,0:T(8,128)(2,1)S(1)} async-done(((bf16[8,2,128,128]{3,2,1,0:T(8,128)(2,1)}), bf16[8,2,128,128]{3,2,1,0:T(8,128)(2,1)S(1)}, u32[]{:S(2)}, u32[]{:S(2)}) %all-to-all-start.4) | async-done | bytes 524320 | tf_op jit(solution)/shard_map/cond/branch_1_fun/all_to_all | solution.py:535
  54.7 0.0 copy-done.4
  54.7 13.7 %branch_1_fun.18 = (f32[16,128,128]{2,1,0:T(8,128)}, f32[16,128,128]{2,1,0:T(8,128)}, bf16[16,128,128]{2,1,0:T(8,128)(2,1)}, bf16[1296,128]{1,0:T(8,128)(2,1)}, ...) custom-call(s32[1,68]{1,0:T(1,128)S(1)} %get-tuple-element.112.row_ref, ...), custom_call_target="tpu_custom_call" | custom-call | tf_op jit(solution)/shard_map/cond/branch_1_fun/pallas_call | solution.py:558
  68.4 2.7 %collective-permute-start.8 = (bf16[1296,128]{1,0:T(8,128)(2,1)}, bf16[1296,128]{1,0:T(8,128)(2,1)S(1)}, u32[]{:S(2)}, u32[]{:S(2)}) collective-permute-start(bf16[1296,128]{1,0:T(8,128)(2,1)} %get-tuple-element.141.right_ref), channel_id=1, source_target_pairs={{0,1},{1,2},{2,3},{3,4},{4,5},{5,6},{6,7},{8,9},{9,10},{10,11},{11... | collective-permute-start | bytes 995336 | tf_op jit(solution)/shard_map/cond/branch_1_fun/ppermute | solution.py:525
  71.1 1.3 collective-permute-start.9
  72.4 2.0 %branch_1_fun.19 = (bf16[8,2,128,128]{3,2,1,0:T(8,128)(2,1)}, bf16[4,128,128]{2,1,0:T(8,128)(2,1)}) custom-call(s32[8,4]{1,0:T(8,128)S(1)} %bitcast.39, s32[1]{0:T(128)} %bitcast.5.place_ref, bf16[16,128,128]{2,1,0:T(8,128)(2,1)} %get-tuple-element.138.zb_ref), custom_call_target="tpu_custom_call" | custom-call | tf_op jit(solution)/shard_map/cond/branch_1_fun/pallas_call | solution.py:529
  74.4 3.9 %all-to-all-start.5 = ((bf16[8,2,128,128]{3,2,1,0:T(8,128)(2,1)}), bf16[8,2,128,128]{3,2,1,0:T(8,128)(2,1)S(1)}, u32[]{:S(2)}, u32[]{:S(2)}) async-start(bf16[8,2,128,128]{3,2,1,0:T(8,128)(2,1)} %get-tuple-element.139), calls=%async_computation.5 | async-start | bytes 1048576 | tf_op jit(solution)/shard_map/cond/branch_1_fun/all_to_all | solution.py:535
  78.3 4.4 %branch_1_fun.20.rest_0_ = f32[16,128,128]{2,1,0:T(8,128)} custom-call(f32[16,128,128]{2,1,0:T(8,128)} %get-tuple-element.144.z_ref.z1_ref, bf16[16,128,128]{2,1,0:T(8,128)(2,1)} %get-tuple-element.205.self_ref, f32[16,128,1]{2,1,0:T(8,128)} %copy.55.res_ref, f32[1,128]{1,0:T(1,128)S(1)} %reshape_tile.5.freq_ref.rest_1_), custom_call_target="tpu_custom_call" | custom-call | tf_op jit(solution)/shard_map/cond/branch_1_fun/pallas_call | solution.py:537
  82.7 5.3 %collective-permute-done.8.arrived_ref = bf16[1296,128]{1,0:T(8,128)(2,1)S(1)} collective-permute-done((bf16[1296,128]{1,0:T(8,128)(2,1)}, bf16[1296,128]{1,0:T(8,128)(2,1)S(1)}, u32[]{:S(2)}, u32[]{:S(2)}) %collective-permute-start.8) | collective-permute-done | bytes 331808 | tf_op jit(solution)/shard_map/cond/branch_1_fun/ppermute | solution.py:525
  88.0 0.0 collective-permute-done.9.beyond_ref
  88.0 2.0 %branch_1_fun.21 = (bf16[2048,128]{1,0:T(8,128)(2,1)}, bf16[16,2048]{1,0:T(8,128)(2,1)}) custom-call(bf16[16,128]{1,0:T(8,128)(2,1)} %pad.6.rows_ref.rest_9_, bf16[1296,128]{1,0:T(8,128)(2,1)} %get-tuple-element.142.left_ref, bf16[1296,128]{1,0:T(8,128)(2,1)} %get-tuple-element.141.right_ref, bf16[1296,128]{1,0:T(8,128)(2,1)S(1)} %collective-permute-done.8.arrived_ref, ...), custom_call_target="tpu_custom_call" | custom-call | flops 17179869184 | bytes 16777216 | tf_op jit(solution)/shard_map/cond/branch_1_fun/pallas_call | solution.py:539
  90.0 3.9 %all-to-all-done.5.incoming_ref = bf16[8,2,128,128]{3,2,1,0:T(8,128)(2,1)S(1)} async-done(((bf16[8,2,128,128]{3,2,1,0:T(8,128)(2,1)}), bf16[8,2,128,128]{3,2,1,0:T(8,128)(2,1)S(1)}, u32[]{:S(2)}, u32[]{:S(2)}) %all-to-all-start.5) | async-done | bytes 524320 | tf_op jit(solution)/shard_map/cond/branch_1_fun/all_to_all | solution.py:535
  93.9 11.5 %branch_1_fun.22 = (f32[16,128,128]{2,1,0:T(8,128)}, f32[16,128,128]{2,1,0:T(8,128)}, bf16[16,128,128]{2,1,0:T(8,128)(2,1)}, bf16[1296,128]{1,0:T(8,128)(2,1)}, bf16[1296,128]{1,0:T(8,128)(2,1)}) custom-call(s32[1,68]{1,0:T(1,128)S(1)} %get-tuple-element.112.row_ref, s32[1,272]{1,0:T(1,128)S(1)} %get-tuple-element.113.slot_ref, s32[1]{0:T(128)} %bitcast.5.place_ref, ...), custom_call_target="tpu_custom_call" | custom-call | tf_op jit(solution)/shard_map/cond/branch_1_fun/pallas_call | solution.py:558
  105.4 2.7 %collective-permute-start.10 = (bf16[1296,128]{1,0:T(8,128)(2,1)}, bf16[1296,128]{1,0:T(8,128)(2,1)S(1)}, u32[]{:S(2)}, u32[]{:S(2)}) collective-permute-start(bf16[1296,128]{1,0:T(8,128)(2,1)} %get-tuple-element.150.right_ref), channel_id=1, source_target_pairs={{0,1},{1,2},{2,3},{3,4},{4,5},{5,6},{6,7},{8,9},{9,10},{10,11},{11... | collective-permute-start | bytes 995336 | tf_op jit(solution)/shard_map/cond/branch_1_fun/ppermute | solution.py:525
  108.1 1.3 collective-permute-start.11
  109.4 1.9 %branch_1_fun.23 = (bf16[8,2,128,128]{3,2,1,0:T(8,128)(2,1)}, bf16[4,128,128]{2,1,0:T(8,128)(2,1)}) custom-call(s32[8,4]{1,0:T(8,128)S(1)} %bitcast.41, s32[1]{0:T(128)} %bitcast.5.place_ref, bf16[16,128,128]{2,1,0:T(8,128)(2,1)} %get-tuple-element.147.zb_ref), custom_call_target="tpu_custom_call" | custom-call | tf_op jit(solution)/shard_map/cond/branch_1_fun/pallas_call | solution.py:529
  111.4 4.2 %all-to-all-start.6 = ((bf16[8,2,128,128]{3,2,1,0:T(8,128)(2,1)}), bf16[8,2,128,128]{3,2,1,0:T(8,128)(2,1)S(1)}, u32[]{:S(2)}, u32[]{:S(2)}) async-start(bf16[8,2,128,128]{3,2,1,0:T(8,128)(2,1)} %get-tuple-element.148), calls=%async_computation.6 | async-start | bytes 1048576 | tf_op jit(solution)/shard_map/cond/branch_1_fun/all_to_all | solution.py:535
  115.5 4.4 %branch_1_fun.24.rest_0_ = f32[16,128,128]{2,1,0:T(8,128)} custom-call(f32[16,128,128]{2,1,0:T(8,128)} %get-tuple-element.153.z_ref.z2_ref, bf16[16,128,128]{2,1,0:T(8,128)(2,1)} %get-tuple-element.205.self_ref, f32[16,128,1]{2,1,0:T(8,128)} %copy.55.res_ref, f32[1,128]{1,0:T(1,128)S(1)} %reshape_tile.5.freq_ref.rest_1_), custom_call_target="tpu_custom_call" | custom-call | tf_op jit(solution)/shard_map/cond/branch_1_fun/pallas_call | solution.py:537
  119.9 4.8 %collective-permute-done.10.arrived_ref = bf16[1296,128]{1,0:T(8,128)(2,1)S(1)} collective-permute-done((bf16[1296,128]{1,0:T(8,128)(2,1)}, bf16[1296,128]{1,0:T(8,128)(2,1)S(1)}, u32[]{:S(2)}, u32[]{:S(2)}) %collective-permute-start.10) | collective-permute-done | bytes 331808 | tf_op jit(solution)/shard_map/cond/branch_1_fun/ppermute | solution.py:525
  124.7 0.0 collective-permute-done.11.beyond_ref
  124.7 2.0 %branch_1_fun.25 = (bf16[2048,128]{1,0:T(8,128)(2,1)}, bf16[16,2048]{1,0:T(8,128)(2,1)}) custom-call(bf16[16,128]{1,0:T(8,128)(2,1)} %pad.6.rows_ref.rest_9_, bf16[1296,128]{1,0:T(8,128)(2,1)} %get-tuple-element.151.left_ref, bf16[1296,128]{1,0:T(8,128)(2,1)} %get-tuple-element.150.right_ref, bf16[1296,128]{1,0:T(8,128)(2,1)S(1)} %collective-permute-done.10.arrived_ref, ...), custom_call_target="tpu_custom_call" | custom-call | flops 17179869184 | bytes 16777216 | tf_op jit(solution)/shard_map/cond/branch_1_fun/pallas_call | solution.py:539
  126.7 4.1 %all-to-all-done.6.incoming_ref = bf16[8,2,128,128]{3,2,1,0:T(8,128)(2,1)S(1)} async-done(((bf16[8,2,128,128]{3,2,1,0:T(8,128)(2,1)}), bf16[8,2,128,128]{3,2,1,0:T(8,128)(2,1)S(1)}, u32[]{:S(2)}, u32[]{:S(2)}) %all-to-all-start.6) | async-done | bytes 524320 | tf_op jit(solution)/shard_map/cond/branch_1_fun/all_to_all | solution.py:535
  130.9 9.0 %branch_1_fun.26 = f32[32,8,128]{2,1,0:T(8,128)S(1)} custom-call(s32[1,68]{1,0:T(1,128)S(1)} %get-tuple-element.112.row_ref, s32[1,272]{1,0:T(1,128)S(1)} %get-tuple-element.113.slot_ref, s32[1]{0:T(128)} %bitcast.5.place_ref, bf16[272,128,128]{2,1,0:T(8,128)(2,1)} %get-tuple-element.137.blocks_ref, ...), custom_call_target="tpu_custom_call" | custom-call | tf_op jit(solution)/shard_map/cond/branch_1_fun/pallas_call | solution.py:570
  139.9 9.6 %all_to_all.38.pay_ref = f32[32,8,128]{2,1,0:T(8,128)S(1)} all-to-all(f32[32,8,128]{2,1,0:T(8,128)S(1)} %branch_1_fun.26), channel_id=1, replica_groups=mesh['wide'=4,'narrow'=8] {'wide','narrow'}, dimensions={0} | all-to-all | bytes 262144 | tf_op jit(solution)/shard_map/cond/branch_1_fun/all_to_all | solution.py:580
  149.5 3.2 %branch_1_fun.27 = (f32[16,128,128]{2,1,0:T(8,128)}, f32[2,32]{1,0:T(2,128)}) custom-call(f32[32,8,128]{2,1,0:T(8,128)S(1)} %all_to_all.38.pay_ref, f32[8,128]{1,0:T(8,128)S(1)} %get-tuple-element.159.beta_ref, f32[16,128,128]{2,1,0:T(8,128)} %get-tuple-element.129.z_ref.z0_ref, f32[16,128,128]{2,1,0:T(8,128)} %get-tuple-element.144.z_ref.z1_ref, ...), custom_call_target="tpu_custom_call" | custom-call | tf_op jit(solution)/shard_map/cond/branch_1_fun/pallas_call | solution.py:581
  (2 shorter events, 0.0 us)
Async XLA Ops:
  2.8 15.0 %all-to-all-start.8 = ((f32[32,8,128]{2,1,0:T(8,128)}), f32[32,8,128]{2,1,0:T(8,128)S(1)}, u32[]{:S(2)}, u32[]{:S(2)}) async-start(f32[32,8,128]{2,1,0:T(8,128)} %shard_map.138), calls=%async_computation.8 | async-start | bytes 262144 | tf_op jit(solution)/shard_map/all_to_all | solution.py:611
  10.1 0.7 copy-start
  20.1 30.6 %copy-start.2 = (s16[2048,2]{1,0:T(8,128)(2,1)}, s16[2048,2]{1,0:T(8,128)(2,1)S(1)}, u32[]{:S(2)}) copy-start(s16[2048,2]{1,0:T(8,128)(2,1)S(1)} %get-tuple-element.133.rest_2_) | copy-start | bytes 24580 | tf_op jit(solution)/shard_map/cond
  26.9 21.7 %collective-permute-start.6 = (bf16[1296,128]{1,0:T(8,128)(2,1)}, bf16[1296,128]{1,0:T(8,128)(2,1)S(1)}, u32[]{:S(2)}, u32[]{:S(2)}) collective-permute-start(bf16[1296,128]{1,0:T(8,128)(2,1)} %get-tuple-element.126.right_ref), channel_id=1, source_target_pairs={{0,1},{1,2},{2,3},{3,4},{4,5},{5,6},{6,7},{8,9},{9,10},{10,11},{11... | collective-permute-start | bytes 995336 | tf_op jit(solution)/shard_map/cond/branch_1_fun/ppermute | solution.py:525
  30.1 18.6 %collective-permute-start.7 = (bf16[1296,128]{1,0:T(8,128)(2,1)}, bf16[1296,128]{1,0:T(8,128)(2,1)S(1)}, u32[]{:S(2)}, u32[]{:S(2)}) collective-permute-start(bf16[1296,128]{1,0:T(8,128)(2,1)} %get-tuple-element.127.left_ref), channel_id=1, source_target_pairs={{1,0},{2,1},{3,2},{4,3},{5,4},{6,5},{7,6},{9,8},{10,9},{11,10},{12... | collective-permute-start | bytes 995336 | tf_op jit(solution)/shard_map/cond/branch_1_fun/ppermute | solution.py:525
  33.3 21.4 %all-to-all-start.4 = ((bf16[8,2,128,128]{3,2,1,0:T(8,128)(2,1)}), bf16[8,2,128,128]{3,2,1,0:T(8,128)(2,1)S(1)}, u32[]{:S(2)}, u32[]{:S(2)}) async-start(bf16[8,2,128,128]{3,2,1,0:T(8,128)(2,1)} %get-tuple-element.124), calls=%async_computation.4 | async-start | bytes 1048576 | tf_op jit(solution)/shard_map/cond/branch_1_fun/all_to_all | solution.py:535
  45.4 9.3 %copy-start.4 = (s32[16]{0:T(128)S(1)}, s32[16]{0:T(128)}, u32[]{:S(2)}) copy-start(s32[16]{0:T(128)} %get-tuple-element.199.jacobi_ref.rest_6_) | copy-start | bytes 196 | tf_op jit(solution)/shard_map/cond
  68.4 19.5 %collective-permute-start.8 = (bf16[1296,128]{1,0:T(8,128)(2,1)}, bf16[1296,128]{1,0:T(8,128)(2,1)S(1)}, u32[]{:S(2)}, u32[]{:S(2)}) collective-permute-start(bf16[1296,128]{1,0:T(8,128)(2,1)} %get-tuple-element.141.right_ref), channel_id=1, source_target_pairs={{0,1},{1,2},{2,3},{3,4},{4,5},{5,6},{6,7},{8,9},{9,10},{10,11},{11... | collective-permute-start | bytes 995336 | tf_op jit(solution)/shard_map/cond/branch_1_fun/ppermute | solution.py:525
  71.1 16.8 %collective-permute-start.9 = (bf16[1296,128]{1,0:T(8,128)(2,1)}, bf16[1296,128]{1,0:T(8,128)(2,1)S(1)}, u32[]{:S(2)}, u32[]{:S(2)}) collective-permute-start(bf16[1296,128]{1,0:T(8,128)(2,1)} %get-tuple-element.142.left_ref), channel_id=1, source_target_pairs={{1,0},{2,1},{3,2},{4,3},{5,4},{6,5},{7,6},{9,8},{10,9},{11,10},{12... | collective-permute-start | bytes 995336 | tf_op jit(solution)/shard_map/cond/branch_1_fun/ppermute | solution.py:525
  74.4 19.5 %all-to-all-start.5 = ((bf16[8,2,128,128]{3,2,1,0:T(8,128)(2,1)}), bf16[8,2,128,128]{3,2,1,0:T(8,128)(2,1)S(1)}, u32[]{:S(2)}, u32[]{:S(2)}) async-start(bf16[8,2,128,128]{3,2,1,0:T(8,128)(2,1)} %get-tuple-element.139), calls=%async_computation.5 | async-start | bytes 1048576 | tf_op jit(solution)/shard_map/cond/branch_1_fun/all_to_all | solution.py:535
  105.4 19.3 %collective-permute-start.10 = (bf16[1296,128]{1,0:T(8,128)(2,1)}, bf16[1296,128]{1,0:T(8,128)(2,1)S(1)}, u32[]{:S(2)}, u32[]{:S(2)}) collective-permute-start(bf16[1296,128]{1,0:T(8,128)(2,1)} %get-tuple-element.150.right_ref), channel_id=1, source_target_pairs={{0,1},{1,2},{2,3},{3,4},{4,5},{5,6},{6,7},{8,9},{9,10},{10,11},{11... | collective-permute-start | bytes 995336 | tf_op jit(solution)/shard_map/cond/branch_1_fun/ppermute | solution.py:525
  108.1 16.6 %collective-permute-start.11 = (bf16[1296,128]{1,0:T(8,128)(2,1)}, bf16[1296,128]{1,0:T(8,128)(2,1)S(1)}, u32[]{:S(2)}, u32[]{:S(2)}) collective-permute-start(bf16[1296,128]{1,0:T(8,128)(2,1)} %get-tuple-element.151.left_ref), channel_id=1, source_target_pairs={{1,0},{2,1},{3,2},{4,3},{5,4},{6,5},{7,6},{9,8},{10,9},{11,10},{12... | collective-permute-start | bytes 995336 | tf_op jit(solution)/shard_map/cond/branch_1_fun/ppermute | solution.py:525
  111.4 19.5 %all-to-all-start.6 = ((bf16[8,2,128,128]{3,2,1,0:T(8,128)(2,1)}), bf16[8,2,128,128]{3,2,1,0:T(8,128)(2,1)S(1)}, u32[]{:S(2)}, u32[]{:S(2)}) async-start(bf16[8,2,128,128]{3,2,1,0:T(8,128)(2,1)} %get-tuple-element.148), calls=%async_computation.6 | async-start | bytes 1048576 | tf_op jit(solution)/shard_map/cond/branch_1_fun/all_to_all | solution.py:535

commit v5 on v4

--- a/solution.py
+++ b/solution.py
@@ -99,7 +99,19 @@
     pay_ref[...] = jnp.broadcast_to(rows[None], pay_ref.shape)
 
 
-def order_kernel(peers, blocks, lists_ref, order_ref, slot_ref, row_ref):
+def order_kernel(
+    peers, blocks, lists_ref, pairs_ref, pcoef_ref, omega_ref, order_ref, slot_ref, row_ref, ends_ref,
+    rows_ref, cols_ref, freq_ref,
+):
+    for k in range(2):
+        row = jnp.broadcast_to(pairs_ref[k : k + 1, :], (16, pairs_ref.shape[1]))
+        ends_ref[16 * k : 16 * (k + 1), :] = row.astype(i16)
+    numbers = pairs_ref[...].astype(f32)
+    numbers = jnp.concatenate([numbers, jnp.zeros((6, numbers.shape[1]), f32)], axis=0)
+    cols_ref[...] = jnp.transpose(numbers)[:, :2].astype(i32).astype(i16)
+    freq_ref[...] = jnp.concatenate([omega_ref[...]] * (2 * CASES), axis=1)
+    own = pcoef_ref[...]
+    rows_ref[...] = jnp.concatenate([own, jnp.zeros_like(own)], axis=0).astype(bf16)
     entries = lists_ref.shape[1]
     places = order_ref.shape[1]
     quads = row_ref.shape[1]
@@ -164,7 +176,7 @@
 
 def emit(
     plan, w_of, ends_ref, jacobi_ref, needs_ref, place_ref, table_ref, rows_ref,
-    z_ref, zb_out_ref, right_ref, left_ref, zv_ref, zb_ref, both_ref, sems,
+    z_ref, send_ref, own_ref, right_ref, left_ref, go_refs, zv_ref, zb_ref, sv_ref, both_ref, sems,
 ):
     blocks, size, width = zb_ref.shape
     peers = needs_ref.shape[0]
@@ -175,11 +187,16 @@
         z = jnp.dot(table_ref[jacobi_ref[n]], w_of(n).astype(bf16), preferred_element_type=f32)
         zv_ref[n] = z
         zb_ref[n] = z.astype(bf16)
-    pack = pltpu.make_async_copy(zb_ref, zb_out_ref, sems.at[1])
+    for j in range(peers):
+        for s in range(base):
+            sv_ref[j, s] = zb_ref[needs_ref[j, s]]
+    pack = pltpu.make_async_copy(sv_ref, send_ref, sems.at[1])
     pack.start()
     save = pltpu.make_async_copy(zv_ref, z_ref, sems.at[0])
     save.start()
     mine = place_ref[0]
+    for s in range(CAP):
+        own_ref[s] = zb_ref[needs_ref[mine, s]]
     left_ref[pl.ds(nodes, node_rows), :] = rows_ref[...]
     right_ref[pl.ds(nodes, node_rows), :] = rows_ref[...]
     for s in range(base, plan[1]):
@@ -187,58 +204,54 @@
             peer = jnp.clip(mine + step, 0, peers - 1)
             there = nodes + node_rows + (s - base) * size
             out[pl.ds(there, size), :] = zb_ref[needs_ref[peer, s]]
-    chunk = nodes if base < CAP else 128
-
-    def body(step, carry):
-        start = pl.multiple_of(step * chunk, chunk)
-        both_ref[pl.ds(start, chunk), :] = charges(ends_ref, zb_ref, start, chunk)
-        return carry
-
-    lax.fori_loop(0, 2 * nodes // chunk, body, 0)
-    left_ref[pl.ds(0, nodes), :] = both_ref[pl.ds(0, nodes), :]
-    right_ref[pl.ds(0, nodes), :] = both_ref[pl.ds(nodes, nodes), :]
-    save.wait()
-    pack.wait()
-
-
-def pack_kernel(plan, needs_ref, place_ref, zb_ref, send_ref, own_ref, *extra_refs):
-    peers, base = send_ref.shape[:2]
-    mine = place_ref[0]
-    for j in range(peers):
-        for s in range(base):
-            send_ref[j, s] = zb_ref[needs_ref[j, s]]
-    for s in range(CAP):
-        own_ref[s] = zb_ref[needs_ref[mine, s]]
     at = 0
     for distance in range(2, peers):
         if plan[distance] > base:
             for step in (distance, -distance):
                 peer = jnp.clip(mine + step, 0, peers - 1)
                 for s in range(base, plan[distance]):
-                    extra_refs[at][s - base] = zb_ref[needs_ref[peer, s]]
+                    go_refs[at][s - base] = zb_ref[needs_ref[peer, s]]
                 at += 1
+    chunk = nodes if base < CAP else 128
+
+    def body(step, carry):
+        start = pl.multiple_of(step * chunk, chunk)
+        both_ref[pl.ds(start, chunk), :] = charges(ends_ref, zb_ref, start, chunk)
+        return carry
+
+    lax.fori_loop(0, 2 * nodes // chunk, body, 0)
+    left_ref[pl.ds(0, nodes), :] = both_ref[pl.ds(0, nodes), :]
+    right_ref[pl.ds(0, nodes), :] = both_ref[pl.ds(nodes, nodes), :]
+    save.wait()
+    pack.wait()
 
 
 def start_kernel(
     plan, pay_ref, side_ref, ends_ref, jacobi_ref, needs_ref, place_ref, table_ref, rows_ref,
-    w_ref, beta_ref, z_ref, zb_out_ref, right_ref, left_ref, zv_ref, zb_ref, both_ref, sems,
-):
+    w_ref, beta_ref, z_ref, send_ref, own_ref, right_ref, left_ref, *rest,
+):
+    go, rest = split(plan, rest)
+    wv_ref, zv_ref, zb_ref, sv_ref, both_ref, sems = rest
     total = jnp.sum(pay_ref[:, 0, :], axis=0, keepdims=True)
     beta = jnp.sqrt(both_parts(total))
     beta_ref[...] = jnp.broadcast_to(beta, beta_ref.shape)
-    w_ref[...] = side_ref[...] / beta[None]
+    wv_ref[...] = side_ref[...] / beta[None]
+    save = pltpu.make_async_copy(wv_ref, w_ref, sems.at[2])
+    save.start()
     emit(
-        plan, lambda n: w_ref[n], ends_ref, jacobi_ref, needs_ref, place_ref, table_ref, rows_ref,
-        z_ref, zb_out_ref, right_ref, left_ref, zv_ref, zb_ref, both_ref, sems,
-    )
+        plan, lambda n: wv_ref[n], ends_ref, jacobi_ref, needs_ref, place_ref, table_ref, rows_ref,
+        z_ref, send_ref, own_ref, right_ref, left_ref, go, zv_ref, zb_ref, sv_ref, both_ref, sems,
+    )
+    save.wait()
 
 
 def local_kernel(z_ref, self_ref, res_ref, freq_ref, part_ref):
     freq = freq_ref[...]
+    res = jnp.transpose(res_ref[...])
     for n in range(z_ref.shape[0]):
         z = z_ref[n]
         flux = jnp.dot(self_ref[n], z.astype(bf16), preferred_element_type=f32)
-        part_ref[n] = freq * flux - turned(res_ref[n] * z)
+        part_ref[n] = freq * flux - turned(res[:, n : n + 1] * z)
 
 
 def charge_kernel(rows_ref, left_ref, right_ref, arrived_ref, beyond_ref, charge_ref, plus_ref):
@@ -254,12 +267,13 @@
     plus_ref[...] = jnp.broadcast_to(row, (16, 2 * nodes)).astype(bf16)
 
 
-def drop_into(acc_ref, group, freq_ref, cols_ref, charge_ref, plus_ref):
+def drop_into(acc_ref, group, beside, freq_ref, cols_ref, charge_ref, plus_ref):
     blocks, size, width = acc_ref.shape
     scale = 1.0 / (freq_ref[...] * freq_ref[...])
 
     def body(step, carry):
         start = pl.multiple_of(step * group * size, group * size)
+        beside(step)
         plus = plus_ref[...]
         node = lax.broadcasted_iota(i32, plus.shape, 1).astype(i16)
         none = jnp.zeros_like(plus)
@@ -289,19 +303,16 @@
         source = held_ref if order_ref is not None else blocks_ref
         return pltpu.make_async_copy(source.at[here], held_ref.at[here], sems.at[step])
 
-    for step in range(runs):
-        if order_ref is None:
+    def fetch(i, carry, step):
+        p = step * piece + i
+        pltpu.make_async_copy(
+            blocks_ref.at[order_ref[0, p]], held_ref.at[p], sems.at[step]
+        ).start()
+        return carry
+
+    if order_ref is None:
+        for step in range(runs):
             copy(step).start()
-            continue
-
-        def fetch(i, carry, step=step):
-            p = step * piece + i
-            pltpu.make_async_copy(
-                blocks_ref.at[order_ref[0, p]], held_ref.at[p], sems.at[step]
-            ).start()
-            return carry
-
-        lax.fori_loop(0, piece, fetch, 0, unroll=4)
     for fetched in later:
         fetched.start()
     peers, base, size, width = incoming_ref.shape
@@ -326,7 +337,18 @@
                 else:
                     block = extra_refs[2 * (distance - 2) + side][s - base]
                 source_ref[slot] = block
-    drop_into(acc_ref, acc_ref.shape[0] // 2 if base < CAP else 1, *drop_refs)
+    halves = base < CAP and runs % 2 == 0
+
+    def beside(step):
+        if order_ref is not None and halves:
+            for r in range(runs // 2):
+                for i in range(piece):
+                    fetch(i, 0, step=step * (runs // 2) + r)
+
+    if order_ref is not None and not halves:
+        for step in range(runs):
+            lax.fori_loop(0, piece, functools.partial(fetch, step=step), 0)
+    drop_into(acc_ref, acc_ref.shape[0] // 2 if base < CAP else 1, beside, *drop_refs)
 
     def body(step, carry):
         copy(step).wait()
@@ -358,7 +380,7 @@
 
 
 def middle_kernel(
-    plan, first, row_ref, slot_ref, place_ref, blocks_ref, incoming_ref, own_ref, arrived_ref,
+    plan, first, row_ref, slot_ref, place_ref, blocks_ref, incoming_ref, own_in_ref, arrived_ref,
     beyond_ref, *rest,
 ):
     come, rest = split(plan, rest)
@@ -368,14 +390,14 @@
     order_ref = None
     if first:
         order_ref, rest = rest[0], rest[1:]
-    w_ref, z_ref, zb_out_ref, right_ref, left_ref = rest[:5]
-    rest = rest[5:]
+    w_ref, z_ref, send_ref, own_ref, right_ref, left_ref = rest[:6]
+    go, rest = split(plan, rest[6:])
     if first:
         sorted_ref, rest = rest[0], rest[1:]
-    acc_ref, source_ref, held_ref, run_sems, wv_ref, zv_ref, zb_ref, both_ref, sems = rest
+    acc_ref, source_ref, held_ref, run_sems, wv_ref, zv_ref, zb_ref, sv_ref, both_ref, sems = rest
     bring = pltpu.make_async_copy(part_ref, zv_ref, sems.at[0])
     couple(
-        plan, order_ref, row_ref, slot_ref, place_ref, blocks_ref, incoming_ref, own_ref,
+        plan, order_ref, row_ref, slot_ref, place_ref, blocks_ref, incoming_ref, own_in_ref,
         arrived_ref, beyond_ref, come, (freq_ref, cols_ref, charge_ref, plus_ref), acc_ref,
         source_ref, held_ref, run_sems, [bring],
     )
@@ -388,7 +410,7 @@
     save.start()
     emit(
         plan, lambda n: wv_ref[n], ends_ref, jacobi_ref, needs_ref, place_ref, table_ref, rows_ref,
-        z_ref, zb_out_ref, right_ref, left_ref, zv_ref, zb_ref, both_ref, sems,
+        z_ref, send_ref, own_ref, right_ref, left_ref, go, zv_ref, zb_ref, sv_ref, both_ref, sems,
     )
     save.wait()
     if first:
@@ -435,7 +457,22 @@
     pay_ref[...] = jnp.broadcast_to(jnp.concatenate(rows, axis=0)[None], pay_ref.shape)
 
 
-def finish_kernel(pay_ref, beta_ref, z0_ref, z1_ref, z2_ref, out_ref, norm_ref):
+def finish_kernel(
+    pay_ref, beta_ref, z0_ref, z1_ref, z2_ref, out_ref, norm_ref, held_ref, made_ref, in_sems, out_sems,
+):
+    parts = out_sems.shape[0]
+    group = out_ref.shape[0] // parts
+    arrive = []
+    for p in range(parts):
+        here = pl.ds(p * group, group)
+        arrive.append(
+            [
+                pltpu.make_async_copy(z.at[here], held_ref.at[k, here], in_sems.at[p, k])
+                for k, z in enumerate((z0_ref, z1_ref, z2_ref))
+            ]
+        )
+        for copy in arrive[p]:
+            copy.start()
     total = jnp.sum(pay_ref[...], axis=0)
     real = lane_is_real(total.shape)
     even = jnp.where(real, total, pltpu.roll(total, F, 1))
@@ -462,8 +499,20 @@
     norm = low[ITERS, ITERS] * beta
     norm_ref[...] = jnp.concatenate([norm, pltpu.roll(norm, 2 * F, 1)], axis=0)[:, :F]
     weights = [STEP * beta * weight for weight in weights]
-    for n in range(out_ref.shape[0]):
-        out_ref[n] = weights[0] * z0_ref[n] + weights[1] * z1_ref[n] + weights[2] * z2_ref[n]
+    leave = []
+    for p in range(parts):
+        for copy in arrive[p]:
+            copy.wait()
+        for n in range(p * group, (p + 1) * group):
+            total = weights[0] * held_ref[0, n]
+            for k in range(1, ITERS):
+                total = total + weights[k] * held_ref[k, n]
+            made_ref[n] = total
+        here = pl.ds(p * group, group)
+        leave.append(pltpu.make_async_copy(made_ref.at[here], out_ref.at[here], out_sems.at[p]))
+        leave[p].start()
+    for copy in leave:
+        copy.wait()
 
 
 def call(kernel, outs, ins, places=None, **more):
@@ -490,15 +539,18 @@
     far = [d for d in range(2, peers) if plan[d] > base]
     halo = kept((nodes + scale.shape[0] + (plan[1] - base) * size, width), bf16)
     vec = kept((blocks, size, width), f32)
-    emitted = [vec, kept((blocks, size, width), bf16), halo, halo]
-    packed = [
+    emitted = [
+        vec,
         kept((peers, base, size, width), bf16),
         kept((CAP, size, width), bf16),
+        halo,
+        halo,
     ] + [kept((plan[d] - base, size, width), bf16) for d in far for side in range(2)]
-    spots = [HB, HB, VM, VM]
+    spots = [HB, HB] + [VM] * (len(emitted) - 2)
     buffers = [
         pltpu.VMEM((blocks, size, width), f32),
         pltpu.VMEM((blocks, size, width), bf16),
+        pltpu.VMEM((peers, base, size, width), bf16),
         pltpu.VMEM((2 * nodes, width), bf16),
         pltpu.SemaphoreType.DMA((4,)),
     ]
@@ -509,12 +561,12 @@
         pltpu.VMEM((places, size, size), bf16),
         pltpu.SemaphoreType.DMA((places // (RUN * QUAD),)),
     ]
-    w, beta, z, zb, right, left = call(
+    w, beta, z, send, own, right, left, *go = call(
         functools.partial(start_kernel, plan),
         [vec, whole((8, width), f32)] + emitted,
         [VM, VM, VM, SM, SM, SM, VM, VM],
-        [VM, VM] + spots,
-        scratch_shapes=buffers,
+        [HB, VM] + spots,
+        scratch_shapes=[pltpu.VMEM((blocks, size, width), f32)] + buffers,
     )(near_core(pay), right_side, ends, jacobi_ids, needs, place, table, scale)
     basis = [w]
     fields = [z]
@@ -526,19 +578,20 @@
 
         arrived = moved(right, 1)
         beyond = moved(left, -1)
-        send, own, *go = call(functools.partial(pack_kernel, plan), packed, [SM, SM, VM])(
-            needs, place, in_hbm(zb)
-        )
         come = []
         for at, d in enumerate(far):
             come += [moved(go[2 * at], d), moved(go[2 * at + 1], -d)]
         incoming = near_core(lax.all_to_all(send, "narrow", 0, 0))
-        later, send = lax.optimization_barrier((z, send))
-        (part,) = call(local_kernel, [vec], [VM] * 4)(in_hbm(later), selfs, res, freq)
+        parts = 2 if blocks % 16 == 0 else 1
+        block = pl.BlockSpec((blocks // parts, size, width), lambda i: (i, 0, 0))
+        line = pl.BlockSpec((blocks // parts, size), lambda i: (i, 0))
+        (part,) = call(
+            local_kernel, [vec], [block, block, line, VM], [block], grid=(parts,)
+        )(in_hbm(z), selfs, res, in_hbm(freq))
         head = pl.BlockSpec((nodes, width), lambda i: (0, 0))
         charge, plus = call(
             charge_kernel,
-            [kept((2 * nodes, width), bf16), kept((16, 2 * nodes), bf16)],
+            [pltpu.VMEM((2 * nodes, width), bf16), pltpu.VMEM((16, 2 * nodes), bf16)],
             [VM, head, head, VM, VM],
             grid=(1,),
             cost_estimate=pl.CostEstimate(
@@ -551,19 +604,20 @@
         held = couple_blocks if first else sorted_blocks
         common = (
             rows, slots, place, in_hbm(held), incoming, in_hbm(own), arrived, beyond, *come,
-            in_hbm(part), freq, ends_col, in_hbm(charge), in_hbm(plus),
+            in_hbm(part), in_hbm(freq), ends_col, charge, plus,
         )
         specs = [SM, SM, SM, HB] + [VM] * (4 + len(come)) + [HB] + [VM] * 4
         if step + 1 < ITERS:
-            w, z, zb, right, left, *copies = call(
+            w, z, send, own, right, left, *more = call(
                 functools.partial(middle_kernel, plan, first),
                 [vec] + emitted + ([kept((places, size, size), bf16)] if first else []),
                 specs + [VM, SM, SM, VM, VM] + ([SM] if first else []),
                 [HB] + spots + ([HB] if first else []),
                 scratch_shapes=coupling + [pltpu.VMEM((blocks, size, width), f32)] + buffers,
             )(*common, ends, jacobi_ids, needs, table, scale, *([order] if first else []))
+            go = more[: extras(plan)]
             if first:
-                (sorted_blocks,) = copies
+                sorted_blocks = more[-1]
             basis.append(w)
             fields.append(z)
         else:
@@ -578,7 +632,21 @@
                 ],
             )(*common, *map(in_hbm, basis))
     sums = near_core(lax.all_to_all(sums, AXES, 0, 0))
-    return call(finish_kernel, [vec, whole((CASES, F), f32)], [VM] * 5)(
+    parts = 4
+    while blocks % parts:
+        parts //= 2
+    return call(
+        finish_kernel,
+        [vec, whole((CASES, F), f32)],
+        [VM, VM] + [HB] * ITERS,
+        [HB, VM],
+        scratch_shapes=[
+            pltpu.VMEM((ITERS, blocks, size, width), f32),
+            pltpu.VMEM((blocks, size, width), f32),
+            pltpu.SemaphoreType.DMA((parts, ITERS)),
+            pltpu.SemaphoreType.DMA((parts,)),
+        ],
+    )(
         sums, beta, *map(in_hbm, fields)
     )
 
@@ -595,11 +663,8 @@
     group = lax.axis_index("wide")
     mine = lax.axis_index("narrow")
     node_rows = nodes // NODE_ROW
-    freq = jnp.tile(omega, 2 * CASES).reshape(1, width)
     pairs = jnp.transpose(branch_nodes, (1, 0, 2)).reshape(2, blocks * size)
     pairs = jnp.where(pairs[0] == pairs[1], -1, pairs)
-    ends = jnp.repeat(pairs.astype(i16), 16, axis=0)
-    ends_col = jnp.transpose(pairs).astype(i16)
     quads = (entries + (QUAD - 1) * blocks) // QUAD
     quads = -(-quads // RUN) * RUN
 
@@ -609,23 +674,30 @@
         [VM] * 2,
     )(in_hbm(couple_list), in_hbm(right_side))
     pay = lax.all_to_all(pay, AXES, 0, 0)
-    order, slots, rows = call(
+    order, slots, rows, ends, rows16, ends_col, freq = call(
         functools.partial(order_kernel, peers, blocks),
-        [whole((1, quads * QUAD), i32), whole((1, quads * QUAD), i32), whole((1, quads), i32)],
-        [VM],
-    )(couple_list)
+        [
+            whole((1, quads * QUAD), i32),
+            whole((1, quads * QUAD), i32),
+            whole((1, quads), i32),
+            kept((32, blocks * size), i16),
+            kept((PAD * node_rows, NODE_ROW), bf16),
+            kept((blocks * size, 2), i16),
+            kept((1, width), f32),
+        ],
+        [VM] * 4,
+    )(couple_list, pairs, pcoef.reshape(node_rows, NODE_ROW), omega.reshape(1, -1))
     needs = lax.dynamic_slice(
         pay, (group * peers, 1, mine * CAP), (peers, 1, CAP)
     ).reshape(peers, CAP).astype(i32)
-    rows16 = jnp.pad(pcoef.astype(bf16).reshape(node_rows, 128), ((0, node_rows), (0, 0)))
     shared = (
         pay, in_hbm(right_side), jacobi_ids, needs, mine.reshape(1), in_hbm(preconditioners),
         in_hbm(ends), in_hbm(ends_col), in_hbm(self_blocks),
-        in_hbm(resistance.reshape(blocks, size, 1)), in_hbm(rows16), freq, (order, slots, rows),
+        in_hbm(resistance), in_hbm(rows16), freq, (order, slots, rows),
         in_hbm(couple_blocks),
     )
     full = (CAP,) * peers
-    near = (2,) + tuple(max(2, CAP // distance) for distance in range(1, peers))
+    near = (1,) + tuple(max(1, CAP // distance) for distance in range(1, peers))
     reach = np.abs(np.arange(devices)[:, None] % peers - np.arange(peers)[None, :])
     allowed = np.where(reach == 0, CAP, np.asarray(near)[reach]).astype(np.float32)
     fits = jnp.all(pay[:, 2, :peers] <= allowed)

time: 154 us -> 147 us (0.955)
  starting transfers between devices: 32.7 us -> 54.4 us
  waiting for transfers between devices: 30.1 us -> 13.6 us
  Pallas kernels: 70.5 us -> 60.5 us
  local copies, waits for them, and re-layouts: 5.96 us -> 2.75 us
    ppermute x6 -> x12, starting transfers between devices: 12.4 us -> 29.7 us  [moved(): return near_core(lax.ppermute(value, 'narrow', route))]
    pallas_call x10 -> x7, Pallas kernels: 28.1 us -> 18.4 us  [the longest x3 11.5 us: iterate(): call(local_kernel, [vec], [block, block, line, VM], [block], grid=(parts,))]
    ppermute x6 -> x12, waiting for transfers between devices: 13.4 us -> 3.74 us  [moved(): return near_core(lax.ppermute(value, 'narrow', route))]
    all_to_all x3, waiting for transfers between devices: 12.1 us -> 6.33 us  [iterate(): incoming = near_core(lax.all_to_all(send, 'narrow', 0, 0))]
    all_to_all x3, starting transfers between devices: 13 us -> 17.5 us  [iterate(): incoming = near_core(lax.all_to_all(send, 'narrow', 0, 0))]
    reshape x1 -> x0, local copies, waits for them, and re-layouts: 2.06 us -> none  [on_device(): resistance.reshape(blocks, size, 1)]
  transfers between devices with their start and end apart: 10 -> 16, of which waited for: 7 -> 6; matrix products, arithmetic and copies ran while one was open for 3% -> 1% of each run, Pallas kernels for 17% -> 11%
where the time goes in v5:
time: 147 us; the launch traced here: 146 us
  Pallas kernels  60.5 us (41%)
  starting transfers between devices  54.4 us (37%)
  waiting for transfers between devices  13.6 us (9%)
  blocking collectives  11.1 us (8%)
  local copies, waits for them, and re-layouts  2.75 us (2%)
  between operations  1.51 us (1%)
  other arithmetic  1.5 us (1%)
    ppermute x12, starting transfers between devices, moved(): return near_core(lax.ppermute(value, 'narrow', route))  29.7 us
    pallas_call x2, Pallas kernels, iterate(): call(functools.partial(middle_kernel, plan, first), [vec] + emitted + ([k...  24.3 us
    all_to_all x3, starting transfers between devices, iterate(): incoming = near_core(lax.all_to_all(send, 'narrow', 0, 0))  17.5 us
    pallas_call x3, Pallas kernels, iterate(): call(local_kernel, [vec], [block, block, line, VM], [block], grid=(parts,))  11.5 us
    all_to_all x1, blocking collectives, iterate(): sums = near_core(lax.all_to_all(sums, AXES, 0, 0))  11.1 us
    pallas_call x1, Pallas kernels, iterate(): call(functools.partial(last_kernel, plan), [whole((devices, 8, 128), f32)...  8.91 us
    all_to_all x1, starting transfers between devices, on_device(): pay = lax.all_to_all(pay, AXES, 0, 0)  7.3 us
    all_to_all x3, waiting for transfers between devices, iterate(): incoming = near_core(lax.all_to_all(send, 'narrow', 0, 0))  6.33 us
  transfers between devices with their start and end apart: 16, of which 6 were waited for; matrix products, arithmetic and copies ran while one was open for 1% of the time, Pallas kernels for 11%

profile of v5, /device:TPU:0, one launch (start us, length us, event | category | flops | bytes accessed | tf_op | source)
XLA Modules:
  0.0 146.0 jit_solution(17926032980001756637)
XLA Ops:
  0.6 2.2 %shard_map.136 = f32[32,8,128]{2,1,0:T(8,128)} custom-call(s32[3,224]{1,0:T(4,128)} %lists_ref.3, f32[16,128,128]{2,1,0:T(8,128)} %right_ref.1), custom_call_target="tpu_custom_call" | custom-call | tf_op jit(solution)/shard_map/pallas_call | solution.py:671
  2.8 7.3 %all-to-all-start.8 = ((f32[32,8,128]{2,1,0:T(8,128)}), f32[32,8,128]{2,1,0:T(8,128)S(1)}, u32[]{:S(2)}, u32[]{:S(2)}) async-start(f32[32,8,128]{2,1,0:T(8,128)} %shard_map.136), calls=%async_computation.8 | async-start | bytes 262144 | tf_op jit(solution)/shard_map/all_to_all | solution.py:676
  10.1 0.7 copy.50
  10.8 0.0 copy-start
  10.9 0.7 copy-done
  11.5 0.0 copy-start.1
  11.5 0.7 copy-done.1
  12.2 0.0 copy-start.2
  12.2 0.7 copy-done.2
  12.9 1.4 shard_map.137
  14.3 3.6 %all-to-all-done.8 = f32[32,8,128]{2,1,0:T(8,128)S(1)} async-done(((f32[32,8,128]{2,1,0:T(8,128)}), f32[32,8,128]{2,1,0:T(8,128)S(1)}, u32[]{:S(2)}, u32[]{:S(2)}) %all-to-all-start.8) | async-done | bytes 131104 | tf_op jit(solution)/shard_map/all_to_all | solution.py:676
  17.8 1.4 compare_reduce_fusion
  19.9 0.1 dynamic-slice_convert_fusion
  20.0 125.9 %conditional.1 = ((f32[16,128,128]{2,1,0:T(8,128)}, f32[2,32]{1,0:T(2,128)})) conditional(s32[]{:T(128)} %convert_element_type.9, (f32[32,8,128]{2,1,0:T(8,128)S(1)}, f32[16,128,128]{2,1,0:T(8,128)}, s16[32,2048]{1,0:T(8,128)(2,1)}, s32[16]{0:T(128)}, s32[8,1,4]{2,1,0:T(1,128)S(1)}, /*index=5*/s32[]{:T(128)}, bf16[8,128,128]{2,1,0:T(8,128)(2,1)}, ...), branch_computations={%region_1.2_spmd, %region_2.3_spmd} | conditional | flops 51539607552 | bytes 66421364 | solution.py:704
  20.1 5.4 %branch_1_fun.11 = (f32[16,128,128]{2,1,0:T(8,128)}, f32[8,128]{1,0:T(8,128)S(1)}, f32[16,128,128]{2,1,0:T(8,128)}, bf16[8,1,128,128]{3,2,1,0:T(8,128)(2,1)}, bf...) custom-call(f32[32,8,128]{2,1,0:T(8,128)S(1)} %get-tuple-element.110, ...), custom_call_target="tpu_custom_call" | custom-call | tf_op jit(solution)/shard_map/cond/branch_1_fun/pallas_call | solution.py:564
  25.5 3.2 %collective-permute-start.6 = (bf16[1424,128]{1,0:T(8,128)(2,1)}, bf16[1424,128]{1,0:T(8,128)(2,1)S(1)}, u32[]{:S(2)}, u32[]{:S(2)}) collective-permute-start(bf16[1424,128]{1,0:T(8,128)(2,1)} %get-tuple-element.119.right_ref), channel_id=1, source_target_pairs={{0,1},{1,2},{2,3},{3,4},{4,5},{5,6},{6,7},{8,9},{9,10},{10,11},{11... | collective-permute-start | bytes 1093640 | tf_op jit(solution)/shard_map/cond/branch_1_fun/ppermute | solution.py:577
  28.7 1.3 collective-permute-start.7
  30.0 4.9 %all-to-all-start.4 = ((bf16[8,1,128,128]{3,2,1,0:T(8,128)(2,1)}), bf16[8,1,128,128]{3,2,1,0:T(8,128)(2,1)S(1)}, u32[]{:S(2)}, u32[]{:S(2)}) async-start(bf16[8,1,128,128]{3,2,1,0:T(8,128)(2,1)} %get-tuple-element.117), calls=%async_computation.4 | async-start | bytes 524288 | tf_op jit(solution)/shard_map/cond/branch_1_fun/all_to_all | solution.py:584
  34.9 3.9 %collective-permute-start.8 = (bf16[1,128,128]{2,1,0:T(8,128)(2,1)}, bf16[1,128,128]{2,1,0:T(8,128)(2,1)S(1)}, u32[]{:S(2)}, u32[]{:S(2)}) collective-permute-start(bf16[1,128,128]{2,1,0:T(8,128)(2,1)} %get-tuple-element.121), channel_id=1, source_target_pairs={{0,2},{1,3},{2,4},{3,5},{4,6},{5,7},{8,10},{9,11},{10,12},{11,13},... | collective-permute-start | bytes 98312 | tf_op jit(solution)/shard_map/cond/branch_1_fun/ppermute | solution.py:577
  38.8 1.3 collective-permute-start.9
  40.1 3.8 %branch_1_fun.12.rest_2_ = f32[16,128,128]{2,1,0:T(8,128)} custom-call(f32[16,128,128]{2,1,0:T(8,128)} %get-tuple-element.123.z_ref.z0_ref, bf16[16,128,128]{2,1,0:T(8,128)(2,1)} %get-tuple-element.195.self_ref, f32[16,128]{1,0:T(8,128)} %get-tuple-element.197.res_ref, f32[1,128]{1,0:T(1,128)} %get-tuple-element.126.freq_ref.rest_3_), custom_call_target="tpu_custom_call" | custom-call | tf_op jit(solution)/shard_map/cond/branch_1_fun/pallas_call | solution.py:588
  44.0 0.0 copy-start.4
  44.0 2.9 %collective-permute-done.6.arrived_ref = bf16[1424,128]{1,0:T(8,128)(2,1)S(1)} collective-permute-done((bf16[1424,128]{1,0:T(8,128)(2,1)}, bf16[1424,128]{1,0:T(8,128)(2,1)S(1)}, u32[]{:S(2)}, u32[]{:S(2)}) %collective-permute-start.6) | collective-permute-done | bytes 364576 | tf_op jit(solution)/shard_map/cond/branch_1_fun/ppermute | solution.py:577
  46.9 0.0 collective-permute-done.7.beyond_ref
  46.9 1.2 branch_1_fun.13
  48.1 0.0 collective-permute-done.8.rest_0_
  48.1 0.0 collective-permute-done.9.rest_1_
  48.1 0.6 all-to-all-done.4.incoming_ref
  48.7 0.0 copy-done.4
  48.7 12.8 %branch_1_fun.14 = (f32[16,128,128]{2,1,0:T(8,128)}, f32[16,128,128]{2,1,0:T(8,128)}, bf16[8,1,128,128]{3,2,1,0:T(8,128)(2,1)}, bf16[4,128,128]{2,1,0:T(8,128)(2...) custom-call(s32[1,68]{1,0:T(1,128)S(1)} %get-tuple-element.106.row_r, ...), custom_call_target="tpu_custom_call" | custom-call | tf_op jit(solution)/shard_map/cond/branch_1_fun/pallas_call | solution.py:611
  61.5 3.7 %collective-permute-start.10 = (bf16[1424,128]{1,0:T(8,128)(2,1)}, bf16[1424,128]{1,0:T(8,128)(2,1)S(1)}, u32[]{:S(2)}, u32[]{:S(2)}) collective-permute-start(bf16[1424,128]{1,0:T(8,128)(2,1)} %get-tuple-element.134.right_ref), channel_id=1, source_target_pairs={{0,1},{1,2},{2,3},{3,4},{4,5},{5,6},{6,7},{8,9},{9,10},{10,11},{11... | collective-permute-start | bytes 1093640 | tf_op jit(solution)/shard_map/cond/branch_1_fun/ppermute | solution.py:577
  65.3 1.3 collective-permute-start.11
  66.6 5.9 %all-to-all-start.5 = ((bf16[8,1,128,128]{3,2,1,0:T(8,128)(2,1)}), bf16[8,1,128,128]{3,2,1,0:T(8,128)(2,1)S(1)}, u32[]{:S(2)}, u32[]{:S(2)}) async-start(bf16[8,1,128,128]{3,2,1,0:T(8,128)(2,1)} %get-tuple-element.132), calls=%async_computation.5 | async-start | bytes 524288 | tf_op jit(solution)/shard_map/cond/branch_1_fun/all_to_all | solution.py:584
  72.5 3.9 %collective-permute-start.12 = (bf16[1,128,128]{2,1,0:T(8,128)(2,1)}, bf16[1,128,128]{2,1,0:T(8,128)(2,1)S(1)}, u32[]{:S(2)}, u32[]{:S(2)}) collective-permute-start(bf16[1,128,128]{2,1,0:T(8,128)(2,1)} %get-tuple-element.136), channel_id=1, source_target_pairs={{0,2},{1,3},{2,4},{3,5},{4,6},{5,7},{8,10},{9,11},{10,12},{11,13},... | collective-permute-start | bytes 98312 | tf_op jit(solution)/shard_map/cond/branch_1_fun/ppermute | solution.py:577
  76.4 1.3 collective-permute-start.13
  77.7 3.8 %branch_1_fun.15.rest_2_ = f32[16,128,128]{2,1,0:T(8,128)} custom-call(f32[16,128,128]{2,1,0:T(8,128)} %get-tuple-element.138.z_ref.z1_ref, bf16[16,128,128]{2,1,0:T(8,128)(2,1)} %get-tuple-element.195.self_ref, f32[16,128]{1,0:T(8,128)} %get-tuple-element.197.res_ref, f32[1,128]{1,0:T(1,128)} %get-tuple-element.126.freq_ref.rest_3_), custom_call_target="tpu_custom_call" | custom-call | tf_op jit(solution)/shard_map/cond/branch_1_fun/pallas_call | solution.py:588
  81.6 0.8 collective-permute-done.10.arrived_ref
  82.4 0.0 collective-permute-done.11.beyond_ref
  82.4 1.2 branch_1_fun.16
  83.6 0.0 collective-permute-done.12.rest_0_
  83.6 0.0 collective-permute-done.13.rest_1_
  83.6 2.6 %all-to-all-done.5.incoming_ref = bf16[8,1,128,128]{3,2,1,0:T(8,128)(2,1)S(1)} async-done(((bf16[8,1,128,128]{3,2,1,0:T(8,128)(2,1)}), bf16[8,1,128,128]{3,2,1,0:T(8,128)(2,1)S(1)}, u32[]{:S(2)}, u32[]{:S(2)}) %all-to-all-start.5) | async-done | bytes 262176 | tf_op jit(solution)/shard_map/cond/branch_1_fun/all_to_all | solution.py:584
  86.2 11.5 %branch_1_fun.17 = (f32[16,128,128]{2,1,0:T(8,128)}, f32[16,128,128]{2,1,0:T(8,128)}, bf16[8,1,128,128]{3,2,1,0:T(8,128)(2,1)}, bf16[4,128,128]{2,1,0:T(8,128)(2...) custom-call(s32[1,68]{1,0:T(1,128)S(1)} %get-tuple-element.106.row_r, ...), custom_call_target="tpu_custom_call" | custom-call | tf_op jit(solution)/shard_map/cond/branch_1_fun/pallas_call | solution.py:611
  97.7 3.0 %collective-permute-start.14 = (bf16[1424,128]{1,0:T(8,128)(2,1)}, bf16[1424,128]{1,0:T(8,128)(2,1)S(1)}, u32[]{:S(2)}, u32[]{:S(2)}) collective-permute-start(bf16[1424,128]{1,0:T(8,128)(2,1)} %get-tuple-element.143.right_ref), channel_id=1, source_target_pairs={{0,1},{1,2},{2,3},{3,4},{4,5},{5,6},{6,7},{8,9},{9,10},{10,11},{11... | collective-permute-start | bytes 1093640 | tf_op jit(solution)/shard_map/cond/branch_1_fun/ppermute | solution.py:577
  100.7 1.3 collective-permute-start.15
  102.0 6.6 %all-to-all-start.6 = ((bf16[8,1,128,128]{3,2,1,0:T(8,128)(2,1)}), bf16[8,1,128,128]{3,2,1,0:T(8,128)(2,1)S(1)}, u32[]{:S(2)}, u32[]{:S(2)}) async-start(bf16[8,1,128,128]{3,2,1,0:T(8,128)(2,1)} %get-tuple-element.141), calls=%async_computation.6 | async-start | bytes 524288 | tf_op jit(solution)/shard_map/cond/branch_1_fun/all_to_all | solution.py:584
  108.6 3.9 %collective-permute-start.16 = (bf16[1,128,128]{2,1,0:T(8,128)(2,1)}, bf16[1,128,128]{2,1,0:T(8,128)(2,1)S(1)}, u32[]{:S(2)}, u32[]{:S(2)}) collective-permute-start(bf16[1,128,128]{2,1,0:T(8,128)(2,1)} %get-tuple-element.145), channel_id=1, source_target_pairs={{0,2},{1,3},{2,4},{3,5},{4,6},{5,7},{8,10},{9,11},{10,12},{11,13},... | collective-permute-start | bytes 98312 | tf_op jit(solution)/shard_map/cond/branch_1_fun/ppermute | solution.py:577
  112.5 1.5 %collective-permute-start.17 = (bf16[1,128,128]{2,1,0:T(8,128)(2,1)}, bf16[1,128,128]{2,1,0:T(8,128)(2,1)S(1)}, u32[]{:S(2)}, u32[]{:S(2)}) collective-permute-start(bf16[1,128,128]{2,1,0:T(8,128)(2,1)} %get-tuple-element.146), channel_id=1, source_target_pairs={{2,0},{3,1},{4,2},{5,3},{6,4},{7,5},{10,8},{11,9},{12,10},{13,11},... | collective-permute-start | bytes 98312 | tf_op jit(solution)/shard_map/cond/branch_1_fun/ppermute | solution.py:577
  114.0 3.8 %branch_1_fun.18.rest_2_ = f32[16,128,128]{2,1,0:T(8,128)} custom-call(f32[16,128,128]{2,1,0:T(8,128)} %get-tuple-element.147.z_ref.z2_ref, bf16[16,128,128]{2,1,0:T(8,128)(2,1)} %get-tuple-element.195.self_ref, f32[16,128]{1,0:T(8,128)} %get-tuple-element.197.res_ref, f32[1,128]{1,0:T(1,128)} %get-tuple-element.126.freq_ref.rest_3_), custom_call_target="tpu_custom_call" | custom-call | tf_op jit(solution)/shard_map/cond/branch_1_fun/pallas_call | solution.py:588
  117.9 0.0 collective-permute-done.14.arrived_ref
  117.9 0.0 collective-permute-done.15.beyond_ref
  117.9 1.2 branch_1_fun.19
  119.1 0.0 collective-permute-done.16.rest_0_
  119.1 0.0 collective-permute-done.17.rest_1_
  119.1 3.1 %all-to-all-done.6.incoming_ref = bf16[8,1,128,128]{3,2,1,0:T(8,128)(2,1)S(1)} async-done(((bf16[8,1,128,128]{3,2,1,0:T(8,128)(2,1)}), bf16[8,1,128,128]{3,2,1,0:T(8,128)(2,1)S(1)}, u32[]{:S(2)}, u32[]{:S(2)}) %all-to-all-start.6) | async-done | bytes 262176 | tf_op jit(solution)/shard_map/cond/branch_1_fun/all_to_all | solution.py:584
  122.2 8.9 %branch_1_fun.20 = f32[32,8,128]{2,1,0:T(8,128)S(1)} custom-call(s32[1,68]{1,0:T(1,128)S(1)} %get-tuple-element.106.row_ref, s32[1,272]{1,0:T(1,128)S(1)} %get-tuple-element.107.slot_ref, s32[1]{0:T(128)} %bitcast.2.place_ref, bf16[272,128,128]{2,1,0:T(8,128)(2,1)} %get-tuple-element.131.blocks_ref, ...), custom_call_target="tpu_custom_call" | custom-call | tf_op jit(solution)/shard_map/cond/branch_1_fun/pallas_call | solution.py:624
  131.1 11.1 %all_to_all.38.pay_ref = f32[32,8,128]{2,1,0:T(8,128)S(1)} all-to-all(f32[32,8,128]{2,1,0:T(8,128)S(1)} %branch_1_fun.20), channel_id=1, replica_groups=mesh['wide'=4,'narrow'=8] {'wide','narrow'}, dimensions={0} | all-to-all | bytes 262144 | tf_op jit(solution)/shard_map/cond/branch_1_fun/all_to_all | solution.py:634
  142.3 3.3 %branch_1_fun.21 = (f32[16,128,128]{2,1,0:T(8,128)}, f32[2,32]{1,0:T(2,128)}) custom-call(f32[32,8,128]{2,1,0:T(8,128)S(1)} %all_to_all.38.pay_ref, f32[8,128]{1,0:T(8,128)S(1)} %get-tuple-element.153.beta_ref, f32[16,128,128]{2,1,0:T(8,128)} %get-tuple-element.123.z_ref.z0_ref, f32[16,128,128]{2,1,0:T(8,128)} %get-tuple-element.138.z_ref.z1_ref, ...), custom_call_target="tpu_custom_call" | custom-call | tf_op jit(solution)/shard_map/cond/branch_1_fun/pallas_call | solution.py:638
  (2 shorter events, 0.0 us)
Async XLA Ops:
  2.8 15.0 %all-to-all-start.8 = ((f32[32,8,128]{2,1,0:T(8,128)}), f32[32,8,128]{2,1,0:T(8,128)S(1)}, u32[]{:S(2)}, u32[]{:S(2)}) async-start(f32[32,8,128]{2,1,0:T(8,128)} %shard_map.136), calls=%async_computation.8 | async-start | bytes 262144 | tf_op jit(solution)/shard_map/all_to_all | solution.py:676
  10.8 0.7 copy-start
  11.5 0.7 copy-start.1
  12.2 0.7 copy-start.2
  25.5 21.4 %collective-permute-start.6 = (bf16[1424,128]{1,0:T(8,128)(2,1)}, bf16[1424,128]{1,0:T(8,128)(2,1)S(1)}, u32[]{:S(2)}, u32[]{:S(2)}) collective-permute-start(bf16[1424,128]{1,0:T(8,128)(2,1)} %get-tuple-element.119.right_ref), channel_id=1, source_target_pairs={{0,1},{1,2},{2,3},{3,4},{4,5},{5,6},{6,7},{8,9},{9,10},{10,11},{11... | collective-permute-start | bytes 1093640 | tf_op jit(solution)/shard_map/cond/branch_1_fun/ppermute | solution.py:577
  28.7 18.2 %collective-permute-start.7 = (bf16[1424,128]{1,0:T(8,128)(2,1)}, bf16[1424,128]{1,0:T(8,128)(2,1)S(1)}, u32[]{:S(2)}, u32[]{:S(2)}) collective-permute-start(bf16[1424,128]{1,0:T(8,128)(2,1)} %get-tuple-element.120.left_ref), channel_id=1, source_target_pairs={{1,0},{2,1},{3,2},{4,3},{5,4},{6,5},{7,6},{9,8},{10,9},{11,10},{12... | collective-permute-start | bytes 1093640 | tf_op jit(solution)/shard_map/cond/branch_1_fun/ppermute | solution.py:577
  30.0 18.8 %all-to-all-start.4 = ((bf16[8,1,128,128]{3,2,1,0:T(8,128)(2,1)}), bf16[8,1,128,128]{3,2,1,0:T(8,128)(2,1)S(1)}, u32[]{:S(2)}, u32[]{:S(2)}) async-start(bf16[8,1,128,128]{3,2,1,0:T(8,128)(2,1)} %get-tuple-element.117), calls=%async_computation.4 | async-start | bytes 524288 | tf_op jit(solution)/shard_map/cond/branch_1_fun/all_to_all | solution.py:584
  34.9 13.2 %collective-permute-start.8 = (bf16[1,128,128]{2,1,0:T(8,128)(2,1)}, bf16[1,128,128]{2,1,0:T(8,128)(2,1)S(1)}, u32[]{:S(2)}, u32[]{:S(2)}) collective-permute-start(bf16[1,128,128]{2,1,0:T(8,128)(2,1)} %get-tuple-element.121), channel_id=1, source_target_pairs={{0,2},{1,3},{2,4},{3,5},{4,6},{5,7},{8,10},{9,11},{10,12},{11,13},... | collective-permute-start | bytes 98312 | tf_op jit(solution)/shard_map/cond/branch_1_fun/ppermute | solution.py:577
  38.8 9.3 %collective-permute-start.9 = (bf16[1,128,128]{2,1,0:T(8,128)(2,1)}, bf16[1,128,128]{2,1,0:T(8,128)(2,1)S(1)}, u32[]{:S(2)}, u32[]{:S(2)}) collective-permute-start(bf16[1,128,128]{2,1,0:T(8,128)(2,1)} %get-tuple-element.122), channel_id=1, source_target_pairs={{2,0},{3,1},{4,2},{5,3},{6,4},{7,5},{10,8},{11,9},{12,10},{13,11},... | collective-permute-start | bytes 98312 | tf_op jit(solution)/shard_map/cond/branch_1_fun/ppermute | solution.py:577
  44.0 4.8 %copy-start.4 = (s32[16]{0:T(128)S(1)}, s32[16]{0:T(128)}, u32[]{:S(2)}) copy-start(s32[16]{0:T(128)} %get-tuple-element.191.jacobi_ref.rest_8_) | copy-start | bytes 196 | tf_op jit(solution)/shard_map/cond
  61.5 20.8 %collective-permute-start.10 = (bf16[1424,128]{1,0:T(8,128)(2,1)}, bf16[1424,128]{1,0:T(8,128)(2,1)S(1)}, u32[]{:S(2)}, u32[]{:S(2)}) collective-permute-start(bf16[1424,128]{1,0:T(8,128)(2,1)} %get-tuple-element.134.right_ref), channel_id=1, source_target_pairs={{0,1},{1,2},{2,3},{3,4},{4,5},{5,6},{6,7},{8,9},{9,10},{10,11},{11... | collective-permute-start | bytes 1093640 | tf_op jit(solution)/shard_map/cond/branch_1_fun/ppermute | solution.py:577
  65.3 17.1 %collective-permute-start.11 = (bf16[1424,128]{1,0:T(8,128)(2,1)}, bf16[1424,128]{1,0:T(8,128)(2,1)S(1)}, u32[]{:S(2)}, u32[]{:S(2)}) collective-permute-start(bf16[1424,128]{1,0:T(8,128)(2,1)} %get-tuple-element.135.left_ref), channel_id=1, source_target_pairs={{1,0},{2,1},{3,2},{4,3},{5,4},{6,5},{7,6},{9,8},{10,9},{11,10},{12... | collective-permute-start | bytes 1093640 | tf_op jit(solution)/shard_map/cond/branch_1_fun/ppermute | solution.py:577
  66.6 19.6 %all-to-all-start.5 = ((bf16[8,1,128,128]{3,2,1,0:T(8,128)(2,1)}), bf16[8,1,128,128]{3,2,1,0:T(8,128)(2,1)S(1)}, u32[]{:S(2)}, u32[]{:S(2)}) async-start(bf16[8,1,128,128]{3,2,1,0:T(8,128)(2,1)} %get-tuple-element.132), calls=%async_computation.5 | async-start | bytes 524288 | tf_op jit(solution)/shard_map/cond/branch_1_fun/all_to_all | solution.py:584
  72.5 11.0 %collective-permute-start.12 = (bf16[1,128,128]{2,1,0:T(8,128)(2,1)}, bf16[1,128,128]{2,1,0:T(8,128)(2,1)S(1)}, u32[]{:S(2)}, u32[]{:S(2)}) collective-permute-start(bf16[1,128,128]{2,1,0:T(8,128)(2,1)} %get-tuple-element.136), channel_id=1, source_target_pairs={{0,2},{1,3},{2,4},{3,5},{4,6},{5,7},{8,10},{9,11},{10,12},{11,13},... | collective-permute-start | bytes 98312 | tf_op jit(solution)/shard_map/cond/branch_1_fun/ppermute | solution.py:577
  76.4 7.1 %collective-permute-start.13 = (bf16[1,128,128]{2,1,0:T(8,128)(2,1)}, bf16[1,128,128]{2,1,0:T(8,128)(2,1)S(1)}, u32[]{:S(2)}, u32[]{:S(2)}) collective-permute-start(bf16[1,128,128]{2,1,0:T(8,128)(2,1)} %get-tuple-element.137), channel_id=1, source_target_pairs={{2,0},{3,1},{4,2},{5,3},{6,4},{7,5},{10,8},{11,9},{12,10},{13,11},... | collective-permute-start | bytes 98312 | tf_op jit(solution)/shard_map/cond/branch_1_fun/ppermute | solution.py:577
  97.7 20.2 %collective-permute-start.14 = (bf16[1424,128]{1,0:T(8,128)(2,1)}, bf16[1424,128]{1,0:T(8,128)(2,1)S(1)}, u32[]{:S(2)}, u32[]{:S(2)}) collective-permute-start(bf16[1424,128]{1,0:T(8,128)(2,1)} %get-tuple-element.143.right_ref), channel_id=1, source_target_pairs={{0,1},{1,2},{2,3},{3,4},{4,5},{5,6},{6,7},{8,9},{9,10},{10,11},{11... | collective-permute-start | bytes 1093640 | tf_op jit(solution)/shard_map/cond/branch_1_fun/ppermute | solution.py:577
  100.7 17.2 %collective-permute-start.15 = (bf16[1424,128]{1,0:T(8,128)(2,1)}, bf16[1424,128]{1,0:T(8,128)(2,1)S(1)}, u32[]{:S(2)}, u32[]{:S(2)}) collective-permute-start(bf16[1424,128]{1,0:T(8,128)(2,1)} %get-tuple-element.144.left_ref), channel_id=1, source_target_pairs={{1,0},{2,1},{3,2},{4,3},{5,4},{6,5},{7,6},{9,8},{10,9},{11,10},{12... | collective-permute-start | bytes 1093640 | tf_op jit(solution)/shard_map/cond/branch_1_fun/ppermute | solution.py:577
  102.0 20.2 %all-to-all-start.6 = ((bf16[8,1,128,128]{3,2,1,0:T(8,128)(2,1)}), bf16[8,1,128,128]{3,2,1,0:T(8,128)(2,1)S(1)}, u32[]{:S(2)}, u32[]{:S(2)}) async-start(bf16[8,1,128,128]{3,2,1,0:T(8,128)(2,1)} %get-tuple-element.141), calls=%async_computation.6 | async-start | bytes 524288 | tf_op jit(solution)/shard_map/cond/branch_1_fun/all_to_all | solution.py:584
  108.6 10.5 %collective-permute-start.16 = (bf16[1,128,128]{2,1,0:T(8,128)(2,1)}, bf16[1,128,128]{2,1,0:T(8,128)(2,1)S(1)}, u32[]{:S(2)}, u32[]{:S(2)}) collective-permute-start(bf16[1,128,128]{2,1,0:T(8,128)(2,1)} %get-tuple-element.145), channel_id=1, source_target_pairs={{0,2},{1,3},{2,4},{3,5},{4,6},{5,7},{8,10},{9,11},{10,12},{11,13},... | collective-permute-start | bytes 98312 | tf_op jit(solution)/shard_map/cond/branch_1_fun/ppermute | solution.py:577
  112.5 6.6 %collective-permute-start.17 = (bf16[1,128,128]{2,1,0:T(8,128)(2,1)}, bf16[1,128,128]{2,1,0:T(8,128)(2,1)S(1)}, u32[]{:S(2)}, u32[]{:S(2)}) collective-permute-start(bf16[1,128,128]{2,1,0:T(8,128)(2,1)} %get-tuple-element.146), channel_id=1, source_target_pairs={{2,0},{3,1},{4,2},{5,3},{6,4},{7,5},{10,8},{11,9},{12,10},{13,11},... | collective-permute-start | bytes 98312 | tf_op jit(solution)/shard_map/cond/branch_1_fun/ppermute | solution.py:577

commit v6 on v5

--- a/solution.py
+++ b/solution.py
@@ -95,7 +95,7 @@
     held = jnp.sum(jnp.where(name // blocks == lane, present, 0.0), axis=0, keepdims=True)
     right = right_ref[...]
     squares = jnp.sum(jnp.sum(right * right, axis=0), axis=0, keepdims=True)
-    rows = jnp.concatenate([squares, needs, held, jnp.zeros((5, 128), f32)], axis=0)
+    rows = jnp.concatenate([squares, needs, held], axis=0)
     pay_ref[...] = jnp.broadcast_to(rows[None], pay_ref.shape)
 
 
@@ -670,7 +670,7 @@
 
     (pay,) = call(
         functools.partial(setup_kernel, peers, blocks),
-        [whole((devices, 8, 128), f32)],
+        [whole((devices, 3, 128), f32)],
         [VM] * 2,
     )(in_hbm(couple_list), in_hbm(right_side))
     pay = lax.all_to_all(pay, AXES, 0, 0)

time: 147 us -> 147 us (level)
  no operation moved by 1% of the time
where the time goes in v6:
time: 147 us; the launch traced here: 145 us
  Pallas kernels  60.5 us (41%)
  starting transfers between devices  53.9 us (37%)
  waiting for transfers between devices  13.2 us (9%)
  blocking collectives  11.4 us (8%)
  local copies, waits for them, and re-layouts  2.75 us (2%)
  between operations  1.51 us (1%)
  other arithmetic  1.5 us (1%)
    ppermute x12, starting transfers between devices, moved(): return near_core(lax.ppermute(value, 'narrow', route))  29.3 us
    pallas_call x2, Pallas kernels, iterate(): call(functools.partial(middle_kernel, plan, first), [vec] + emitted + ([k...  24.3 us
    all_to_all x3, starting transfers between devices, iterate(): incoming = near_core(lax.all_to_all(send, 'narrow', 0, 0))  17.3 us
    pallas_call x3, Pallas kernels, iterate(): call(local_kernel, [vec], [block, block, line, VM], [block], grid=(parts,))  11.5 us
    all_to_all x1, blocking collectives, iterate(): sums = near_core(lax.all_to_all(sums, AXES, 0, 0))  11.4 us
    pallas_call x1, Pallas kernels, iterate(): call(functools.partial(last_kernel, plan), [whole((devices, 8, 128), f32)...  8.91 us
    all_to_all x1, starting transfers between devices, on_device(): pay = lax.all_to_all(pay, AXES, 0, 0)  7.3 us
    all_to_all x3, waiting for transfers between devices, iterate(): incoming = near_core(lax.all_to_all(send, 'narrow', 0, 0))  6.29 us
  transfers between devices with their start and end apart: 16, of which 6 were waited for; matrix products, arithmetic and copies ran while one was open for 1% of the time, Pallas kernels for 11%

profile of v6, /device:TPU:0, one launch (start us, length us, event | category | flops | bytes accessed | tf_op | source)
XLA Modules:
  0.0 145.3 jit_solution(10722736914290513258)
XLA Ops:
  0.6 2.1 %shard_map.136 = f32[32,3,128]{2,1,0:T(4,128)} custom-call(s32[3,224]{1,0:T(4,128)} %lists_ref.3, f32[16,128,128]{2,1,0:T(8,128)} %right_ref.1), custom_call_target="tpu_custom_call" | custom-call | tf_op jit(solution)/shard_map/pallas_call | solution.py:671
  2.8 7.3 %all-to-all-start.8 = ((f32[32,3,128]{2,1,0:T(4,128)}), f32[32,3,128]{2,1,0:T(4,128)S(1)}, u32[]{:S(2)}, u32[]{:S(2)}) async-start(f32[32,3,128]{2,1,0:T(4,128)} %shard_map.136), calls=%async_computation.8 | async-start | bytes 131072 | tf_op jit(solution)/shard_map/all_to_all | solution.py:676
  10.1 0.7 copy.50
  10.8 0.0 copy-start
  10.8 0.7 copy-done
  11.5 0.0 copy-start.1
  11.5 0.7 copy-done.1
  12.2 0.0 copy-start.2
  12.2 0.7 copy-done.2
  12.9 1.4 shard_map.137
  14.2 3.1 %all-to-all-done.8 = f32[32,3,128]{2,1,0:T(4,128)S(1)} async-done(((f32[32,3,128]{2,1,0:T(4,128)}), f32[32,3,128]{2,1,0:T(4,128)S(1)}, u32[]{:S(2)}, u32[]{:S(2)}) %all-to-all-start.8) | async-done | bytes 49184 | tf_op jit(solution)/shard_map/all_to_all | solution.py:676
  17.3 1.4 compare_reduce_fusion
  19.4 0.1 dynamic-slice_convert_fusion
  19.5 125.7 %conditional.1 = ((f32[16,128,128]{2,1,0:T(8,128)}, f32[2,32]{1,0:T(2,128)})) conditional(s32[]{:T(128)} %convert_element_type.9, (f32[32,3,128]{2,1,0:T(4,128)S(1)}, f32[16,128,128]{2,1,0:T(8,128)}, s16[32,2048]{1,0:T(8,128)(2,1)}, s32[16]{0:T(128)}, s32[8,1,4]{2,1,0:T(1,128)S(1)}, /*index=5*/s32[]{:T(128)}, bf16[8,128,128]{2,1,0:T(8,128)(2,1)}, ...), branch_computations={%region_1.2_spmd, %region_2.3_spmd} | conditional | flops 51539607552 | bytes 66421364 | solution.py:704
  19.6 5.4 %branch_1_fun.11 = (f32[16,128,128]{2,1,0:T(8,128)}, f32[8,128]{1,0:T(8,128)S(1)}, f32[16,128,128]{2,1,0:T(8,128)}, bf16[8,1,128,128]{3,2,1,0:T(8,128)(2,1)}, bf...) custom-call(f32[32,3,128]{2,1,0:T(4,128)S(1)} %get-tuple-element.110, ...), custom_call_target="tpu_custom_call" | custom-call | tf_op jit(solution)/shard_map/cond/branch_1_fun/pallas_call | solution.py:564
  25.0 2.7 %collective-permute-start.6 = (bf16[1424,128]{1,0:T(8,128)(2,1)}, bf16[1424,128]{1,0:T(8,128)(2,1)S(1)}, u32[]{:S(2)}, u32[]{:S(2)}) collective-permute-start(bf16[1424,128]{1,0:T(8,128)(2,1)} %get-tuple-element.119.right_ref), channel_id=1, source_target_pairs={{0,1},{1,2},{2,3},{3,4},{4,5},{5,6},{6,7},{8,9},{9,10},{10,11},{11... | collective-permute-start | bytes 1093640 | tf_op jit(solution)/shard_map/cond/branch_1_fun/ppermute | solution.py:577
  27.7 1.3 collective-permute-start.7
  29.0 4.9 %all-to-all-start.4 = ((bf16[8,1,128,128]{3,2,1,0:T(8,128)(2,1)}), bf16[8,1,128,128]{3,2,1,0:T(8,128)(2,1)S(1)}, u32[]{:S(2)}, u32[]{:S(2)}) async-start(bf16[8,1,128,128]{3,2,1,0:T(8,128)(2,1)} %get-tuple-element.117), calls=%async_computation.4 | async-start | bytes 524288 | tf_op jit(solution)/shard_map/cond/branch_1_fun/all_to_all | solution.py:584
  33.9 3.9 %collective-permute-start.8 = (bf16[1,128,128]{2,1,0:T(8,128)(2,1)}, bf16[1,128,128]{2,1,0:T(8,128)(2,1)S(1)}, u32[]{:S(2)}, u32[]{:S(2)}) collective-permute-start(bf16[1,128,128]{2,1,0:T(8,128)(2,1)} %get-tuple-element.121), channel_id=1, source_target_pairs={{0,2},{1,3},{2,4},{3,5},{4,6},{5,7},{8,10},{9,11},{10,12},{11,13},... | collective-permute-start | bytes 98312 | tf_op jit(solution)/shard_map/cond/branch_1_fun/ppermute | solution.py:577
  37.8 1.3 collective-permute-start.9
  39.1 3.8 %branch_1_fun.12.rest_2_ = f32[16,128,128]{2,1,0:T(8,128)} custom-call(f32[16,128,128]{2,1,0:T(8,128)} %get-tuple-element.123.z_ref.z0_ref, bf16[16,128,128]{2,1,0:T(8,128)(2,1)} %get-tuple-element.195.self_ref, f32[16,128]{1,0:T(8,128)} %get-tuple-element.197.res_ref, f32[1,128]{1,0:T(1,128)} %get-tuple-element.126.freq_ref.rest_3_), custom_call_target="tpu_custom_call" | custom-call | tf_op jit(solution)/shard_map/cond/branch_1_fun/pallas_call | solution.py:588
  43.0 0.0 copy-start.4
  43.0 3.0 %collective-permute-done.6.arrived_ref = bf16[1424,128]{1,0:T(8,128)(2,1)S(1)} collective-permute-done((bf16[1424,128]{1,0:T(8,128)(2,1)}, bf16[1424,128]{1,0:T(8,128)(2,1)S(1)}, u32[]{:S(2)}, u32[]{:S(2)}) %collective-permute-start.6) | collective-permute-done | bytes 364576 | tf_op jit(solution)/shard_map/cond/branch_1_fun/ppermute | solution.py:577
  46.0 0.0 collective-permute-done.7.beyond_ref
  46.0 1.2 branch_1_fun.13
  47.1 0.0 collective-permute-done.8.rest_0_
  47.2 0.0 collective-permute-done.9.rest_1_
  47.2 0.6 all-to-all-done.4.incoming_ref
  47.7 0.0 copy-done.4
  47.7 12.8 %branch_1_fun.14 = (f32[16,128,128]{2,1,0:T(8,128)}, f32[16,128,128]{2,1,0:T(8,128)}, bf16[8,1,128,128]{3,2,1,0:T(8,128)(2,1)}, bf16[4,128,128]{2,1,0:T(8,128)(2...) custom-call(s32[1,68]{1,0:T(1,128)S(1)} %get-tuple-element.106.row_r, ...), custom_call_target="tpu_custom_call" | custom-call | tf_op jit(solution)/shard_map/cond/branch_1_fun/pallas_call | solution.py:611
  60.5 3.8 %collective-permute-start.10 = (bf16[1424,128]{1,0:T(8,128)(2,1)}, bf16[1424,128]{1,0:T(8,128)(2,1)S(1)}, u32[]{:S(2)}, u32[]{:S(2)}) collective-permute-start(bf16[1424,128]{1,0:T(8,128)(2,1)} %get-tuple-element.134.right_ref), channel_id=1, source_target_pairs={{0,1},{1,2},{2,3},{3,4},{4,5},{5,6},{6,7},{8,9},{9,10},{10,11},{11... | collective-permute-start | bytes 1093640 | tf_op jit(solution)/shard_map/cond/branch_1_fun/ppermute | solution.py:577
  64.3 1.3 collective-permute-start.11
  65.6 5.9 %all-to-all-start.5 = ((bf16[8,1,128,128]{3,2,1,0:T(8,128)(2,1)}), bf16[8,1,128,128]{3,2,1,0:T(8,128)(2,1)S(1)}, u32[]{:S(2)}, u32[]{:S(2)}) async-start(bf16[8,1,128,128]{3,2,1,0:T(8,128)(2,1)} %get-tuple-element.132), calls=%async_computation.5 | async-start | bytes 524288 | tf_op jit(solution)/shard_map/cond/branch_1_fun/all_to_all | solution.py:584
  71.5 3.9 %collective-permute-start.12 = (bf16[1,128,128]{2,1,0:T(8,128)(2,1)}, bf16[1,128,128]{2,1,0:T(8,128)(2,1)S(1)}, u32[]{:S(2)}, u32[]{:S(2)}) collective-permute-start(bf16[1,128,128]{2,1,0:T(8,128)(2,1)} %get-tuple-element.136), channel_id=1, source_target_pairs={{0,2},{1,3},{2,4},{3,5},{4,6},{5,7},{8,10},{9,11},{10,12},{11,13},... | collective-permute-start | bytes 98312 | tf_op jit(solution)/shard_map/cond/branch_1_fun/ppermute | solution.py:577
  75.4 1.3 collective-permute-start.13
  76.7 3.8 %branch_1_fun.15.rest_2_ = f32[16,128,128]{2,1,0:T(8,128)} custom-call(f32[16,128,128]{2,1,0:T(8,128)} %get-tuple-element.138.z_ref.z1_ref, bf16[16,128,128]{2,1,0:T(8,128)(2,1)} %get-tuple-element.195.self_ref, f32[16,128]{1,0:T(8,128)} %get-tuple-element.197.res_ref, f32[1,128]{1,0:T(1,128)} %get-tuple-element.126.freq_ref.rest_3_), custom_call_target="tpu_custom_call" | custom-call | tf_op jit(solution)/shard_map/cond/branch_1_fun/pallas_call | solution.py:588
  80.6 0.8 collective-permute-done.10.arrived_ref
  81.3 0.0 collective-permute-done.11.beyond_ref
  81.3 1.2 branch_1_fun.16
  82.5 0.0 collective-permute-done.12.rest_0_
  82.5 0.0 collective-permute-done.13.rest_1_
  82.6 2.6 %all-to-all-done.5.incoming_ref = bf16[8,1,128,128]{3,2,1,0:T(8,128)(2,1)S(1)} async-done(((bf16[8,1,128,128]{3,2,1,0:T(8,128)(2,1)}), bf16[8,1,128,128]{3,2,1,0:T(8,128)(2,1)S(1)}, u32[]{:S(2)}, u32[]{:S(2)}) %all-to-all-start.5) | async-done | bytes 262176 | tf_op jit(solution)/shard_map/cond/branch_1_fun/all_to_all | solution.py:584
  85.1 11.5 %branch_1_fun.17 = (f32[16,128,128]{2,1,0:T(8,128)}, f32[16,128,128]{2,1,0:T(8,128)}, bf16[8,1,128,128]{3,2,1,0:T(8,128)(2,1)}, bf16[4,128,128]{2,1,0:T(8,128)(2...) custom-call(s32[1,68]{1,0:T(1,128)S(1)} %get-tuple-element.106.row_r, ...), custom_call_target="tpu_custom_call" | custom-call | tf_op jit(solution)/shard_map/cond/branch_1_fun/pallas_call | solution.py:611
  96.6 3.0 %collective-permute-start.14 = (bf16[1424,128]{1,0:T(8,128)(2,1)}, bf16[1424,128]{1,0:T(8,128)(2,1)S(1)}, u32[]{:S(2)}, u32[]{:S(2)}) collective-permute-start(bf16[1424,128]{1,0:T(8,128)(2,1)} %get-tuple-element.143.right_ref), channel_id=1, source_target_pairs={{0,1},{1,2},{2,3},{3,4},{4,5},{5,6},{6,7},{8,9},{9,10},{10,11},{11... | collective-permute-start | bytes 1093640 | tf_op jit(solution)/shard_map/cond/branch_1_fun/ppermute | solution.py:577
  99.7 1.3 collective-permute-start.15
  101.0 6.6 %all-to-all-start.6 = ((bf16[8,1,128,128]{3,2,1,0:T(8,128)(2,1)}), bf16[8,1,128,128]{3,2,1,0:T(8,128)(2,1)S(1)}, u32[]{:S(2)}, u32[]{:S(2)}) async-start(bf16[8,1,128,128]{3,2,1,0:T(8,128)(2,1)} %get-tuple-element.141), calls=%async_computation.6 | async-start | bytes 524288 | tf_op jit(solution)/shard_map/cond/branch_1_fun/all_to_all | solution.py:584
  107.6 3.9 %collective-permute-start.16 = (bf16[1,128,128]{2,1,0:T(8,128)(2,1)}, bf16[1,128,128]{2,1,0:T(8,128)(2,1)S(1)}, u32[]{:S(2)}, u32[]{:S(2)}) collective-permute-start(bf16[1,128,128]{2,1,0:T(8,128)(2,1)} %get-tuple-element.145), channel_id=1, source_target_pairs={{0,2},{1,3},{2,4},{3,5},{4,6},{5,7},{8,10},{9,11},{10,12},{11,13},... | collective-permute-start | bytes 98312 | tf_op jit(solution)/shard_map/cond/branch_1_fun/ppermute | solution.py:577
  111.5 1.5 %collective-permute-start.17 = (bf16[1,128,128]{2,1,0:T(8,128)(2,1)}, bf16[1,128,128]{2,1,0:T(8,128)(2,1)S(1)}, u32[]{:S(2)}, u32[]{:S(2)}) collective-permute-start(bf16[1,128,128]{2,1,0:T(8,128)(2,1)} %get-tuple-element.146), channel_id=1, source_target_pairs={{2,0},{3,1},{4,2},{5,3},{6,4},{7,5},{10,8},{11,9},{12,10},{13,11},... | collective-permute-start | bytes 98312 | tf_op jit(solution)/shard_map/cond/branch_1_fun/ppermute | solution.py:577
  113.0 3.8 %branch_1_fun.18.rest_2_ = f32[16,128,128]{2,1,0:T(8,128)} custom-call(f32[16,128,128]{2,1,0:T(8,128)} %get-tuple-element.147.z_ref.z2_ref, bf16[16,128,128]{2,1,0:T(8,128)(2,1)} %get-tuple-element.195.self_ref, f32[16,128]{1,0:T(8,128)} %get-tuple-element.197.res_ref, f32[1,128]{1,0:T(1,128)} %get-tuple-element.126.freq_ref.rest_3_), custom_call_target="tpu_custom_call" | custom-call | tf_op jit(solution)/shard_map/cond/branch_1_fun/pallas_call | solution.py:588
  116.9 0.0 collective-permute-done.14.arrived_ref
  116.9 0.0 collective-permute-done.15.beyond_ref
  116.9 1.2 branch_1_fun.19
  118.1 0.0 collective-permute-done.16.rest_0_
  118.1 0.0 collective-permute-done.17.rest_1_
  118.1 3.1 %all-to-all-done.6.incoming_ref = bf16[8,1,128,128]{3,2,1,0:T(8,128)(2,1)S(1)} async-done(((bf16[8,1,128,128]{3,2,1,0:T(8,128)(2,1)}), bf16[8,1,128,128]{3,2,1,0:T(8,128)(2,1)S(1)}, u32[]{:S(2)}, u32[]{:S(2)}) %all-to-all-start.6) | async-done | bytes 262176 | tf_op jit(solution)/shard_map/cond/branch_1_fun/all_to_all | solution.py:584
  121.2 8.9 %branch_1_fun.20 = f32[32,8,128]{2,1,0:T(8,128)S(1)} custom-call(s32[1,68]{1,0:T(1,128)S(1)} %get-tuple-element.106.row_ref, s32[1,272]{1,0:T(1,128)S(1)} %get-tuple-element.107.slot_ref, s32[1]{0:T(128)} %bitcast.2.place_ref, bf16[272,128,128]{2,1,0:T(8,128)(2,1)} %get-tuple-element.131.blocks_ref, ...), custom_call_target="tpu_custom_call" | custom-call | tf_op jit(solution)/shard_map/cond/branch_1_fun/pallas_call | solution.py:624
  130.2 11.4 %all_to_all.38.pay_ref = f32[32,8,128]{2,1,0:T(8,128)S(1)} all-to-all(f32[32,8,128]{2,1,0:T(8,128)S(1)} %branch_1_fun.20), channel_id=1, replica_groups=mesh['wide'=4,'narrow'=8] {'wide','narrow'}, dimensions={0} | all-to-all | bytes 262144 | tf_op jit(solution)/shard_map/cond/branch_1_fun/all_to_all | solution.py:634
  141.6 3.3 %branch_1_fun.21 = (f32[16,128,128]{2,1,0:T(8,128)}, f32[2,32]{1,0:T(2,128)}) custom-call(f32[32,8,128]{2,1,0:T(8,128)S(1)} %all_to_all.38.pay_ref, f32[8,128]{1,0:T(8,128)S(1)} %get-tuple-element.153.beta_ref, f32[16,128,128]{2,1,0:T(8,128)} %get-tuple-element.123.z_ref.z0_ref, f32[16,128,128]{2,1,0:T(8,128)} %get-tuple-element.138.z_ref.z1_ref, ...), custom_call_target="tpu_custom_call" | custom-call | tf_op jit(solution)/shard_map/cond/branch_1_fun/pallas_call | solution.py:638
  (2 shorter events, 0.0 us)
Async XLA Ops:
  2.8 14.6 %all-to-all-start.8 = ((f32[32,3,128]{2,1,0:T(4,128)}), f32[32,3,128]{2,1,0:T(4,128)S(1)}, u32[]{:S(2)}, u32[]{:S(2)}) async-start(f32[32,3,128]{2,1,0:T(4,128)} %shard_map.136), calls=%async_computation.8 | async-start | bytes 131072 | tf_op jit(solution)/shard_map/all_to_all | solution.py:676
  10.8 0.7 copy-start
  11.5 0.7 copy-start.1
  12.2 0.7 copy-start.2
  25.0 21.0 %collective-permute-start.6 = (bf16[1424,128]{1,0:T(8,128)(2,1)}, bf16[1424,128]{1,0:T(8,128)(2,1)S(1)}, u32[]{:S(2)}, u32[]{:S(2)}) collective-permute-start(bf16[1424,128]{1,0:T(8,128)(2,1)} %get-tuple-element.119.right_ref), channel_id=1, source_target_pairs={{0,1},{1,2},{2,3},{3,4},{4,5},{5,6},{6,7},{8,9},{9,10},{10,11},{11... | collective-permute-start | bytes 1093640 | tf_op jit(solution)/shard_map/cond/branch_1_fun/ppermute | solution.py:577
  27.7 18.2 %collective-permute-start.7 = (bf16[1424,128]{1,0:T(8,128)(2,1)}, bf16[1424,128]{1,0:T(8,128)(2,1)S(1)}, u32[]{:S(2)}, u32[]{:S(2)}) collective-permute-start(bf16[1424,128]{1,0:T(8,128)(2,1)} %get-tuple-element.120.left_ref), channel_id=1, source_target_pairs={{1,0},{2,1},{3,2},{4,3},{5,4},{6,5},{7,6},{9,8},{10,9},{11,10},{12... | collective-permute-start | bytes 1093640 | tf_op jit(solution)/shard_map/cond/branch_1_fun/ppermute | solution.py:577
  29.0 18.7 %all-to-all-start.4 = ((bf16[8,1,128,128]{3,2,1,0:T(8,128)(2,1)}), bf16[8,1,128,128]{3,2,1,0:T(8,128)(2,1)S(1)}, u32[]{:S(2)}, u32[]{:S(2)}) async-start(bf16[8,1,128,128]{3,2,1,0:T(8,128)(2,1)} %get-tuple-element.117), calls=%async_computation.4 | async-start | bytes 524288 | tf_op jit(solution)/shard_map/cond/branch_1_fun/all_to_all | solution.py:584
  33.9 13.3 %collective-permute-start.8 = (bf16[1,128,128]{2,1,0:T(8,128)(2,1)}, bf16[1,128,128]{2,1,0:T(8,128)(2,1)S(1)}, u32[]{:S(2)}, u32[]{:S(2)}) collective-permute-start(bf16[1,128,128]{2,1,0:T(8,128)(2,1)} %get-tuple-element.121), channel_id=1, source_target_pairs={{0,2},{1,3},{2,4},{3,5},{4,6},{5,7},{8,10},{9,11},{10,12},{11,13},... | collective-permute-start | bytes 98312 | tf_op jit(solution)/shard_map/cond/branch_1_fun/ppermute | solution.py:577
  37.8 9.3 %collective-permute-start.9 = (bf16[1,128,128]{2,1,0:T(8,128)(2,1)}, bf16[1,128,128]{2,1,0:T(8,128)(2,1)S(1)}, u32[]{:S(2)}, u32[]{:S(2)}) collective-permute-start(bf16[1,128,128]{2,1,0:T(8,128)(2,1)} %get-tuple-element.122), channel_id=1, source_target_pairs={{2,0},{3,1},{4,2},{5,3},{6,4},{7,5},{10,8},{11,9},{12,10},{13,11},... | collective-permute-start | bytes 98312 | tf_op jit(solution)/shard_map/cond/branch_1_fun/ppermute | solution.py:577
  43.0 4.8 %copy-start.4 = (s32[16]{0:T(128)S(1)}, s32[16]{0:T(128)}, u32[]{:S(2)}) copy-start(s32[16]{0:T(128)} %get-tuple-element.191.jacobi_ref.rest_8_) | copy-start | bytes 196 | tf_op jit(solution)/shard_map/cond
  60.5 20.8 %collective-permute-start.10 = (bf16[1424,128]{1,0:T(8,128)(2,1)}, bf16[1424,128]{1,0:T(8,128)(2,1)S(1)}, u32[]{:S(2)}, u32[]{:S(2)}) collective-permute-start(bf16[1424,128]{1,0:T(8,128)(2,1)} %get-tuple-element.134.right_ref), channel_id=1, source_target_pairs={{0,1},{1,2},{2,3},{3,4},{4,5},{5,6},{6,7},{8,9},{9,10},{10,11},{11... | collective-permute-start | bytes 1093640 | tf_op jit(solution)/shard_map/cond/branch_1_fun/ppermute | solution.py:577
  64.3 17.0 %collective-permute-start.11 = (bf16[1424,128]{1,0:T(8,128)(2,1)}, bf16[1424,128]{1,0:T(8,128)(2,1)S(1)}, u32[]{:S(2)}, u32[]{:S(2)}) collective-permute-start(bf16[1424,128]{1,0:T(8,128)(2,1)} %get-tuple-element.135.left_ref), channel_id=1, source_target_pairs={{1,0},{2,1},{3,2},{4,3},{5,4},{6,5},{7,6},{9,8},{10,9},{11,10},{12... | collective-permute-start | bytes 1093640 | tf_op jit(solution)/shard_map/cond/branch_1_fun/ppermute | solution.py:577
  65.6 19.5 %all-to-all-start.5 = ((bf16[8,1,128,128]{3,2,1,0:T(8,128)(2,1)}), bf16[8,1,128,128]{3,2,1,0:T(8,128)(2,1)S(1)}, u32[]{:S(2)}, u32[]{:S(2)}) async-start(bf16[8,1,128,128]{3,2,1,0:T(8,128)(2,1)} %get-tuple-element.132), calls=%async_computation.5 | async-start | bytes 524288 | tf_op jit(solution)/shard_map/cond/branch_1_fun/all_to_all | solution.py:584
  71.5 11.0 %collective-permute-start.12 = (bf16[1,128,128]{2,1,0:T(8,128)(2,1)}, bf16[1,128,128]{2,1,0:T(8,128)(2,1)S(1)}, u32[]{:S(2)}, u32[]{:S(2)}) collective-permute-start(bf16[1,128,128]{2,1,0:T(8,128)(2,1)} %get-tuple-element.136), channel_id=1, source_target_pairs={{0,2},{1,3},{2,4},{3,5},{4,6},{5,7},{8,10},{9,11},{10,12},{11,13},... | collective-permute-start | bytes 98312 | tf_op jit(solution)/shard_map/cond/branch_1_fun/ppermute | solution.py:577
  75.4 7.1 %collective-permute-start.13 = (bf16[1,128,128]{2,1,0:T(8,128)(2,1)}, bf16[1,128,128]{2,1,0:T(8,128)(2,1)S(1)}, u32[]{:S(2)}, u32[]{:S(2)}) collective-permute-start(bf16[1,128,128]{2,1,0:T(8,128)(2,1)} %get-tuple-element.137), channel_id=1, source_target_pairs={{2,0},{3,1},{4,2},{5,3},{6,4},{7,5},{10,8},{11,9},{12,10},{13,11},... | collective-permute-start | bytes 98312 | tf_op jit(solution)/shard_map/cond/branch_1_fun/ppermute | solution.py:577
  96.6 20.2 %collective-permute-start.14 = (bf16[1424,128]{1,0:T(8,128)(2,1)}, bf16[1424,128]{1,0:T(8,128)(2,1)S(1)}, u32[]{:S(2)}, u32[]{:S(2)}) collective-permute-start(bf16[1424,128]{1,0:T(8,128)(2,1)} %get-tuple-element.143.right_ref), channel_id=1, source_target_pairs={{0,1},{1,2},{2,3},{3,4},{4,5},{5,6},{6,7},{8,9},{9,10},{10,11},{11... | collective-permute-start | bytes 1093640 | tf_op jit(solution)/shard_map/cond/branch_1_fun/ppermute | solution.py:577
  99.7 17.2 %collective-permute-start.15 = (bf16[1424,128]{1,0:T(8,128)(2,1)}, bf16[1424,128]{1,0:T(8,128)(2,1)S(1)}, u32[]{:S(2)}, u32[]{:S(2)}) collective-permute-start(bf16[1424,128]{1,0:T(8,128)(2,1)} %get-tuple-element.144.left_ref), channel_id=1, source_target_pairs={{1,0},{2,1},{3,2},{4,3},{5,4},{6,5},{7,6},{9,8},{10,9},{11,10},{12... | collective-permute-start | bytes 1093640 | tf_op jit(solution)/shard_map/cond/branch_1_fun/ppermute | solution.py:577
  101.0 20.3 %all-to-all-start.6 = ((bf16[8,1,128,128]{3,2,1,0:T(8,128)(2,1)}), bf16[8,1,128,128]{3,2,1,0:T(8,128)(2,1)S(1)}, u32[]{:S(2)}, u32[]{:S(2)}) async-start(bf16[8,1,128,128]{3,2,1,0:T(8,128)(2,1)} %get-tuple-element.141), calls=%async_computation.6 | async-start | bytes 524288 | tf_op jit(solution)/shard_map/cond/branch_1_fun/all_to_all | solution.py:584
  107.6 10.5 %collective-permute-start.16 = (bf16[1,128,128]{2,1,0:T(8,128)(2,1)}, bf16[1,128,128]{2,1,0:T(8,128)(2,1)S(1)}, u32[]{:S(2)}, u32[]{:S(2)}) collective-permute-start(bf16[1,128,128]{2,1,0:T(8,128)(2,1)} %get-tuple-element.145), channel_id=1, source_target_pairs={{0,2},{1,3},{2,4},{3,5},{4,6},{5,7},{8,10},{9,11},{10,12},{11,13},... | collective-permute-start | bytes 98312 | tf_op jit(solution)/shard_map/cond/branch_1_fun/ppermute | solution.py:577
  111.5 6.6 %collective-permute-start.17 = (bf16[1,128,128]{2,1,0:T(8,128)(2,1)}, bf16[1,128,128]{2,1,0:T(8,128)(2,1)S(1)}, u32[]{:S(2)}, u32[]{:S(2)}) collective-permute-start(bf16[1,128,128]{2,1,0:T(8,128)(2,1)} %get-tuple-element.146), channel_id=1, source_target_pairs={{2,0},{3,1},{4,2},{5,3},{6,4},{7,5},{10,8},{11,9},{12,10},{13,11},... | collective-permute-start | bytes 98312 | tf_op jit(solution)/shard_map/cond/branch_1_fun/ppermute | solution.py:577
